TPU v7x, 32 devices: a whole 2x2x4 slice. The times are simulated.
32 devices in a mesh: section: 4 (over y, x), dp: 8 (over z, core).
Axes of the slice: x: 2, y: 2, z: 4, core: 2. Of those that a mesh axis runs over, the one named last changes fastest.
Arguments:
- codes: int32 [16, 264], P('dp'), may hold values from 0 to 16383
- labels: int32 [16, 264], P('dp'), may hold values from 0 to 16383
- picks: int32 [16, 32], P('dp'), may hold values from 0 to 263
- classes: int32 [16, 3], P('dp'), may hold values from 0 to 999
- null_mask: int32 [16, 3], P('dp'), may hold values 0 or 1
- starts: int32 [16, 4], P('dp'), may hold values from 0 to 264, as said below
- master: float32 [69632, 768], P(('section', 'dp'))
- momentum: float32 [69632, 768], P(('section', 'dp'))
- average: float32 [69632, 768], P(('section', 'dp'))
Outputs:
- loss_sum: float32 [], replicated
- token_count: float32 [], replicated
- grad_norm: float32 [], replicated
- new_master: float32 [69632, 768], P(('section', 'dp'))
- new_momentum: float32 [69632, 768], P(('section', 'dp'))
- new_average: float32 [69632, 768], P(('section', 'dp'))
Inputs may be any that keep to these rules, and one draw needn't show every extreme that they name: In each row starts[r,0] = 0, the columns do not fall, and the last column is the row's live length; every segment but the first and last of a row holds 257 slots; the last row's live length is 264.
All inputs are finite; a program needn't handle non-finite values. No bound on the sum of `null_mask` on one device may be relied on, other than what follows from the above.
Results may differ from a plain program's by a relative error of at most 0.024.
The roundings to bfloat16 on the way count: a program that leaves them out, or rounds other values in their place, can miss the bound.
Values may be sent and summed in bfloat16 or wider, within the bound.
A program may use at most 768 MiB of HBM per device.

v0:
```python
import math

import jax
import jax.numpy as jnp
from jax import lax
from jax.sharding import PartitionSpec as P

D = 768
HEADS = 12
HD = 64
FF = 2048
VOCAB = 16384
CLASSES = 1001
SLOTS = 264
MB = 2
SEGS = 3


rope_base = 10000.0
clip_limit = 1.0
rate_factor = 0.25
momentum_decay = 0.9
average_decay = 0.8
norm_eps = 1e-06


def for_sending(shard):

    def short(part):
        return part.astype(jnp.bfloat16) if part.dtype == jnp.float32 else part

    return jax.tree.map(short, shard)


def from_behind(shard, axis, by):
    count = lax.axis_size(axis)
    pairs = [(i, i + by) for i in range(count) if 0 <= i + by < count]
    return lax.ppermute(shard, axis, pairs)


def plain_dot(left, right):
    return jnp.dot(left, right, preferred_element_type=jnp.float32)


def contract_rows(left, right):
    return lax.dot_general(
        left, right, (((0,), (0,)), ((), ())), preferred_element_type=jnp.float32
    )


def contract_cols(left, right):
    return lax.dot_general(
        left, right, (((1,), (1,)), ((), ())), preferred_element_type=jnp.float32
    )


def rms_scale(value_in, gain):
    return (
        value_in * lax.rsqrt(jnp.mean(value_in * value_in, axis=-1, keepdims=True) + 1e-06) * gain
    )


def rotate(value_in, cosine, sine_part):
    half_size = value_in.shape[-1] // 2
    first_half = value_in[..., :half_size]
    second_half = value_in[..., half_size:]
    return jnp.concatenate(
        [
            first_half * cosine - second_half * sine_part,
            second_half * cosine + first_half * sine_part,
        ],
        axis=-1,
    )


def row_layout(starts_row, classes_row, null_row, codes_row):
    slot_ids = jnp.arange(SLOTS, dtype=jnp.int32)
    segment = jnp.sum((starts_row[None, 1:] <= slot_ids[:, None]).astype(jnp.int32), axis=1)
    seg_start = jnp.take(starts_row, segment)
    position = slot_ids - seg_start
    live_end = starts_row[SEGS]
    is_first = (position == 0) & (slot_ids < live_end)
    clamped = jnp.minimum(segment, SEGS - 1)
    class_row = jnp.where(
        jnp.take(null_row, clamped) > 0, CLASSES - 1, jnp.take(classes_row, clamped)
    )
    row_index = jnp.where(is_first, VOCAB + class_row, codes_row)
    following = jnp.concatenate([segment[1:], jnp.full((1,), SEGS + 1, jnp.int32)])
    counted = (following == segment) & (slot_ids + 1 < live_end)
    allowed = (segment[:, None] == segment[None, :]) & (slot_ids[None, :] <= slot_ids[:, None])
    frequency = rope_base ** (-jnp.arange(HD // 2, dtype=jnp.float32) * 2.0 / HD)
    angles = position.astype(jnp.float32)[:, None] * frequency[None, :]
    return (row_index, counted, allowed, jnp.cos(angles)[:, None, :], jnp.sin(angles)[:, None, :])


def layer_pieces(weights):
    offset_rows = 4 * D
    return (
        weights[:D],
        weights[D : 2 * D],
        weights[2 * D : 3 * D],
        weights[3 * D : 4 * D],
        weights[offset_rows : offset_rows + FF],
        weights[offset_rows + FF : offset_rows + 2 * FF],
        weights[offset_rows + 2 * FF : offset_rows + 3 * FF],
        weights[offset_rows + 3 * FF].astype(jnp.float32),
        weights[offset_rows + 3 * FF + 1].astype(jnp.float32),
    )


def zero_kept():
    fl = jnp.float32
    bf = jnp.bfloat16
    return (
        jnp.zeros((SLOTS, D), fl),
        jnp.zeros((SLOTS, D), bf),
        jnp.zeros((SLOTS, HEADS, HD), bf),
        jnp.zeros((SLOTS, HEADS, HD), bf),
        jnp.zeros((SLOTS, HEADS, HD), bf),
        jnp.zeros((HEADS, SLOTS, SLOTS), fl),
        jnp.zeros((HEADS, SLOTS, SLOTS), bf),
        jnp.zeros((SLOTS, D), bf),
        jnp.zeros((SLOTS, D), fl),
        jnp.zeros((SLOTS, D), bf),
        jnp.zeros((SLOTS, FF), fl),
        jnp.zeros((SLOTS, FF), fl),
        jnp.zeros((SLOTS, FF), bf),
    )


def zero_saved():
    bf = jnp.bfloat16
    return (
        jnp.zeros((SLOTS, D), bf),
        jnp.zeros((SLOTS, FF), bf),
        jnp.zeros((SLOTS, FF), bf),
        jnp.zeros((SLOTS, D), bf),
        jnp.zeros((SLOTS, D), bf),
        jnp.zeros((SLOTS, D), bf),
        jnp.zeros((SLOTS, D), bf),
    )


def layer_forward(weights, stream_in, cosine, sine_part, allowed):
    w_query, w_key, w_value, w_out, w_gate, w_up, w_down, gain_attn, gain_mlp = layer_pieces(
        weights
    )
    stream = stream_in.astype(jnp.float32)
    normed_a = rms_scale(stream, gain_attn).astype(jnp.bfloat16)
    query_raw = plain_dot(normed_a, w_query).reshape(SLOTS, HEADS, HD)
    key_raw = plain_dot(normed_a, w_key).reshape(SLOTS, HEADS, HD)
    query_rows = (rotate(query_raw, cosine, sine_part) * HD ** (-0.5)).astype(jnp.bfloat16)
    key_rows = rotate(key_raw, cosine, sine_part).astype(jnp.bfloat16)
    value_rows = plain_dot(normed_a, w_value).astype(jnp.bfloat16).reshape(SLOTS, HEADS, HD)
    scores = jnp.einsum("qhd,khd->hqk", query_rows, key_rows, preferred_element_type=jnp.float32)
    attn_probs = jax.nn.softmax(jnp.where(allowed[None], scores, -1e30), axis=-1)
    probs_low = attn_probs.astype(jnp.bfloat16)
    attn_mixed = (
        jnp.einsum("hqk,khd->qhd", probs_low, value_rows, preferred_element_type=jnp.float32)
        .astype(jnp.bfloat16)
        .reshape(SLOTS, D)
    )
    hidden = stream + plain_dot(attn_mixed, w_out)
    normed_b = rms_scale(hidden, gain_mlp).astype(jnp.bfloat16)
    gate_proj = contract_cols(normed_b, w_gate)
    up_proj = contract_cols(normed_b, w_up)
    inner_act = (jax.nn.silu(gate_proj) * up_proj).astype(jnp.bfloat16)
    result = (hidden + plain_dot(inner_act, w_down)).astype(jnp.bfloat16)
    kept_vals = (
        stream,
        normed_a,
        query_rows,
        key_rows,
        value_rows,
        attn_probs,
        probs_low,
        attn_mixed,
        hidden,
        normed_b,
        gate_proj,
        up_proj,
        inner_act,
    )
    return (result, kept_vals)


def layer_input_grads(weights, kept_vals, grad_in, cosine, sine_part):
    w_query, w_key, w_value, w_out, w_gate, w_up, w_down, gain_attn, gain_mlp = layer_pieces(
        weights
    )
    (
        stream,
        normed_a,
        query_rows,
        key_rows,
        value_rows,
        attn_probs,
        probs_low,
        attn_mixed,
        hidden,
        normed_b,
        gate_proj,
        up_proj,
        inner_act,
    ) = kept_vals
    grad_inner = contract_cols(grad_in, w_down)
    sigmoid_g = jax.nn.sigmoid(gate_proj)
    grad_gate = (grad_inner * up_proj * sigmoid_g * (1.0 + gate_proj * (1.0 - sigmoid_g))).astype(
        jnp.bfloat16
    )
    grad_up = (grad_inner * gate_proj * sigmoid_g).astype(jnp.bfloat16)
    grad_normb = plain_dot(grad_gate, w_gate) + plain_dot(grad_up, w_up)
    _, pull_mlp = jax.vjp(rms_scale, hidden, gain_mlp)
    grad_hidden, grad_gmlp = pull_mlp(grad_normb)
    grad_hidden = grad_hidden + grad_in.astype(jnp.float32)
    grad_branch = grad_hidden.astype(jnp.bfloat16)
    grad_mixed = contract_cols(grad_branch, w_out).astype(jnp.bfloat16).reshape(SLOTS, HEADS, HD)
    grad_value = (
        jnp.einsum("hqk,qhd->khd", probs_low, grad_mixed, preferred_element_type=jnp.float32)
        .astype(jnp.bfloat16)
        .reshape(SLOTS, D)
    )
    grad_probs = jnp.einsum(
        "qhd,khd->hqk", grad_mixed, value_rows, preferred_element_type=jnp.float32
    )
    grad_scores = (
        attn_probs * (grad_probs - jnp.sum(attn_probs * grad_probs, axis=-1, keepdims=True))
    ).astype(jnp.bfloat16)
    grad_query = jnp.einsum(
        "hqk,khd->qhd", grad_scores, key_rows, preferred_element_type=jnp.float32
    ) * HD ** (-0.5)
    grad_key = jnp.einsum(
        "hqk,qhd->khd", grad_scores, query_rows, preferred_element_type=jnp.float32
    )
    grad_qraw = rotate(grad_query, cosine, -sine_part).astype(jnp.bfloat16).reshape(SLOTS, D)
    grad_kraw = rotate(grad_key, cosine, -sine_part).astype(jnp.bfloat16).reshape(SLOTS, D)
    grad_norma = (
        contract_cols(grad_qraw, w_query)
        + contract_cols(grad_kraw, w_key)
        + contract_cols(grad_value, w_value)
    )
    _, pull_attn = jax.vjp(rms_scale, stream, gain_attn)
    grad_stream, grad_gattn = pull_attn(grad_norma)
    grad_prev = (grad_stream + grad_hidden).astype(jnp.bfloat16)
    saved = (grad_in, grad_gate, grad_up, grad_branch, grad_qraw, grad_kraw, grad_value)
    return (grad_prev, saved, jnp.stack([grad_gattn, grad_gmlp]))


def layer_weight_grads(kept_vals, saved):
    (
        stream,
        normed_a,
        query_rows,
        key_rows,
        value_rows,
        attn_probs,
        probs_low,
        attn_mixed,
        hidden,
        normed_b,
        gate_proj,
        up_proj,
        inner_act,
    ) = kept_vals
    grad_in, grad_gate, grad_up, grad_branch, grad_qraw, grad_kraw, grad_value = saved
    return jnp.concatenate(
        [
            contract_rows(normed_a, grad_qraw),
            contract_rows(normed_a, grad_kraw),
            contract_rows(normed_a, grad_value),
            contract_rows(attn_mixed, grad_branch),
            contract_rows(grad_gate, normed_b),
            contract_rows(grad_up, normed_b),
            contract_rows(inner_act, grad_in),
        ],
        axis=0,
    )


def head_step(weights, picked, picked_labels, counted_f):
    stream = picked.astype(jnp.float32)
    gain_final = weights[VOCAB].astype(jnp.float32)
    out_table = weights[:VOCAB]
    normed = rms_scale(stream, gain_final).astype(jnp.bfloat16)
    logits = contract_cols(normed, out_table)
    log_total = jax.nn.logsumexp(logits, axis=-1)
    target = jnp.take_along_axis(logits, picked_labels[:, None], axis=1)[:, 0]
    loss_part = jnp.sum(counted_f * (log_total - target))
    vocab_ids = lax.broadcasted_iota(jnp.int32, logits.shape, 1)
    grad_logits = (
        (
            jnp.exp(logits - log_total[:, None])
            - (vocab_ids == picked_labels[:, None]).astype(jnp.float32)
        )
        * counted_f[:, None]
    ).astype(jnp.bfloat16)
    grad_table = contract_rows(grad_logits, normed)
    grad_normed = plain_dot(grad_logits, out_table)
    _, pull_head = jax.vjp(rms_scale, stream, gain_final)
    grad_stream, grad_gain = pull_head(grad_normed)
    rows_grad = jnp.concatenate([grad_table, grad_gain[None]], axis=0)
    return (grad_stream, rows_grad, loss_part, jnp.sum(counted_f))


def shards(codes, labels, picks, classes, null_mask, starts, master, momentum, average):
    section_id = lax.axis_index("section")
    learn_rate = rate_factor * math.sqrt(
        master.shape[0] * lax.axis_size("section") * lax.axis_size("dp")
    )
    embed_factor = math.sqrt(D)
    gathered = lax.all_gather(master.astype(jnp.bfloat16), "dp", axis=0, tiled=True)
    matrix_rows = 4 * D + 3 * FF
    zero_val = jnp.zeros((), jnp.float32)

    def batch_layout(slot_mb):
        return row_layout(starts[slot_mb], classes[slot_mb], null_mask[slot_mb], codes[slot_mb])

    def embed_forward(weights, grad_acc, stream_in, slot_mb, active):
        row_index = batch_layout(slot_mb)[0]
        looked = (jnp.take(weights, row_index, axis=0).astype(jnp.float32) * embed_factor).astype(
            jnp.bfloat16
        )
        return (looked, grad_acc, zero_val, zero_val, zero_kept())

    def middle_forward(weights, grad_acc, stream_in, slot_mb, active):
        _, _, allowed, cosine, sine_part = batch_layout(slot_mb)
        result, kept_vals = layer_forward(weights, stream_in, cosine, sine_part, allowed)
        return (result, grad_acc, zero_val, zero_val, kept_vals)

    def final_forward(weights, grad_acc, stream_in, slot_mb, active):
        counted = batch_layout(slot_mb)[1]
        picks_row = picks[slot_mb]
        counted_f = (jnp.take(counted, picks_row) & active).astype(jnp.float32)
        picked = jnp.take(stream_in, picks_row, axis=0)
        grad_pick, rows_grad, loss_part, count_part = head_step(
            weights, picked, jnp.take(labels[slot_mb], picks_row), counted_f
        )
        grad_stream = (
            jnp.zeros((SLOTS, D), jnp.float32).at[picks_row].add(grad_pick).astype(jnp.bfloat16)
        )
        return (
            grad_stream,
            grad_acc.at[: VOCAB + 1].add(rows_grad),
            loss_part,
            count_part,
            zero_kept(),
        )

    grad_acc = jnp.zeros((gathered.shape[0], D), jnp.float32)
    received = jnp.zeros((SLOTS, D), jnp.bfloat16)
    kept_stash = jax.tree.map(lambda arr: jnp.zeros((MB,) + arr.shape, arr.dtype), zero_kept())
    head_grads = jnp.zeros((MB, SLOTS, D), jnp.bfloat16)
    loss_acc = zero_val
    count_acc = zero_val
    for tick_num in range(MB + 3):
        micro_num = tick_num - section_id
        active = (micro_num >= 0) & (micro_num < MB)
        slot_mb = jnp.clip(micro_num, 0, MB - 1)
        outgoing, grad_acc, loss_part, count_part, kept_vals = lax.switch(
            section_id,
            [embed_forward, middle_forward, middle_forward, final_forward],
            gathered,
            grad_acc,
            received,
            slot_mb,
            active,
        )
        loss_acc = loss_acc + loss_part
        count_acc = count_acc + count_part
        kept_stash = jax.tree.map(
            lambda stash, fresh: stash.at[slot_mb].set(jnp.where(active, fresh, stash[slot_mb])),
            kept_stash,
            kept_vals,
        )
        head_grads = head_grads.at[slot_mb].set(jnp.where(active, outgoing, head_grads[slot_mb]))
        if tick_num < MB + 2:
            received = jax.tree.map(
                lambda part, own: part.astype(own.dtype),
                from_behind(for_sending(outgoing), "section", 1),
                outgoing,
            )
    loss_all, count_all = lax.psum((loss_acc, count_acc), ("section", "dp"))
    back_weights = lax.all_gather(master.astype(jnp.bfloat16), "dp", axis=0, tiled=True)

    def embed_backward(weights, grad_acc, grad_in, slot_mb):
        row_index = batch_layout(slot_mb)[0]
        return (
            jnp.zeros_like(grad_in),
            grad_acc.at[row_index].add(grad_in.astype(jnp.float32) * embed_factor),
            zero_saved(),
        )

    def middle_backward(weights, grad_acc, grad_in, slot_mb):
        _, _, allowed, cosine, sine_part = batch_layout(slot_mb)
        kept_vals = jax.tree.map(lambda stash: stash[slot_mb], kept_stash)
        grad_prev, saved, gain_grads = layer_input_grads(
            weights, kept_vals, grad_in, cosine, sine_part
        )
        return (grad_prev, grad_acc.at[matrix_rows : matrix_rows + 2].add(gain_grads), saved)

    def final_backward(weights, grad_acc, grad_in, slot_mb):
        return (head_grads[slot_mb], grad_acc, zero_saved())

    saved_stash = jax.tree.map(lambda arr: jnp.zeros((MB,) + arr.shape, arr.dtype), zero_saved())
    received = jnp.zeros((SLOTS, D), jnp.bfloat16)
    for tick_num in range(MB + 3):
        micro_num = tick_num - (3 - section_id)
        active = (micro_num >= 0) & (micro_num < MB)
        slot_mb = jnp.clip(micro_num, 0, MB - 1)
        grad_in = jnp.where(active, received, jnp.zeros_like(received))
        outgoing, grad_acc, saved = lax.switch(
            section_id,
            [embed_backward, middle_backward, middle_backward, final_backward],
            back_weights,
            grad_acc,
            grad_in,
            slot_mb,
        )
        saved_stash = jax.tree.map(
            lambda stash, fresh: stash.at[slot_mb].set(jnp.where(active, fresh, stash[slot_mb])),
            saved_stash,
            saved,
        )
        if tick_num < MB + 2:
            received = jax.tree.map(
                lambda part, own: part.astype(own.dtype),
                from_behind(for_sending(outgoing), "section", -1),
                outgoing,
            )

    def pass_acc(grad_acc, slot_mb):
        return grad_acc

    def add_weights(grad_acc, slot_mb):
        kept_vals = jax.tree.map(lambda stash: stash[slot_mb], kept_stash)
        saved = jax.tree.map(lambda stash: stash[slot_mb], saved_stash)
        return grad_acc.at[:matrix_rows].add(layer_weight_grads(kept_vals, saved))

    for micro_idx in range(MB):
        grad_acc = lax.switch(
            section_id, [pass_acc, add_weights, add_weights, pass_acc], grad_acc, micro_idx
        )
    shard_grad = lax.psum_scatter(grad_acc, "dp", scatter_dimension=0, tiled=True)
    squares = jnp.sum(shard_grad * shard_grad)
    norm_sq = lax.psum(squares, ("section", "dp"))
    grad_norm = jnp.sqrt(norm_sq)
    clipped = shard_grad * jnp.minimum(1.0, clip_limit / (grad_norm + norm_eps))
    new_momentum = momentum_decay * momentum + clipped
    new_master = master - learn_rate * (clipped + momentum_decay * new_momentum)
    new_average = average_decay * average + (1.0 - average_decay) * new_master
    return (loss_all, count_all, grad_norm, new_master, new_momentum, new_average)


def solution(mesh):
    return jax.shard_map(
        shards,
        mesh=mesh,
        in_specs=(
            P("dp", None),
            P("dp", None),
            P("dp", None),
            P("dp", None),
            P("dp", None),
            P("dp", None),
            P(("section", "dp"), None),
            P(("section", "dp"), None),
            P(("section", "dp"), None),
        ),
        out_specs=(
            P(),
            P(),
            P(),
            P(("section", "dp"), None),
            P(("section", "dp"), None),
            P(("section", "dp"), None),
        ),
        check_vma=False,
    )
```

profile of v0, /device:TPU:0, one launch (start us, length us, event | category | flops | bytes accessed | tf_op | source)
XLA Modules:
  0.0 3004.5 jit_solution(18306736973885601019)
XLA Ops:
  17.4 230.4 %all-gather.2.cloned.1.call-done = bf16[17408,768]{1,0:T(8,128)(2,1)} async-done(((bf16[2176,768]{1,0:T(8,128)(2,1)}), bf16[17408,768]{1,0:T(8,128)(2,1)}) %all-gather.2.cloned.1.call-update) | async-done | bytes 26738704 | tf_op jit(solution)/shard_map/all_gather | solution.py:311
  247.9 81.5 %conditional.38 = (f32[17408,768]{1,0:T(8,128)}, f32[]{:T(128)}, f32[]{:T(128)}, bf16[264,768]{1,0:T(8,128)(2,1)}, bf16[264,12,64]{2,1,0:T(8,128)(2,1)}, /*index...) conditional(s32[]{:T(128)} %clamp.2, (s32[]{:T(128)}, ...), branch_computations={%region_0.5_spmd, %region_2.10_spmd, %region_7.15_spmd, %region_12... | conditional | flops 3964155648 | bytes 229554496
  422.6 63.4 %conditional.34 = (f32[17408,768]{1,0:T(8,128)}, f32[]{:T(128)}, f32[]{:T(128)}, f32[264,768]{1,0:T(8,128)}, bf16[264,768]{1,0:T(8,128)(2,1)}, /*index=5*/bf16[2...) conditional(s32[]{:T(128)} %clamp.2, (s32[]{:T(128)}, ...), branch_computations={%region_22.31_spmd, %region_24.37_spmd, %region_30.0_spmd, %region... | conditional | flops 3965776384 | bytes 377821504
  573.4 63.4 %conditional.35 = (f32[17408,768]{1,0:T(8,128)}, f32[]{:T(128)}, f32[]{:T(128)}, f32[264,768]{1,0:T(8,128)}, bf16[264,768]{1,0:T(8,128)(2,1)}, /*index=5*/bf16[2...) conditional(s32[]{:T(128)} %clamp.2, (s32[]{:T(128)}, ...), branch_computations={%region_46.55_spmd, %region_48.61_spmd, %region_54.67_spmd, %regio... | conditional | flops 3965776384 | bytes 377821504
  636.8 60.9 %collective-permute-start.2 = (bf16[264,768]{1,0:T(8,128)(2,1)}, bf16[264,768]{1,0:T(8,128)(2,1)}, u32[]{:S(2)}, u32[]{:S(2)}) collective-permute-start(bf16[264,768]{1,0:T(8,128)(2,1)} %get-tuple-element.4331), channel_id=1, source_target_pairs={{0,8},{8,16},{16,24},{1,9},{9,17},{17,25},{2,10},{10,18},{18,26},{... | collective-permute-start | bytes 1216520 | tf_op jit(solution)/shard_map/ppermute | solution.py:38
  757.8 63.7 %conditional.36 = (f32[17408,768]{1,0:T(8,128)}, f32[]{:T(128)}, f32[]{:T(128)}, f32[264,768]{1,0:T(8,128)}, bf16[264,768]{1,0:T(8,128)(2,1)}, /*index=5*/bf16[2...) conditional(s32[]{:T(128)} %clamp.2, (s32[]{:T(128)}, ...), branch_computations={%region_70.79_spmd, %region_72.85_spmd, %region_78.91_spmd, %regio... | conditional | flops 3965776384 | bytes 377821504
  821.5 212.2 %collective-permute-start.3 = (bf16[264,768]{1,0:T(8,128)(2,1)}, bf16[264,768]{1,0:T(8,128)(2,1)}, u32[]{:S(2)}, u32[]{:S(2)}) collective-permute-start(bf16[264,768]{1,0:T(8,128)(2,1)} %get-tuple-element.4332), channel_id=1, source_target_pairs={{0,8},{8,16},{16,24},{1,9},{9,17},{17,25},{2,10},{10,18},{18,26},{... | collective-permute-start | bytes 1216520 | tf_op jit(solution)/shard_map/ppermute | solution.py:38
  1093.6 65.8 %conditional.37 = (f32[17408,768]{1,0:T(8,128)}, f32[]{:T(128)}, f32[]{:T(128)}, f32[264,768]{1,0:T(8,128)}, bf16[264,768]{1,0:T(8,128)(2,1)}, /*index=5*/bf16[2...) conditional(s32[]{:T(128)} %clamp.2, (s32[]{:T(128)}, ...), branch_computations={%region_94.103_spmd, %region_96.109_spmd, %region_102.115_spmd, %r... | conditional | flops 3965776384 | bytes 377821504
  1184.0 73.7 %conditional.27 = (bf16[264,768]{1,0:T(8,128)(2,1)}, f32[17408,768]{1,0:T(8,128)}, bf16[264,768]{1,0:T(8,128)(2,1)}, bf16[264,2048]{1,0:T(8,128)(2,1)}, bf16[264...) conditional(s32[]{:T(128)} %clamp.2, (s32[]{:T(128)}, ...), branch_computations={%region_130.140_spmd, %region_133.149_spmd, %region_142.158_spmd, ... | conditional | flops 4188738560 | bytes 156934048 | solution.py:411
  1195.9 36.8 %scatter_fusion = f32[17408,768]{1,0:T(8,128)} fusion(f32[17408,768]{1,0:T(8,128)} %get-tuple-element.2540, s32[264]{0:T(512)S(1)} %compare_select_fusion.22, f32[264,768]{1,0:T(8,128)} %convert_multiply_fusion), kind=kCustom, calls=%fused_computation.26 | custom fusion | flops 202752 | bytes 2434080 | tf_op jit(solution)/shard_map/cond/branch_0_fun/scatter-add | solution.py:389
  1279.4 207.3 %collective-permute-done.4 = bf16[264,768]{1,0:T(8,128)(2,1)S(1)} collective-permute-done((bf16[264,768]{1,0:T(8,128)(2,1)}, bf16[264,768]{1,0:T(8,128)(2,1)S(1)}, u32[]{:S(2)}, u32[]{:S(2)}) %collective-permute-start.4) | collective-permute-done | bytes 405536 | tf_op jit(solution)/shard_map/ppermute | solution.py:38
  1487.5 72.4 %conditional.28 = (bf16[264,768]{1,0:T(8,128)(2,1)}, f32[17408,768]{1,0:T(8,128)}, bf16[264,768]{1,0:T(8,128)(2,1)}, bf16[264,2048]{1,0:T(8,128)(2,1)}, bf16[264...) conditional(s32[]{:T(128)} %clamp.2, (s32[]{:T(128)}, ...), branch_computations={%region_152.162_spmd, %region_155.171_spmd, %region_164.180_spmd, ... | conditional | flops 4188738560 | bytes 156934048 | solution.py:411
  1498.8 36.8 %scatter_fusion.1 = f32[17408,768]{1,0:T(8,128)} fusion(f32[17408,768]{1,0:T(8,128)} %get-tuple-element.2578, s32[264]{0:T(512)S(1)} %compare_select_fusion.25, f32[264,768]{1,0:T(8,128)} %convert_multiply_fusion.1), kind=kCustom, calls=%fused_computation.27 | custom fusion | flops 202752 | bytes 2434080 | tf_op jit(solution)/shard_map/cond/branch_0_fun/scatter-add | solution.py:389
  1579.3 183.7 %collective-permute-done.5 = bf16[264,768]{1,0:T(8,128)(2,1)S(1)} collective-permute-done((bf16[264,768]{1,0:T(8,128)(2,1)}, bf16[264,768]{1,0:T(8,128)(2,1)S(1)}, u32[]{:S(2)}, u32[]{:S(2)}) %collective-permute-start.5) | collective-permute-done | bytes 405536 | tf_op jit(solution)/shard_map/ppermute | solution.py:38
  1763.8 72.7 %conditional.29 = (bf16[264,768]{1,0:T(8,128)(2,1)}, f32[17408,768]{1,0:T(8,128)}, bf16[264,768]{1,0:T(8,128)(2,1)}, bf16[264,2048]{1,0:T(8,128)(2,1)}, bf16[264...) conditional(s32[]{:T(128)} %clamp.2, (s32[]{:T(128)}, ...), branch_computations={%region_174.184_spmd, %region_177.193_spmd, %region_186.202_spmd, ... | conditional | flops 4188738560 | bytes 156934048 | solution.py:411
  1775.4 36.8 %scatter_fusion.2 = f32[17408,768]{1,0:T(8,128)} fusion(f32[17408,768]{1,0:T(8,128)} %get-tuple-element.2616, s32[264]{0:T(512)S(1)} %compare_select_fusion.28, f32[264,768]{1,0:T(8,128)} %convert_multiply_fusion.2), kind=kCustom, calls=%fused_computation.28 | custom fusion | flops 202752 | bytes 2434080 | tf_op jit(solution)/shard_map/cond/branch_0_fun/scatter-add | solution.py:389
  1855.9 131.8 %collective-permute-done.6 = bf16[264,768]{1,0:T(8,128)(2,1)S(1)} collective-permute-done((bf16[264,768]{1,0:T(8,128)(2,1)}, bf16[264,768]{1,0:T(8,128)(2,1)S(1)}, u32[]{:S(2)}, u32[]{:S(2)}) %collective-permute-start.6) | collective-permute-done | bytes 405536 | tf_op jit(solution)/shard_map/ppermute | solution.py:38
  1988.5 72.9 %conditional.30 = (bf16[264,768]{1,0:T(8,128)(2,1)}, f32[17408,768]{1,0:T(8,128)}, bf16[264,768]{1,0:T(8,128)(2,1)}, bf16[264,2048]{1,0:T(8,128)(2,1)}, bf16[264...) conditional(s32[]{:T(128)} %clamp.2, (s32[]{:T(128)}, ...), branch_computations={%region_196.206_spmd, %region_199.215_spmd, %region_208.224_spmd, ... | conditional | flops 4188738560 | bytes 156934048 | solution.py:411
  2000.1 36.8 %scatter_fusion.3 = f32[17408,768]{1,0:T(8,128)} fusion(f32[17408,768]{1,0:T(8,128)} %get-tuple-element.2654, s32[264]{0:T(512)S(1)} %compare_select_fusion.31, f32[264,768]{1,0:T(8,128)} %convert_multiply_fusion.3), kind=kCustom, calls=%fused_computation.29 | custom fusion | flops 202752 | bytes 2434080 | tf_op jit(solution)/shard_map/cond/branch_0_fun/scatter-add | solution.py:389
  2109.0 106.2 %conditional.31 = (f32[17408,768]{1,0:T(8,128)}, bf16[264,768]{1,0:T(8,128)(2,1)}, bf16[264,2048]{1,0:T(8,128)(2,1)}, bf16[264,2048]{1,0:T(8,128)(2,1)}, bf16[26...) conditional(s32[]{:T(128)} %clamp.2, (s32[]{:T(128)}, ...), branch_computations={%region_218.228_spmd, %region_221.236_spmd, %region_229.244_spmd, ... | conditional | flops 4185289728 | bytes 251532320 | solution.py:411
  2119.4 36.2 %scatter_fusion.4 = f32[17408,768]{1,0:T(8,128)} fusion(f32[17408,768]{1,0:T(8,128)} %get-tuple-element.2692, s32[264]{0:T(512)S(1)} %compare_select_fusion.34, f32[264,768]{1,0:T(8,128)S(1)} %convert_multiply_fusion.4), kind=kCustom, calls=%fused_computation.30 | custom fusion | flops 202752 | bytes 2434080 | tf_op jit(solution)/shard_map/cond/branch_0_fun/scatter-add | solution.py:389
  2155.6 35.1 %copy.1363 = f32[17408,768]{1,0:T(8,128)} copy(f32[17408,768]{1,0:T(8,128)} %scatter_fusion.4) | data formatting | bytes 106954752 | tf_op jit(solution)/shard_map/cond
  2247.4 687.7 %reduce-scatter.2.cloned.1.call-done = f32[2176,768]{1,0:T(8,128)} async-done(((f32[17408,768]{1,0:T(8,128)}), f32[2176,768]{1,0:T(8,128)}) %reduce-scatter.2.cloned.1.call-update) | async-done | bytes 6684688 | tf_op jit(solution)/shard_map/reduce_scatter | solution.py:443
  2940.3 38.0 %all-reduce.1 = (f32[]{:T(128)}, f32[]{:T(128)}, f32[]{:T(128)}) all-reduce(f32[]{:T(128)S(6)} %add.1845, f32[]{:T(128)S(6)} %add.1849, f32[]{:T(128)} %multiply_reduce_fusion.18), channel_id=1, replica_groups=mesh['section'=4,'dp'=8] {'section','dp'}, use_global_device_ids=true, to_apply=%region_118.126 | all-reduce | flops 3 | bytes 24 | tf_op jit(solution)/shard_map/psum | solution.py:382
  (895 shorter events, 812.0 us)
Async XLA Ops:
  7.2 240.7 %all-gather.2.cloned.1.call-start = ((), (), s32[]{:S(2)}) async-start(), calls=%async_computation.1 | async-start | bytes 30081024 | tf_op jit(solution)/shard_map/all_gather | solution.py:311
  12.2 235.7 %copy-start.340 = (s32[2,264]{1,0:T(2,128)S(1)}, s32[2,264]{1,0:T(2,128)}, u32[]{:S(2)}) copy-start(s32[2,264]{1,0:T(2,128)} %param.319) | copy-start | bytes 6340
  12.2 235.7 %copy-start.346 = (s32[2,3]{1,0:T(2,128)S(1)}, s32[2,3]{1,0:T(2,128)}, u32[]{:S(2)}) copy-start(s32[2,3]{1,0:T(2,128)} %param.323) | copy-start | bytes 76
  12.2 235.7 %copy-start.352 = (s32[2,3]{1,0:T(2,128)S(1)}, s32[2,3]{1,0:T(2,128)}, u32[]{:S(2)}) copy-start(s32[2,3]{1,0:T(2,128)} %param.322) | copy-start | bytes 76
  12.2 235.7 %copy-start.358 = (s32[2,32]{1,0:T(2,128)S(1)}, s32[2,32]{1,0:T(2,128)}, u32[]{:S(2)}) copy-start(s32[2,32]{1,0:T(2,128)} %param.321) | copy-start | bytes 772
  12.2 235.7 %copy-start.359 = (s32[2,264]{1,0:T(2,128)S(1)}, s32[2,264]{1,0:T(2,128)}, u32[]{:S(2)}) copy-start(s32[2,264]{1,0:T(2,128)} %param.320) | copy-start | bytes 6340
  12.2 235.7 %copy-start.362 = (s32[2,4]{1,0:T(2,128)S(1)}, s32[2,4]{1,0:T(2,128)}, u32[]{:S(2)}) copy-start(s32[2,4]{1,0:T(2,128)} %param.324) | copy-start | bytes 100
  12.2 2922.9 %reduce-scatter.2.cloned.1.call-start = ((), (), s32[]{:S(2)}) async-start(), calls=%async_computation.2 | async-start | bytes 60162048 | tf_op jit(solution)/shard_map/reduce_scatter | solution.py:443
  331.3 91.3 %collective-permute-start = (bf16[264,768]{1,0:T(8,128)(2,1)S(1)}, bf16[264,768]{1,0:T(8,128)(2,1)S(1)}, u32[]{:S(2)}, u32[]{:S(2)}) collective-permute-start(bf16[264,768]{1,0:T(8,128)(2,1)S(1)} %get-tuple-element.4534), channel_id=1, source_target_pairs={{0,8},{8,16},{16,24},{1,9},{9,17},{17,25},{2,10},{10,18},{18,26},{... | collective-permute-start | bytes 1216520 | tf_op jit(solution)/shard_map/ppermute | solution.py:38
  422.6 82.6 %copy-start.113 = (bf16[2,264,768]{2,1,0:T(8,128)(2,1)S(1)}, bf16[2,264,768]{2,1,0:T(8,128)(2,1)}, u32[]{:S(2)}) copy-start(bf16[2,264,768]{2,1,0:T(8,128)(2,1)} %copy-done.112) | copy-start | bytes 2433028
  486.1 87.2 %collective-permute-start.1 = (bf16[264,768]{1,0:T(8,128)(2,1)}, bf16[264,768]{1,0:T(8,128)(2,1)}, u32[]{:S(2)}, u32[]{:S(2)}) collective-permute-start(bf16[264,768]{1,0:T(8,128)(2,1)} %get-tuple-element.4330), channel_id=1, source_target_pairs={{0,8},{8,16},{16,24},{1,9},{9,17},{17,25},{2,10},{10,18},{18,26},{... | collective-permute-start | bytes 1216520 | tf_op jit(solution)/shard_map/ppermute | solution.py:38
  573.3 124.4 %copy-start.115 = (bf16[2,264,768]{2,1,0:T(8,128)(2,1)S(1)}, bf16[2,264,768]{2,1,0:T(8,128)(2,1)}, u32[]{:S(2)}) copy-start(bf16[2,264,768]{2,1,0:T(8,128)(2,1)} %copy-done.114) | copy-start | bytes 2433028
  573.3 126.9 %copy-start.11 = (f32[2,264,768]{2,1,0:T(8,128)S(1)}, f32[2,264,768]{2,1,0:T(8,128)}, u32[]{:S(2)}) copy-start(f32[2,264,768]{2,1,0:T(8,128)} %copy-done.10) | copy-start | bytes 4866052
  636.8 121.0 %collective-permute-start.2 = (bf16[264,768]{1,0:T(8,128)(2,1)}, bf16[264,768]{1,0:T(8,128)(2,1)}, u32[]{:S(2)}, u32[]{:S(2)}) collective-permute-start(bf16[264,768]{1,0:T(8,128)(2,1)} %get-tuple-element.4331), channel_id=1, source_target_pairs={{0,8},{8,16},{16,24},{1,9},{9,17},{17,25},{2,10},{10,18},{18,26},{... | collective-permute-start | bytes 1216520 | tf_op jit(solution)/shard_map/ppermute | solution.py:38
  757.8 275.9 %copy-start.117 = (bf16[2,264,768]{2,1,0:T(8,128)(2,1)S(1)}, bf16[2,264,768]{2,1,0:T(8,128)(2,1)}, u32[]{:S(2)}) copy-start(bf16[2,264,768]{2,1,0:T(8,128)(2,1)} %copy-done.116) | copy-start | bytes 2433028
  757.8 278.5 %copy-start.13 = (f32[2,264,768]{2,1,0:T(8,128)S(1)}, f32[2,264,768]{2,1,0:T(8,128)}, u32[]{:S(2)}) copy-start(f32[2,264,768]{2,1,0:T(8,128)} %copy-done.12) | copy-start | bytes 4866052
  821.5 214.8 %copy-start.80 = (f32[264,768]{1,0:T(8,128)S(1)}, f32[264,768]{1,0:T(8,128)}, u32[]{:S(2)}) copy-start(f32[264,768]{1,0:T(8,128)} %get-tuple-element.2972) | copy-start | bytes 2433028
  821.5 272.1 %collective-permute-start.3 = (bf16[264,768]{1,0:T(8,128)(2,1)}, bf16[264,768]{1,0:T(8,128)(2,1)}, u32[]{:S(2)}, u32[]{:S(2)}) collective-permute-start(bf16[264,768]{1,0:T(8,128)(2,1)} %get-tuple-element.4332), channel_id=1, source_target_pairs={{0,8},{8,16},{16,24},{1,9},{9,17},{17,25},{2,10},{10,18},{18,26},{... | collective-permute-start | bytes 1216520 | tf_op jit(solution)/shard_map/ppermute | solution.py:38
  1257.6 229.0 %collective-permute-start.4 = (bf16[264,768]{1,0:T(8,128)(2,1)}, bf16[264,768]{1,0:T(8,128)(2,1)S(1)}, u32[]{:S(2)}, u32[]{:S(2)}) collective-permute-start(bf16[264,768]{1,0:T(8,128)(2,1)} %get-tuple-element.2975), channel_id=1, source_target_pairs={{8,0},{16,8},{24,16},{9,1},{17,9},{25,17},{10,2},{18,10},{26,18},{... | collective-permute-start | bytes 1216520 | tf_op jit(solution)/shard_map/ppermute | solution.py:38
  1564.2 198.8 %collective-permute-start.5 = (bf16[264,768]{1,0:T(8,128)(2,1)}, bf16[264,768]{1,0:T(8,128)(2,1)S(1)}, u32[]{:S(2)}, u32[]{:S(2)}) collective-permute-start(bf16[264,768]{1,0:T(8,128)(2,1)} %get-tuple-element.2977), channel_id=1, source_target_pairs={{8,0},{16,8},{24,16},{9,1},{17,9},{25,17},{10,2},{18,10},{26,18},{... | collective-permute-start | bytes 1216520 | tf_op jit(solution)/shard_map/ppermute | solution.py:38
  1576.6 186.4 %copy-start.162 = (bf16[2,264,768]{2,1,0:T(8,128)(2,1)}, bf16[2,264,768]{2,1,0:T(8,128)(2,1)S(1)}, u32[]{:S(2)}) copy-start(bf16[2,264,768]{2,1,0:T(8,128)(2,1)S(1)} %fusion.1270) | copy-start | bytes 2433028
  1840.9 146.8 %collective-permute-start.6 = (bf16[264,768]{1,0:T(8,128)(2,1)}, bf16[264,768]{1,0:T(8,128)(2,1)S(1)}, u32[]{:S(2)}, u32[]{:S(2)}) collective-permute-start(bf16[264,768]{1,0:T(8,128)(2,1)} %get-tuple-element.2979), channel_id=1, source_target_pairs={{8,0},{16,8},{24,16},{9,1},{17,9},{25,17},{10,2},{18,10},{26,18},{... | collective-permute-start | bytes 1216520 | tf_op jit(solution)/shard_map/ppermute | solution.py:38
  1853.2 134.5 %copy-start.164 = (bf16[2,264,768]{2,1,0:T(8,128)(2,1)}, bf16[2,264,768]{2,1,0:T(8,128)(2,1)S(1)}, u32[]{:S(2)}) copy-start(bf16[2,264,768]{2,1,0:T(8,128)(2,1)S(1)} %fusion.1269) | copy-start | bytes 2433028
  2065.8 42.4 %collective-permute-start.7 = (bf16[264,768]{1,0:T(8,128)(2,1)}, bf16[264,768]{1,0:T(8,128)(2,1)S(1)}, u32[]{:S(2)}, u32[]{:S(2)}) collective-permute-start(bf16[264,768]{1,0:T(8,128)(2,1)} %get-tuple-element.2981), channel_id=1, source_target_pairs={{8,0},{16,8},{24,16},{9,1},{17,9},{25,17},{10,2},{18,10},{26,18},{... | collective-permute-start | bytes 1216520 | tf_op jit(solution)/shard_map/ppermute | solution.py:38
  (196 other events, 1054.7 us)
Sparse Core Ops, SparseCore 0:
  12.4 235.4 all-gather.1
  2247.5 687.5 reduce-scatter.1
where the time goes:
time: 3030 us; the launch traced here: 3000 us
  waiting for transfers between devices  1460 us (48%)
  other arithmetic  504 us (17%)
  local copies, waits for them, and re-layouts  448 us (15%)
  starting transfers between devices  315 us (10%)
  loops' own time  219 us (7%)
  blocking collectives  38 us (1%)
    reduce_scatter x1, waiting for transfers between devices, shards(): lax.psum_scatter(grad_acc, 'dp', scatter_dimension=0, tiled=True)  688 us
    ppermute x8, waiting for transfers between devices, from_behind(): return lax.ppermute(shard, axis, pairs)  544 us
    ppermute x8, starting transfers between devices, from_behind(): return lax.ppermute(shard, axis, pairs)  315 us
    all_gather x1, waiting for transfers between devices, shards(): lax.all_gather(master.astype(jnp.bfloat16), 'dp', axis=0, tiled=True)  230 us
    scatter x95, other arithmetic, shards(): stash.at[slot_mb].set(jnp.where(active, fresh, stash[slot_mb]))  195 us
    scatter-add x5, other arithmetic, embed_backward(): grad_acc.at[row_index].add(grad_in.astype(jnp.float32) * embed_factor)  183 us
    dynamic_slice x80, local copies, waits for them, and re-layouts, shards(): stash[slot_mb]  137 us
    another operation x122, local copies, waits for them, and re-layouts  126 us
  transfers between devices with their start and end apart: 10, of which 6 were waited for; matrix products, arithmetic and copies ran while one was open for 10% of the time, Pallas kernels for 0%

commit v1 on v0

v1 whole, which is shorter than its diff:
```python
import functools
import math

import jax
import jax.numpy as jnp
from jax import lax
from jax.experimental import pallas as pl
from jax.experimental.pallas import tpu as pltpu
from jax.sharding import PartitionSpec as P

D = 768
HEADS = 12
HD = 64
FF = 2048
VOCAB = 16384
CLASSES = 1001
SLOTS = 264
SP = 272
PICKS = 32
SEGS = 3
MATS = 4 * D + 3 * FF
WROWS = 9232

F32 = jnp.float32
BF16 = jnp.bfloat16

rope_base = 10000.0
clip_limit = 1.0
rate_factor = 0.25
momentum_decay = 0.9
average_decay = 0.8
norm_eps = 1e-06


def nn(left, right):
    return jnp.dot(left, right, preferred_element_type=F32)


def tn(left, right):
    return lax.dot_general(left, right, (((0,), (0,)), ((), ())), preferred_element_type=F32)


def nt(left, right):
    return lax.dot_general(left, right, (((1,), (1,)), ((), ())), preferred_element_type=F32)


def rms_scale(value_in, gain):
    return (
        value_in * lax.rsqrt(jnp.mean(value_in * value_in, axis=-1, keepdims=True) + norm_eps) * gain
    )


def rms_pull(value_in, gain, grad):
    inv = lax.rsqrt(jnp.mean(value_in * value_in, axis=-1, keepdims=True) + norm_eps)
    unit = value_in * inv
    scaled = grad * gain
    grad_in = inv * (scaled - unit * jnp.mean(scaled * unit, axis=-1, keepdims=True))
    return grad_in, jnp.sum(grad * unit, axis=0)


def row_layout(starts_row, classes_row, null_row, codes_row):
    slot_ids = jnp.arange(SLOTS, dtype=jnp.int32)
    segment = jnp.sum((starts_row[None, 1:] <= slot_ids[:, None]).astype(jnp.int32), axis=1)
    seg_start = jnp.sum(
        jnp.where(segment[:, None] == jnp.arange(SEGS + 1)[None, :], starts_row[None, :], 0), axis=1
    )
    position = slot_ids - seg_start
    live_end = starts_row[SEGS]
    is_first = (position == 0) & (slot_ids < live_end)
    clamped = jnp.minimum(segment, SEGS - 1)
    hit = clamped[:, None] == jnp.arange(SEGS)[None, :]
    class_row = jnp.sum(
        jnp.where(hit, jnp.where(null_row > 0, CLASSES - 1, classes_row)[None, :], 0), axis=1
    )
    row_index = jnp.where(is_first, VOCAB + class_row, codes_row)
    following = jnp.concatenate([segment[1:], jnp.full((1,), SEGS + 1, jnp.int32)])
    counted = (following == segment) & (slot_ids + 1 < live_end)
    return row_index, counted, segment, position


MESH = pl.DeviceIdType.MESH
ANY = pl.BlockSpec(memory_space=pl.ANY)
VMEM = pl.BlockSpec(memory_space=pltpu.VMEM)

HALF = 1088
CH = 64
NCH = HALF // CH
CC = 48
NCC = 11
LANE = 4 * HALF
LAG = 2
WINDOW = 2
HOP = 3


def place():
    sec = lax.axis_index("section")
    dp = lax.axis_index("dp")
    z = dp // 2
    c = lax.rem(dp, 2)
    par = lax.rem(sec, 2)
    home = jnp.logical_or(sec == 1, sec == 2)
    return sec, dp, z, c, par, home


def greet_neighbours(sec, dp, z, c, par):
    barrier = pltpu.get_barrier_semaphore()

    def greet(s, e):
        pl.semaphore_signal(barrier, 1, device_id=(s, e), device_id_type=MESH)

    greet(sec, dp + 1 - 2 * c)
    greet(sec + 1 - 2 * par, dp)
    pl.when(z > 0)(lambda: greet(sec, dp - 2))
    pl.when(z < 3)(lambda: greet(sec, dp + 2))
    pl.semaphore_wait(barrier, 2 + (z > 0).astype(jnp.int32) + (z < 3).astype(jnp.int32))


def hop_targets(sec, dp, c, par):
    return {
        "up": (sec, dp + 2),
        "down": (sec, dp - 2),
        "x": (sec + 1 - 2 * par, dp),
        "core": (sec, dp + 1 - 2 * c),
    }


HOPS = ("up", "down", "x", "core")


def tree(z, c, home):
    both = jnp.logical_and
    either = jnp.logical_or
    far = z >= 2
    mid = both(z >= 1, z <= 2)
    never = z < 0
    out = []
    for block in (0, 1):
        for half in (0, 1):
            mine = home if half == 0 else jnp.logical_not(home)
            other = jnp.logical_not(mine)
            source = both(z == block, home)
            at_owner_col = both(z == block, jnp.logical_not(home))
            if block == 0:
                sends = dict(up=either(z == 0, both(mid, mine)), down=never)
                from_up = never
            else:
                sends = dict(up=both(mid, mine), down=z == 1)
                from_up = z == 0
            sends["x"] = either(source, both(far, mine))
            from_x = either(at_owner_col, both(far, other))
            from_down = jnp.logical_not(either(source, either(from_x, from_up)))
            aside = 1 - home.astype(jnp.int32)
            turn = jnp.logical_and(far, other).astype(jnp.int32) + far.astype(jnp.int32) * half
            near = 1 - far.astype(jnp.int32)
            depth = jnp.abs(z - block) + near * aside + turn
            out.append((source, sends, dict(up=from_up, down=from_down, x=from_x), depth))
    lane0 = c == 0
    source = both(both(z == 2, home), lane0)
    sends = dict(
        up=both(z == 2, lane0),
        down=both(mid, lane0),
        x=source,
        core=lane0,
    )
    parents = dict(
        up=both(z <= 1, lane0),
        down=both(z == 3, lane0),
        x=both(both(z == 2, jnp.logical_not(home)), lane0),
    )
    depth = jnp.abs(z - 2) + 1 - home.astype(jnp.int32)
    out.append((source, sends, parents, depth))
    return out


def open_kernel(
    table, index, out, x0, own_sem, recv_sem, recv_c, core_sem, send_sem,
    sent, mine, rx_core, rx_up, rx_down, swap_send, swap_recv, x_send, x_recv, line_send,
    up_recv, down_recv,
):
    sec, dp, z, c, par, home = place()
    targets = hop_targets(sec, dp, c, par)
    classes = tree(z, c, home)
    greet_neighbours(sec, dp, z, c, par)

    def keep(rows):
        return pltpu.make_async_copy(
            table.at[pl.ds(0, rows)],
            out.at[pl.ds(pl.multiple_of(dp * 2 * HALF, 16), rows)],
            own_sem,
        )

    def keep_all():
        keep(2 * HALF).start()
        keep(2 * HALF).wait()

    def keep_few():
        keep(NCC * CC).start()
        keep(NCC * CC).wait()

    pl.when(jnp.logical_and(home, z < 2))(keep_all)
    pl.when(classes[4][0])(keep_few)

    def base(k, lane):
        if k == 4:
            return 4 * 2 * HALF
        return 2 * HALF * (2 * (k // 2) + lane) + HALF * (k % 2)

    def copy(k, hop, j, rows, recv, slot):
        part = out.at[pl.ds(pl.multiple_of(base(k, c) + j * rows, 16), rows)]
        return pltpu.make_async_remote_copy(
            src_ref=part,
            dst_ref=part,
            send_sem=send_sem.at[k, HOPS.index(hop), slot],
            recv_sem=recv,
            device_id=targets[hop],
            device_id_type=MESH,
        )

    def piece(k, j, rows):
        source, sends, _, _ = classes[k]
        recv = recv_c.at[j] if k == 4 else recv_sem.at[k, j]
        slot = lax.rem(j, WINDOW)

        def send(hop):
            to = core_sem.at[k] if hop == "core" else recv
            one = copy(k, hop, j, rows, to, slot)
            pl.when(j >= WINDOW)(one.wait_send)
            one.start()

        pl.when(jnp.logical_not(source))(copy(k, "x", j, rows, recv, slot).wait_recv)
        for hop in HOPS[:3]:
            pl.when(sends[hop])(lambda hop=hop: send(hop))
        send("core")

    def counts(k):
        return (NCC, CC) if k == 4 else (NCH, CH)

    first = sec == 0
    second = sec == 1

    def slot(k):
        return pl.ds(pl.multiple_of(k * SP, 16), SP)

    def order(i):
        low = (z <= 1).astype(jnp.int32)
        return low * (3 - i) + (1 - low) * i

    def swap(k):
        return pltpu.make_async_remote_copy(
            src_ref=sent.at[slot(k)],
            dst_ref=rx_core.at[slot(k)],
            send_sem=swap_send,
            recv_sem=swap_recv.at[k],
            device_id=targets["core"],
            device_id_type=MESH,
        )

    def cross(zz):
        return pltpu.make_async_remote_copy(
            src_ref=mine.at[slot(4 + zz)],
            dst_ref=mine.at[slot(zz)],
            send_sem=x_send,
            recv_sem=x_recv.at[zz],
            device_id=targets["x"],
            device_id_type=MESH,
        )

    def go_up(zz):
        return pltpu.make_async_remote_copy(
            src_ref=mine.at[slot(zz)],
            dst_ref=rx_down.at[slot(zz)],
            send_sem=line_send,
            recv_sem=down_recv.at[zz],
            device_id=targets["up"],
            device_id_type=MESH,
        )

    def go_down(zz):
        return pltpu.make_async_remote_copy(
            src_ref=mine.at[slot(zz)],
            dst_ref=rx_up.at[slot(zz)],
            send_sem=line_send,
            recv_sem=up_recv.at[zz],
            device_id=targets["down"],
            device_id_type=MESH,
        )

    def add(k, ref):
        there = slot(k)
        mine[there, :] = (mine[there, :].astype(F32) + ref[there, :].astype(F32)).astype(BF16)

    def look(row):
        local = index[pl.ds(pl.multiple_of(row * SP, 16), SP), :]
        ids = lax.broadcasted_iota(jnp.int32, (SP, 2 * HALF), 1)
        onehot = jnp.where(ids == local, 1.0, 0.0).astype(BF16)
        return (nn(onehot, table[...]) * math.sqrt(D)).astype(BF16)

    def lookup(i):
        b = i // 2
        zz = order(b // 2)
        p = 1 - lax.rem(b, 2)
        k = 4 * p + zz

        def for_other():
            sent[slot(k), :] = look(2 * (2 * zz + 1 - c) + p)
            swap(k).start()

        def for_self():
            mine[slot(k), :] = look(2 * (2 * zz + c) + p)
            swap(k).wait_recv()
            add(k, rx_core)
            pl.when(p == 1)(lambda: cross(zz).start())

        pl.when(lax.rem(i, 2) == 0)(for_other)
        pl.when(lax.rem(i, 2) == 1)(for_self)

    def chain(zz):
        def from_below():
            go_up(zz).wait_recv()
            add(zz, rx_down)

        def from_above():
            go_down(zz).wait_recv()
            add(zz, rx_up)

        pl.when(second)(cross(zz).wait_recv)
        pl.when(jnp.logical_and(zz >= z, z > 0))(from_below)
        pl.when(jnp.logical_and(zz <= z, z < 3))(from_above)
        pl.when(zz > z)(lambda: go_up(zz).start())
        pl.when(zz < z)(lambda: go_down(zz).start())

    def chains(i):
        for o in range(4):
            zz = order(o)
            hops = jnp.maximum(
                z * (zz >= z).astype(jnp.int32), (3 - z) * (zz <= z).astype(jnp.int32)
            )
            pl.when(i == 4 * o + 3 + 2 * sec + HOP * hops)(lambda zz=zz: chain(zz))

    def step(i, carry):
        for k in range(5):
            count, rows = counts(k)
            j = i - LAG * classes[k][3]
            now = jnp.logical_and(j >= 0, j < count)
            if k == 4:
                now = jnp.logical_and(now, c == 0)
            pl.when(now)(lambda k=k, j=j, rows=rows: piece(k, j, rows))
        pl.when(jnp.logical_and(first, i < 16))(lambda: lookup(i))
        pl.when(sec < 2)(lambda: chains(i))
        return carry

    lax.fori_loop(0, max(NCH + 5 * LAG, 12 + 3 + 2 + 3 * HOP + 1), step, 0)

    def blocks(count, sem):
        return pltpu.make_async_remote_copy(
            src_ref=mine.at[pl.ds(0, count * SP)],
            dst_ref=mine.at[pl.ds(0, count * SP)],
            send_sem=sem,
            recv_sem=sem,
            device_id=targets["core"],
            device_id_type=MESH,
        )

    def finish():
        x0[...] = mine[slot(z), :]
        blocks(3, line_send).wait_send()

    def none():
        x0[...] = jnp.zeros_like(x0)

    def sent_first():
        blocks(8, swap_send).wait_send()
        blocks(4, x_send).wait_send()

    pl.when(first)(sent_first)
    pl.when(sec < 2)(finish)
    pl.when(sec >= 2)(none)

    def drain(k):
        count, rows = counts(k)
        _, sends, _, _ = classes[k]
        for j in range(count - WINDOW, count):
            for hop in HOPS[:3]:
                one = copy(k, hop, j, rows, core_sem.at[k], j % WINDOW)
                pl.when(sends[hop])(one.wait_send)
            copy(k, "core", j, rows, core_sem.at[k], j % WINDOW).wait_send()

    def came(k):
        count, rows = counts(k)
        part = out.at[pl.ds(pl.multiple_of(base(k, 1 - c), 16), count * rows)]
        pltpu.make_async_remote_copy(
            src_ref=part,
            dst_ref=part,
            send_sem=send_sem.at[k, 3, 0],
            recv_sem=core_sem.at[k],
            device_id=targets["core"],
            device_id_type=MESH,
        ).wait_recv()

    for k in range(4):
        drain(k)
        came(k)
    pl.when(c == 0)(lambda: drain(4))
    pl.when(c == 1)(lambda: came(4))


def gather_and_embed(table, index):
    rows = lambda n: pltpu.VMEM((n * SP, D), BF16)
    return pl.pallas_call(
        open_kernel,
        out_shape=(
            jax.ShapeDtypeStruct((WROWS, D), BF16),
            jax.ShapeDtypeStruct((SP, D), BF16),
        ),
        in_specs=[VMEM, VMEM],
        out_specs=(VMEM, VMEM),
        scratch_shapes=[
            pltpu.SemaphoreType.DMA,
            pltpu.SemaphoreType.DMA((4, NCH)),
            pltpu.SemaphoreType.DMA((NCC,)),
            pltpu.SemaphoreType.DMA((5,)),
            pltpu.SemaphoreType.DMA((5, 4, WINDOW)),
            rows(8),
            rows(8),
            rows(8),
            rows(4),
            rows(4),
            pltpu.SemaphoreType.DMA,
            pltpu.SemaphoreType.DMA((8,)),
            pltpu.SemaphoreType.DMA,
            pltpu.SemaphoreType.DMA((4,)),
            pltpu.SemaphoreType.DMA,
            pltpu.SemaphoreType.DMA((4,)),
            pltpu.SemaphoreType.DMA((4,)),
        ],
        compiler_params=pltpu.CompilerParams(
            collective_id=0, has_side_effects=True, vmem_limit_bytes=56 * 2**20
        ),
        name="gather_and_embed",
    )(table, index)


def close_kernel(
    grads, start, block, index, out, squares, loc, rx_core, rx_up, rx_down, rx_x, total, summed,
    all_dx, load_sem, core_sem, core_c, recv_sem, recv_c, core_send, send_sem, out_sem,
    dx_own, dx_send, line_recv, cross_recv, dx_core_send, dx_core_recv,
):
    sec, dp, z, c, par, home = place()
    targets = hop_targets(sec, dp, c, par)
    classes = tree(z, c, home)
    rx = dict(up=rx_up, down=rx_down, x=rx_x)
    del start

    def base(k, lane):
        if k == 4:
            return 4 * 2 * HALF
        return 2 * HALF * (2 * (k // 2) + lane) + HALF * (k % 2)

    def held(k):
        return k * HALF

    def load(k):
        rows = NCC * CC if k == 4 else HALF
        return pltpu.make_async_copy(
            grads.at[pl.ds(pl.multiple_of(base(k, c), 16), rows)],
            loc.at[pl.ds(held(k), rows)],
            load_sem.at[k],
        )

    for k in range(5):
        load(k).start()
    greet_neighbours(sec, dp, z, c, par)

    def to_core(k, j, rows):
        sem = core_c.at[j] if k == 4 else core_sem.at[k, j]
        return pltpu.make_async_remote_copy(
            src_ref=grads.at[pl.ds(pl.multiple_of(base(k, 1 - c) + j * rows, 16), rows)],
            dst_ref=rx_core.at[pl.ds(pl.multiple_of(held(k) + j * rows, 16), rows)],
            send_sem=core_send.at[k],
            recv_sem=sem,
            device_id=targets["core"],
            device_id_type=MESH,
        )

    def start_core(j, carry):
        for k in range(4):
            to_core(k, j, CH).start()
        pl.when(jnp.logical_and(j < NCC, c == 1))(lambda: to_core(4, j, CC).start())
        return carry

    lax.fori_loop(0, NCH, start_core, 0)
    for k in range(5):
        load(k).wait()

    def onward(k, hop, j, rows):
        back = dict(up="down", down="up", x="x")[hop]
        index = ("up", "down", "x").index(back)
        part = pl.ds(pl.multiple_of(held(k) + j * rows, 16), rows)
        return pltpu.make_async_remote_copy(
            src_ref=loc.at[part],
            dst_ref=rx[back].at[part],
            send_sem=send_sem.at[k],
            recv_sem=recv_c.at[index, j] if k == 4 else recv_sem.at[index, k, j],
            device_id=targets[hop],
            device_id_type=MESH,
        )

    def landed(k, hop, j, rows):
        index = ("up", "down", "x").index(hop)
        part = pl.ds(pl.multiple_of(held(k) + j * rows, 16), rows)
        return pltpu.make_async_remote_copy(
            src_ref=loc.at[part],
            dst_ref=rx[hop].at[part],
            send_sem=send_sem.at[k],
            recv_sem=recv_c.at[index, j] if k == 4 else recv_sem.at[index, k, j],
            device_id=targets[hop],
            device_id_type=MESH,
        )

    def write_out(k, j, rows):
        offset = j * rows if k == 4 else HALF * (k % 2) + j * rows
        part = pl.ds(pl.multiple_of(offset, 16), rows)
        return pltpu.make_async_copy(total.at[part], out.at[part], out_sem)

    def start_of(k, j, rows):
        part = pl.ds(pl.multiple_of(held(k) + j * rows, 16), rows)
        to_core(k, j, rows).wait_recv()
        acc = summed.at[pl.ds(0, rows)]
        acc[...] = loc[part, :].astype(F32) + rx_core[part, :].astype(F32)
        return part, acc

    def gathered(k, j, rows):
        part, acc = start_of(k, j, rows)
        for hop in HOPS[:3]:

            def add(hop=hop):
                landed(k, hop, j, rows).wait_recv()
                acc[...] += rx[hop][part, :].astype(F32)

            pl.when(classes[k][1][hop])(add)
        return part, acc

    def pass_on(k, j, rows, part, acc):
        loc[part, :] = acc[...].astype(BF16)
        for hop in HOPS[:3]:
            pl.when(classes[k][2][hop])(lambda hop=hop: onward(k, hop, j, rows).start())

    def relay(k, j, rows):
        part, acc = gathered(k, j, rows)
        pass_on(k, j, rows, part, acc)

    def finish(k, j, rows):
        _, acc = gathered(k, j, rows)
        offset = j * rows if k == 4 else HALF * (k % 2) + j * rows
        value = acc[...]
        total[pl.ds(pl.multiple_of(offset, 16), rows), :] = value
        write_out(k, j, rows).start()
        count_squares(value)

    first = sec == 0
    second = sec == 1
    in_line = sec < 2
    both = jnp.logical_and

    def dx_part(p, zz):
        return all_dx.at[pl.ds(pl.multiple_of((2 * (2 * zz + c) + p) * SP, 16), SP)]

    def move(p, zz, send, recv, target):
        return pltpu.make_async_remote_copy(
            src_ref=dx_part(p, zz),
            dst_ref=dx_part(p, zz),
            send_sem=send,
            recv_sem=recv,
            device_id=target,
            device_id_type=MESH,
        )

    def line(zz, hop):
        return move(par, zz, dx_send, line_recv.at[zz], targets[hop])

    def cross(zz):
        return move(1, zz, dx_send, cross_recv.at[zz], targets["x"])

    def dx_to_core(p, zz):
        return move(p, zz, dx_core_send, dx_core_recv, targets["core"])

    def aside(zz):
        pl.when(first)(lambda: dx_to_core(0, zz).start())
        pl.when(second)(lambda: cross(zz).start())

    def crossed(zz):
        cross(zz).wait_recv()
        dx_to_core(1, zz).start()

    def blocks(count, send, recv):
        return pltpu.make_async_remote_copy(
            src_ref=all_dx.at[pl.ds(0, count * SP)],
            dst_ref=all_dx.at[pl.ds(0, count * SP)],
            send_sem=send,
            recv_sem=recv,
            device_id=targets["core"],
            device_id_type=MESH,
        )

    def own_block():
        own = pltpu.make_async_copy(block, dx_part(par, z), dx_own)
        own.start()
        own.wait()
        pl.when(z < 3)(lambda: line(z, "up").start())
        pl.when(z > 0)(lambda: line(z, "down").start())
        aside(z)

    pl.when(in_line)(own_block)

    def from_below(k):
        line(z - k, "up").wait_recv()
        pl.when(z < 3)(lambda: line(z - k, "up").start())
        aside(z - k)

    def from_above(k):
        line(z + k, "down").wait_recv()
        pl.when(z > 0)(lambda: line(z + k, "down").start())
        aside(z + k)

    def tile(t):
        there = pl.ds(pl.multiple_of(t * 128, 128), 128)
        ids = lax.broadcasted_iota(jnp.int32, (128, 16 * SP), 0) + t * 128
        onehot = jnp.where(ids == index[...], 1.0, 0.0).astype(BF16)
        value = nn(onehot, all_dx[...]) * math.sqrt(D)
        total[there, :] = value
        pltpu.make_async_copy(total.at[there], out.at[there], out_sem).start()
        count_squares(value)

    def collect(i):
        for k in range(1, 4):
            pl.when(both(i == HOP * k, z >= k))(lambda k=k: from_below(k))
            pl.when(both(i == HOP * k, z + k <= 3))(lambda k=k: from_above(k))

    def embed(i):
        pl.when(i == HOP)(lambda: crossed(z))
        for k in range(1, 4):
            pl.when(both(i == HOP * (k + 1), z >= k))(lambda k=k: crossed(z - k))
            pl.when(both(i == HOP * (k + 1), z + k <= 3))(lambda k=k: crossed(z + k))
        begin = 4 * HOP + 2
        pl.when(i == begin)(lambda: blocks(8, dx_core_send, dx_core_recv).wait_recv())
        for half in range(2):
            t = 2 * (i - begin) + half
            pl.when(both(t >= 0, t < 17))(lambda t=t: tile(t))

    squares[...] = jnp.zeros_like(squares)

    def count_squares(value):
        folded = value * value
        size = folded.shape[0]
        while size > 8 and size % 16 == 0:
            size //= 2
            folded = folded[:size] + folded[size:]
        for part in range(size // 8):
            squares[...] += folded[part * 8 : (part + 1) * 8]

    def step(i, carry):
        for k in range(5):
            count, rows = (NCC, CC) if k == 4 else (NCH, CH)
            source, _, _, depth = classes[k]
            j = i - LAG * ((5, 5, 4, 4, 3)[k] - depth)
            now = jnp.logical_and(j >= 0, j < count)
            if k == 4:
                now = jnp.logical_and(now, c == 0)
            pl.when(jnp.logical_and(now, jnp.logical_not(source)))(
                lambda k=k, j=j, rows=rows: relay(k, j, rows)
            )
            pl.when(jnp.logical_and(now, source))(lambda k=k, j=j, rows=rows: finish(k, j, rows))
        pl.when(in_line)(lambda: collect(i))
        pl.when(first)(lambda: embed(i))
        return carry

    lax.fori_loop(0, max(NCH + 5 * LAG, 4 * HOP + 2 + 9), step, 0)
    pl.when(first)(lambda: blocks(8, dx_core_send, dx_core_recv).wait_send())

    def dx_sent(count):
        blocks(count, dx_send, dx_core_recv).wait_send()

    middle = both(z >= 1, z <= 2)
    ends = jnp.logical_not(middle)
    pl.when(both(first, ends))(lambda: dx_sent(1))
    pl.when(both(first, middle))(lambda: dx_sent(5))
    pl.when(both(second, ends))(lambda: dx_sent(5))
    pl.when(both(second, middle))(lambda: dx_sent(9))
    for k in range(5):
        rows = NCC * CC if k == 4 else HALF
        source, _, parents, _ = classes[k]
        whole = pl.ds(held(k), rows)
        sent_core = pltpu.make_async_remote_copy(
            src_ref=grads.at[pl.ds(0, rows)],
            dst_ref=rx_core.at[whole],
            send_sem=core_send.at[k],
            recv_sem=core_c.at[0],
            device_id=targets["core"],
            device_id_type=MESH,
        )
        sent = pltpu.make_async_remote_copy(
            src_ref=loc.at[whole],
            dst_ref=rx_x.at[whole],
            send_sem=send_sem.at[k],
            recv_sem=core_c.at[0],
            device_id=targets["x"],
            device_id_type=MESH,
        )
        if k == 4:
            pl.when(c == 1)(sent_core.wait_send)
            pl.when(jnp.logical_and(jnp.logical_not(source), c == 0))(sent.wait_send)
        else:
            sent_core.wait_send()
            pl.when(jnp.logical_not(source))(sent.wait_send)
    done_all = pltpu.make_async_copy(total, out, out_sem)
    part = pl.ds(0, NCC * CC)
    done_few = pltpu.make_async_copy(total.at[part], out.at[part], out_sem)
    pl.when(jnp.logical_or(jnp.logical_and(home, z < 2), sec == 0))(done_all.wait)
    pl.when(classes[4][0])(done_few.wait)


def reduce_and_scatter(grads, start, block, index):
    rows = LANE + NCC * CC
    return pl.pallas_call(
        close_kernel,
        out_shape=(
            jax.ShapeDtypeStruct((2 * HALF, D), F32),
            jax.ShapeDtypeStruct((8, D), F32),
        ),
        in_specs=[ANY, ANY, VMEM, VMEM],
        out_specs=(ANY, VMEM),
        input_output_aliases={1: 0},
        scratch_shapes=[pltpu.VMEM((rows, D), BF16)] * 5
        + [
            pltpu.VMEM((2 * HALF, D), F32),
            pltpu.VMEM((CH, D), F32),
            pltpu.VMEM((16 * SP, D), BF16),
            pltpu.SemaphoreType.DMA((5,)),
            pltpu.SemaphoreType.DMA((4, NCH)),
            pltpu.SemaphoreType.DMA((NCC,)),
            pltpu.SemaphoreType.DMA((3, 4, NCH)),
            pltpu.SemaphoreType.DMA((3, NCC)),
            pltpu.SemaphoreType.DMA((5,)),
            pltpu.SemaphoreType.DMA((5,)),
            pltpu.SemaphoreType.DMA,
            pltpu.SemaphoreType.DMA,
            pltpu.SemaphoreType.DMA,
            pltpu.SemaphoreType.DMA((4,)),
            pltpu.SemaphoreType.DMA((4,)),
            pltpu.SemaphoreType.DMA,
            pltpu.SemaphoreType.DMA,
        ],
        compiler_params=pltpu.CompilerParams(
            collective_id=1, has_side_effects=True, vmem_limit_bytes=60 * 2**20
        ),
        name="reduce_and_scatter",
    )(grads, start, block, index)


def share_kernel(n_sec, n_dp, block, out, send_sem, recv_sem, own_sem):
    sec = lax.axis_index("section")
    dp = lax.axis_index("dp")
    n = n_sec * n_dp
    me = sec * n_dp + dp
    barrier = pltpu.get_barrier_semaphore()
    own = pltpu.make_async_copy(block, out.at[me], own_sem)
    own.start()

    def peer(k):
        other = lax.rem(me + k, n)
        return (other // n_dp, lax.rem(other, n_dp))

    def greet(k, carry):
        pl.semaphore_signal(barrier, 1, device_id=peer(k), device_id_type=MESH)
        return carry

    lax.fori_loop(1, n, greet, 0)
    pl.semaphore_wait(barrier, n - 1)

    def send(k, carry):
        pltpu.make_async_remote_copy(
            src_ref=block,
            dst_ref=out.at[me],
            send_sem=send_sem,
            recv_sem=recv_sem,
            device_id=peer(k),
            device_id_type=MESH,
        ).start()
        return carry

    lax.fori_loop(1, n, send, 0)
    every = pltpu.make_async_remote_copy(
        src_ref=out.at[pl.ds(0, n - 1)],
        dst_ref=out.at[pl.ds(0, n - 1)],
        send_sem=send_sem,
        recv_sem=recv_sem,
        device_id=peer(1),
        device_id_type=MESH,
    )
    own.wait()
    every.wait_send()
    every.wait_recv()


def share(block, n_sec, n_dp, cid, name):
    return pl.pallas_call(
        functools.partial(share_kernel, n_sec, n_dp),
        out_shape=jax.ShapeDtypeStruct((n_sec * n_dp,) + block.shape, block.dtype),
        in_specs=[VMEM],
        out_specs=VMEM,
        scratch_shapes=[
            pltpu.SemaphoreType.DMA,
            pltpu.SemaphoreType.DMA,
            pltpu.SemaphoreType.DMA,
        ],
        compiler_params=pltpu.CompilerParams(collective_id=cid, has_side_effects=True),
        name=name,
    )(block)


def share_row_kernel(n_dp, block, out, send_sem, recv_sem, own_sem):
    sec = lax.axis_index("section")
    me = lax.axis_index("dp")
    barrier = pltpu.get_barrier_semaphore()
    own = pltpu.make_async_copy(block, out.at[me], own_sem)
    own.start()
    for k in range(1, n_dp):
        pl.semaphore_signal(
            barrier, 1, device_id=(sec, lax.rem(me + k, n_dp)), device_id_type=MESH
        )
    pl.semaphore_wait(barrier, n_dp - 1)
    for k in range(1, n_dp):
        pltpu.make_async_remote_copy(
            src_ref=block,
            dst_ref=out.at[me],
            send_sem=send_sem,
            recv_sem=recv_sem,
            device_id=(sec, lax.rem(me + k, n_dp)),
            device_id_type=MESH,
        ).start()
    every = pltpu.make_async_remote_copy(
        src_ref=out.at[pl.ds(0, n_dp - 1)],
        dst_ref=out.at[pl.ds(0, n_dp - 1)],
        send_sem=send_sem,
        recv_sem=recv_sem,
        device_id=(sec, lax.rem(me + 1, n_dp)),
        device_id_type=MESH,
    )
    own.wait()
    every.wait_send()
    every.wait_recv()


def share_row(block, n_dp, cid, name):
    return pl.pallas_call(
        functools.partial(share_row_kernel, n_dp),
        out_shape=jax.ShapeDtypeStruct((n_dp,) + block.shape, block.dtype),
        in_specs=[VMEM],
        out_specs=VMEM,
        scratch_shapes=[
            pltpu.SemaphoreType.DMA,
            pltpu.SemaphoreType.DMA,
            pltpu.SemaphoreType.DMA,
        ],
        compiler_params=pltpu.CompilerParams(collective_id=cid, has_side_effects=True),
        name=name,
    )(block)


def picked_kernel(block, out, own_sem, send_sem, recv_sem, core_send, core_recv):
    sec, dp, z, c, par, home = place()
    last = sec == 3
    upper = sec >= 2
    barrier = pltpu.get_barrier_semaphore()

    def greet(s, e):
        pl.semaphore_signal(barrier, 1, device_id=(s, e), device_id_type=MESH)

    def rows(p, zz, lane):
        return pl.ds(pl.multiple_of((2 * (2 * zz + lane) + p) * PICKS, PICKS), PICKS)

    def greet_senders():
        for k in range(4):
            greet(2, 2 * k + c)
        for k in range(1, 4):
            greet(3, 2 * lax.rem(z + k, 4) + c)
        greet(3, dp + 1 - 2 * c)

    pl.when(last)(greet_senders)

    def to(k):
        zz = lax.rem(z + k, 4)
        return pltpu.make_async_remote_copy(
            src_ref=block,
            dst_ref=out.at[rows(par, z, c)],
            send_sem=send_sem,
            recv_sem=recv_sem.at[par, z],
            device_id=(3, 2 * zz + c),
            device_id_type=MESH,
        )

    def forward(p, k):
        zz = lax.rem(z + k, 4)
        return pltpu.make_async_remote_copy(
            src_ref=out.at[rows(p, zz, c)],
            dst_ref=out.at[rows(p, zz, c)],
            send_sem=core_send,
            recv_sem=core_recv,
            device_id=(3, dp + 1 - 2 * c),
            device_id_type=MESH,
        )

    def came(p, k):
        zz = lax.rem(z + k, 4)
        return pltpu.make_async_remote_copy(
            src_ref=block,
            dst_ref=out.at[rows(p, zz, c)],
            send_sem=send_sem,
            recv_sem=recv_sem.at[p, zz],
            device_id=(3, dp),
            device_id_type=MESH,
        )

    def every(count):
        return pltpu.make_async_remote_copy(
            src_ref=out.at[pl.ds(0, count * PICKS)],
            dst_ref=out.at[pl.ds(0, count * PICKS)],
            send_sem=core_send,
            recv_sem=core_recv,
            device_id=(3, dp),
            device_id_type=MESH,
        )

    def all_sent(count):
        return pltpu.make_async_remote_copy(
            src_ref=out.at[pl.ds(0, count * PICKS)],
            dst_ref=out.at[pl.ds(0, count * PICKS)],
            send_sem=send_sem,
            recv_sem=core_recv,
            device_id=(3, dp),
            device_id_type=MESH,
        )

    def second():
        pl.semaphore_wait(barrier, 4)
        for k in range(4):
            to(k).start()
        all_sent(4).wait_send()

    def third():
        own = pltpu.make_async_copy(block, out.at[rows(1, z, c)], own_sem)
        own.start()
        pl.semaphore_wait(barrier, 4)
        for k in range(1, 4):
            to(k).start()
        own.wait()
        forward(1, 0).start()
        for k in range(4):
            came(0, k).wait_recv()
            forward(0, k).start()
            if k:
                came(1, k).wait_recv()
                forward(1, k).start()
        all_sent(3).wait_send()
        every(8).wait_send()
        every(8).wait_recv()

    def none():
        out[...] = jnp.zeros_like(out)

    pl.when(sec == 2)(second)
    pl.when(last)(third)
    pl.when(jnp.logical_not(last))(none)


def share_picked(block):
    return pl.pallas_call(
        picked_kernel,
        out_shape=jax.ShapeDtypeStruct((16 * PICKS, D), BF16),
        in_specs=[VMEM],
        out_specs=VMEM,
        scratch_shapes=[
            pltpu.SemaphoreType.DMA,
            pltpu.SemaphoreType.DMA,
            pltpu.SemaphoreType.DMA((2, 4)),
            pltpu.SemaphoreType.DMA,
            pltpu.SemaphoreType.DMA,
        ],
        compiler_params=pltpu.CompilerParams(collective_id=4, has_side_effects=True),
        name="share_picked",
    )(block)


def unpick_kernel(part, out, rx_core, low, rx, core_send, core_recv, send_sem, recv_sem):
    sec, dp, z, c, par, home = place()
    barrier = pltpu.get_barrier_semaphore()

    def greet(s, e):
        pl.semaphore_signal(barrier, 1, device_id=(s, e), device_id_type=MESH)

    def greet_senders():
        for k in range(4):
            pl.when(jnp.logical_or(sec == 2, 2 * k + c != dp))(lambda k=k: greet(3, 2 * k + c))

    pl.when(sec >= 2)(greet_senders)
    pl.when(sec == 3)(lambda: greet(3, dp + 1 - 2 * c))

    def row(p, zz, lane):
        return (2 * (2 * zz + lane) + p) * PICKS

    def swap(p, zz):
        place_there = (2 * zz + p) * PICKS
        return pltpu.make_async_remote_copy(
            src_ref=part.at[pl.ds(pl.multiple_of(row(p, zz, 1 - c), PICKS), PICKS)],
            dst_ref=rx_core.at[pl.ds(place_there, PICKS)],
            send_sem=core_send,
            recv_sem=core_recv,
            device_id=(3, dp + 1 - 2 * c),
            device_id_type=MESH,
        )

    def to(p, k):
        zz = lax.rem(z + k, 4)
        return pltpu.make_async_remote_copy(
            src_ref=low.at[pl.ds(pl.multiple_of((2 * zz + p) * PICKS, PICKS), PICKS)],
            dst_ref=rx.at[z],
            send_sem=send_sem,
            recv_sem=recv_sem,
            device_id=(2 + p, 2 * zz + c),
            device_id_type=MESH,
        )

    def third():
        pl.semaphore_wait(barrier, 8)
        for zz in range(4):
            for p in range(2):
                swap(p, zz).start()
        whole = pltpu.make_async_remote_copy(
            src_ref=rx_core,
            dst_ref=rx_core,
            send_sem=core_send,
            recv_sem=core_recv,
            device_id=(3, dp),
            device_id_type=MESH,
        )
        whole.wait_recv()
        for zz in range(4):
            for p in range(2):
                there = pl.ds((2 * zz + p) * PICKS, PICKS)
                mine = part[pl.ds(pl.multiple_of(row(p, zz, c), PICKS), PICKS), :]
                low[there, :] = (mine + rx_core[there, :]).astype(BF16)
        for k in range(4):
            to(0, k).start()
            if k:
                to(1, k).start()
        whole.wait_send()
        pltpu.make_async_remote_copy(
            src_ref=low.at[pl.ds(0, 7 * PICKS)],
            dst_ref=low.at[pl.ds(0, 7 * PICKS)],
            send_sem=send_sem,
            recv_sem=recv_sem,
            device_id=(3, dp),
            device_id_type=MESH,
        ).wait_send()
        pltpu.make_async_remote_copy(
            src_ref=rx.at[pl.ds(0, 3)],
            dst_ref=rx.at[pl.ds(0, 3)],
            send_sem=send_sem,
            recv_sem=recv_sem,
            device_id=(3, dp),
            device_id_type=MESH,
        ).wait_recv()
        rx[z] = low[pl.ds(pl.multiple_of((2 * z + 1) * PICKS, PICKS), PICKS), :]

    def second():
        pltpu.make_async_remote_copy(
            src_ref=rx,
            dst_ref=rx,
            send_sem=send_sem,
            recv_sem=recv_sem,
            device_id=(3, dp),
            device_id_type=MESH,
        ).wait_recv()

    def none():
        rx[...] = jnp.zeros_like(rx)

    pl.when(sec == 3)(third)
    pl.when(sec == 2)(second)
    pl.when(sec < 2)(none)
    summed = rx[0].astype(F32)
    for k in range(1, 4):
        summed = summed + rx[k].astype(F32)
    out[...] = summed


def unpick(part):
    return pl.pallas_call(
        unpick_kernel,
        out_shape=jax.ShapeDtypeStruct((PICKS, D), F32),
        in_specs=[VMEM],
        out_specs=VMEM,
        scratch_shapes=[
            pltpu.VMEM((8 * PICKS, D), F32),
            pltpu.VMEM((8 * PICKS, D), BF16),
            pltpu.VMEM((4, PICKS, D), BF16),
            pltpu.SemaphoreType.DMA,
            pltpu.SemaphoreType.DMA,
            pltpu.SemaphoreType.DMA,
            pltpu.SemaphoreType.DMA,
        ],
        compiler_params=pltpu.CompilerParams(collective_id=5, has_side_effects=True),
        name="unpick",
    )(part)


NEG = -1e30
FT = 256


def turn(block, cosine, sine, lanes):
    ahead = pltpu.roll(block, 96, 1)
    behind = pltpu.roll(block, 32, 1)
    return block * cosine + jnp.where(lax.rem(lanes, 64) < 32, ahead, behind) * sine


def see(seg_rows, seg_cols):
    rows = lax.broadcasted_iota(jnp.int32, (SP, SP), 0)
    cols = lax.broadcasted_iota(jnp.int32, (SP, SP), 1)
    allowed = jnp.logical_and(seg_rows[...] == seg_cols[...], cols <= rows)
    return jnp.where(allowed, 0.0, NEG)


def softmax_of(scores, unseen):
    masked = scores + unseen
    grown = jnp.exp(masked - jnp.max(masked, axis=-1, keepdims=True))
    return grown / jnp.sum(grown, axis=-1, keepdims=True)


def weight_copies(w_any, w, sems):
    bounds = (0, 3 * D, 4 * D, 4 * D + FF, 4 * D + 2 * FF, MATS, WROWS)
    return [
        pltpu.make_async_copy(
            w_any.at[pl.ds(lo, hi - lo)], w.at[pl.ds(lo, hi - lo)], sems.at[i]
        )
        for i, (lo, hi) in enumerate(zip(bounds[:-1], bounds[1:]))
    ]


def forward_kernel(
    x, w_any, cosine, sine, seg_rows, seg_cols, y, q, k, v, o, h, gate, up, w, m, unseen, sems
):
    copies = weight_copies(w_any, w, sems)
    for i in (5, 0, 1, 2, 3, 4):
        copies[i].start()
    unseen[...] = see(seg_rows, seg_cols)
    lanes = lax.broadcasted_iota(jnp.int32, (SP, 128), 1)
    first = lanes < 64
    copies[5].wait()
    gains = w[pl.ds(MATS, 16), :].astype(F32)
    stream = x[...].astype(F32)
    a1 = rms_scale(stream, gains[0:1]).astype(BF16)
    copies[0].wait()

    def project(b, carry):
        cols = pl.ds(pl.multiple_of(b * 256, 256), 256)
        raw_q = nn(a1, w[pl.ds(0, D), cols])
        raw_k = nn(a1, w[pl.ds(D, D), cols])
        raw_v = nn(a1, w[pl.ds(2 * D, D), cols])
        v[:, cols] = raw_v.astype(BF16)
        for part in range(2):
            there = pl.ds(pl.multiple_of(b * 256 + part * 128, 128), 128)
            here = slice(part * 128, (part + 1) * 128)
            turned_q = turn(raw_q[:, here], cosine[...], sine[...], lanes)
            q[:, there] = (turned_q * HD ** (-0.5)).astype(BF16)
            k[:, there] = turn(raw_k[:, here], cosine[...], sine[...], lanes).astype(BF16)
        return carry

    lax.fori_loop(0, D // 256, project, 0)

    def attend(b, carry):
        cols = pl.ds(pl.multiple_of(b * 128, 128), 128)
        qb, kb, vb = q[:, cols], k[:, cols], v[:, cols]
        zero = jnp.zeros_like(qb)
        p0 = softmax_of(nt(jnp.where(first, qb, zero), kb), unseen[...]).astype(BF16)
        p1 = softmax_of(nt(jnp.where(first, zero, qb), kb), unseen[...]).astype(BF16)
        o[:, cols] = jnp.where(first, nn(p0, vb), nn(p1, vb)).astype(BF16)
        return carry

    lax.fori_loop(0, HEADS // 2, attend, 0)
    copies[1].wait()
    for b in range(3):
        cols = pl.ds(b * 256, 256)
        h[:, cols] = x[:, cols].astype(F32) + nn(o[...], w[pl.ds(3 * D, D), cols])
    a2 = rms_scale(h[...], gains[1:2]).astype(BF16)
    copies[2].wait()
    copies[3].wait()

    def widen(b, carry):
        cols = pl.ds(pl.multiple_of(b * FT, FT), FT)
        g = nt(a2, w[pl.ds(pl.multiple_of(4 * D + b * FT, FT), FT), :])
        u = nt(a2, w[pl.ds(pl.multiple_of(4 * D + FF + b * FT, FT), FT), :])
        gate[:, cols] = g
        up[:, cols] = u
        m[:, cols] = (g / (1.0 + jnp.exp(-g)) * u).astype(BF16)
        return carry

    lax.fori_loop(0, FF // FT, widen, 0)
    copies[4].wait()

    def narrow(b, carry):
        cols = pl.ds(pl.multiple_of(b * 256, 256), 256)
        y[:, cols] = (h[:, cols] + nn(m[...], w[pl.ds(4 * D + 2 * FF, FF), cols])).astype(BF16)
        return carry

    lax.fori_loop(0, 3, narrow, 0)


def forward_call(x, weights, cosine, sine, seg_rows, seg_cols):
    low = jax.ShapeDtypeStruct((SP, D), BF16)
    wide = jax.ShapeDtypeStruct((SP, FF), F32)
    return pl.pallas_call(
        forward_kernel,
        out_shape=(low, low, low, low, low, jax.ShapeDtypeStruct((SP, D), F32), wide, wide),
        in_specs=[VMEM, ANY, VMEM, VMEM, VMEM, VMEM],
        out_specs=(VMEM,) * 8,
        scratch_shapes=[
            pltpu.VMEM((WROWS, D), BF16),
            pltpu.VMEM((SP, FF), BF16),
            pltpu.VMEM((SP, SP), F32),
            pltpu.SemaphoreType.DMA((6,)),
        ],
        compiler_params=pltpu.CompilerParams(vmem_limit_bytes=48 * 2**20),
        name="layer_forward",
    )(x, weights, cosine, sine, seg_rows, seg_cols)


def rms_back(value_in, gain, grad):
    inv = lax.rsqrt(jnp.mean(value_in * value_in, axis=-1, keepdims=True) + norm_eps)
    unit = value_in * inv
    scaled = grad * gain
    grad_in = inv * (scaled - unit * jnp.mean(scaled * unit, axis=-1, keepdims=True))
    return grad_in, jnp.sum(grad * unit, axis=0, keepdims=True)


def backward_kernel(
    with_weights, dy, x, w_any, cosine, sine, seg_rows, seg_cols, q, k, v, o, h, gate, up, *refs
):
    if with_weights:
        dx, grads, w, dgate, dup, m, da, do, dq, dk, dv, unseen, sems = refs
    else:
        dx, w, dgate, dup, m, da, do, dq, dk, dv, unseen, sems = refs
    copies = weight_copies(w_any, w, sems)
    for i in (4, 5, 2, 3, 1, 0):
        copies[i].start()
    unseen[...] = see(seg_rows, seg_cols)
    lanes = lax.broadcasted_iota(jnp.int32, (SP, 128), 1)
    first = lanes < 64
    copies[4].wait()

    def open_mlp(b, carry):
        cols = pl.ds(pl.multiple_of(b * FT, FT), FT)
        dm = nt(dy[...], w[pl.ds(pl.multiple_of(4 * D + 2 * FF + b * FT, FT), FT), :])
        g = gate[:, cols]
        u = up[:, cols]
        sig = 1.0 / (1.0 + jnp.exp(-g))
        dgate[:, cols] = (dm * u * sig * (1.0 + g * (1.0 - sig))).astype(BF16)
        dup[:, cols] = (dm * g * sig).astype(BF16)
        if with_weights:
            m[:, cols] = (g * sig * u).astype(BF16)
        return carry

    lax.fori_loop(0, FF // FT, open_mlp, 0)
    copies[5].wait()
    gains = w[pl.ds(MATS, 16), :].astype(F32)
    copies[2].wait()
    copies[3].wait()

    def close_mlp(b, carry):
        cols = pl.ds(pl.multiple_of(b * 256, 256), 256)
        da[:, cols] = nn(dgate[...], w[pl.ds(4 * D, FF), cols]) + nn(
            dup[...], w[pl.ds(4 * D + FF, FF), cols]
        )
        return carry

    lax.fori_loop(0, 3, close_mlp, 0)
    dh, dg_mlp = rms_back(h[...], gains[1:2], da[...])
    dh = dh + dy[...].astype(F32)
    db = dh.astype(BF16)
    copies[1].wait()
    for b in range(3):
        do[:, pl.ds(b * 256, 256)] = nt(db, w[pl.ds(3 * D + b * 256, 256), :]).astype(BF16)

    def attend(b, carry):
        cols = pl.ds(pl.multiple_of(b * 128, 128), 128)
        qb, kb, vb, dob = q[:, cols], k[:, cols], v[:, cols], do[:, cols]
        zero = jnp.zeros_like(qb)
        parts = []
        for head in range(2):
            keep = first if head == 0 else jnp.logical_not(first)
            probs = softmax_of(nt(jnp.where(keep, qb, zero), kb), unseen[...])
            dprobs = nt(jnp.where(keep, dob, zero), vb)
            along = jnp.sum(probs * dprobs, axis=-1, keepdims=True)
            dscores = (probs * (dprobs - along)).astype(BF16)
            parts.append((nn(dscores, kb), tn(dscores, qb), tn(probs.astype(BF16), dob)))
        dqb = jnp.where(first, parts[0][0], parts[1][0]) * HD ** (-0.5)
        dkb = jnp.where(first, parts[0][1], parts[1][1])
        dq[:, cols] = turn(dqb, cosine[...], -sine[...], lanes).astype(BF16)
        dk[:, cols] = turn(dkb, cosine[...], -sine[...], lanes).astype(BF16)
        dv[:, cols] = jnp.where(first, parts[0][2], parts[1][2]).astype(BF16)
        return carry

    lax.fori_loop(0, HEADS // 2, attend, 0)
    copies[0].wait()
    for b in range(3):
        rows = lambda i, b=b: w[pl.ds(i * D + b * 256, 256), :]
        da[:, pl.ds(b * 256, 256)] = (
            nt(dq[...], rows(0)) + nt(dk[...], rows(1)) + nt(dv[...], rows(2))
        )
    stream = x[...].astype(F32)
    dstream, dg_attn = rms_back(stream, gains[0:1], da[...])
    dx[...] = (dstream + dh).astype(BF16)
    if not with_weights:
        return
    a1 = rms_scale(stream, gains[0:1]).astype(BF16)
    a2 = rms_scale(h[...], gains[1:2]).astype(BF16)
    for b in range(3):
        cols = slice(b * 256, (b + 1) * 256)
        piece = a1[:, cols]
        for i, right in enumerate((dq, dk, dv)):
            grads[pl.ds(i * D + b * 256, 256), :] = tn(piece, right[...]).astype(BF16)
        grads[pl.ds(3 * D + b * 256, 256), :] = tn(o[:, cols], db).astype(BF16)

    def outer(b, carry):
        cols = pl.ds(pl.multiple_of(b * FT, FT), FT)
        base = 4 * D + b * FT
        for i, (left, right) in enumerate(((dgate, a2), (dup, a2), (m, dy))):
            there = pl.ds(pl.multiple_of(base + i * FF, FT), FT)
            grads[there, :] = tn(left[:, cols], right[...]).astype(BF16)
        return carry

    lax.fori_loop(0, FF // FT, outer, 0)
    tail = lax.broadcasted_iota(jnp.int32, (16, D), 0)
    grads[pl.ds(MATS, 16), :] = jnp.where(
        tail == 0, dg_attn, jnp.where(tail == 1, dg_mlp, 0.0)
    ).astype(BF16)


def backward_call(with_weights, dy, x, weights, cosine, sine, seg_rows, seg_cols, kept):
    low = jax.ShapeDtypeStruct((SP, D), BF16)
    out_shape = (low, jax.ShapeDtypeStruct((WROWS, D), BF16)) if with_weights else low
    wide = pltpu.VMEM((SP, FF), BF16)
    narrow = pltpu.VMEM((SP, D), BF16)
    return pl.pallas_call(
        functools.partial(backward_kernel, with_weights),
        out_shape=out_shape,
        in_specs=[VMEM, VMEM, ANY] + [VMEM] * 11,
        out_specs=(VMEM, VMEM) if with_weights else VMEM,
        scratch_shapes=[
            pltpu.VMEM((WROWS, D), BF16),
            wide,
            wide,
            wide,
            pltpu.VMEM((SP, D), F32),
            narrow,
            narrow,
            narrow,
            narrow,
            pltpu.VMEM((SP, SP), F32),
            pltpu.SemaphoreType.DMA((6,)),
        ],
        compiler_params=pltpu.CompilerParams(vmem_limit_bytes=60 * 2**20),
        name="layer_backward_weights" if with_weights else "layer_backward",
    )(dy, x, weights, cosine, sine, seg_rows, seg_cols, *kept)


def shards(codes, labels, picks, classes, null_mask, starts, master, momentum, average):
    sec = lax.axis_index("section")
    d = lax.axis_index("dp")
    n_dp = lax.axis_size("dp")
    n_sec = lax.axis_size("section")
    par = lax.rem(sec, 2)
    own = master.shape[0]
    learn_rate = rate_factor * math.sqrt(own * n_sec * n_dp)
    embed_factor = math.sqrt(D)
    beside = [(0, 1), (1, 0), (2, 3), (3, 2)]
    fast = n_sec == 4 and n_dp == 8 and own == 2 * HALF
    table = master.astype(BF16)
    gain_row = lax.slice_in_dim(table, VOCAB % own, VOCAB % own + 1)[0].astype(F32)
    gain_at = VOCAB // own

    row_index, counted, segment, position = jax.vmap(row_layout)(starts, classes, null_mask, codes)
    picked_labels = jnp.take_along_axis(labels, picks, axis=1)
    picked_counts = jnp.take_along_axis(counted, picks, axis=1).astype(jnp.int32)
    row_index = jnp.pad(row_index, ((0, 0), (0, SP - SLOTS)), constant_values=-1)
    info = jnp.concatenate([row_index, picked_labels, picked_counts], axis=1)
    if fast:
        block = jnp.concatenate([info.reshape(-1).astype(F32), gain_row])
        block = jnp.pad(block, (0, 2048 - block.shape[0])).reshape(16, 128)
        info = share(block, n_sec, n_dp, 2, "share_info").reshape(n_sec, n_dp, 2048)
        g_f = info[3, gain_at, 2 * (SP + 2 * PICKS) :][:D]
        info = info[0, :, : 2 * (SP + 2 * PICKS)].reshape(2 * n_dp, -1).astype(jnp.int32)
    else:
        info = lax.all_gather(info, "dp", axis=0, tiled=True)
        holds = (sec == 3) & (d == gain_at)
        g_f = lax.psum(jnp.where(holds, gain_row, 0.0), ("section", "dp"))
    all_index = info[:, :SP].reshape(-1)
    all_labels = info[:, SP : SP + PICKS].reshape(-1)
    all_counts = info[:, SP + PICKS :].reshape(-1).astype(F32)
    segment = jnp.pad(segment[par], (0, SP - SLOTS), constant_values=SEGS + 2)
    position = jnp.pad(position[par], (0, SP - SLOTS))
    frequency = rope_base ** (-jnp.arange(HD // 2, dtype=F32) * 2.0 / HD)
    angles = position.astype(F32)[:, None] * frequency[None, :]
    cosine = jnp.tile(jnp.cos(angles), (1, 4))
    sine = jnp.tile(jnp.concatenate([-jnp.sin(angles), jnp.sin(angles)], axis=1), (1, 2))
    around = (cosine, sine, segment[:, None], segment[None, :])

    local = jnp.where(sec == 0, all_index, -1) - d * own
    if fast:
        weights, x0 = gather_and_embed(table, local[:, None])
    else:
        gathered = lax.all_gather(table, "dp", axis=0, tiled=True)[:WROWS]
        other = lax.ppermute(gathered, "section", beside)
        weights = jnp.where((sec == 1) | (sec == 2), gathered, other)
        onehot = (local[:, None] == jnp.arange(own)[None, :]).astype(BF16)
        looked = (nn(onehot, table) * embed_factor).astype(BF16)
        looked = lax.psum_scatter(looked, "dp", scatter_dimension=0, tiled=True).reshape(2, SP, D)
        from_first = lax.ppermute(looked[1], "section", [(0, 1)])
        x0 = jnp.where(sec == 0, looked[0], from_first)

    y0 = forward_call(x0, weights, *around)[0]
    x = jnp.where(sec < 2, x0, lax.ppermute(y0, "section", [(0, 2), (1, 3)]))
    y, *kept = forward_call(x, weights, *around)

    my_picks = picks[par]
    picked = jnp.take(y, my_picks, axis=0)
    if fast:
        all_picked = share_picked(picked)
    else:
        all_picked = lax.all_gather(picked, ("section", "dp"), axis=0, tiled=False)
        all_picked = all_picked.reshape(n_sec, n_dp, PICKS, D)[2:].transpose(1, 0, 2, 3)
    all_picked = all_picked.reshape(-1, D).astype(F32)
    af = jnp.where(sec == 3, rms_scale(all_picked, g_f), 0.0).astype(BF16)
    vocab_ids = d * own + jnp.arange(own)
    logits = jnp.where(vocab_ids[None, :] < VOCAB, nt(af, table), -1e30)
    local_max = jnp.max(logits, axis=1)
    hit = vocab_ids[None, :] == all_labels[:, None]
    sums = jnp.stack(
        [
            local_max,
            jnp.sum(jnp.exp(logits - local_max[:, None]), axis=1),
            jnp.sum(jnp.where(hit, logits, 0.0), axis=1),
        ]
    )
    if fast:
        block = jnp.pad(sums.reshape(-1, 128), ((0, 4), (0, 0)))
        every = share_row(block, n_dp, 3, "share_sums")[:, :12].reshape(n_dp, 3, -1)
    else:
        every = lax.all_gather(sums, "dp", axis=0, tiled=False)
    top = jnp.max(every[:, 0], axis=0)
    total = jnp.sum(every[:, 1] * jnp.exp(every[:, 0] - top), axis=0)
    target = jnp.sum(every[:, 2], axis=0)
    log_total = top + jnp.log(total)
    loss_part = jnp.where(
        (sec == 3) & (d == 0), jnp.sum(jnp.where(all_counts > 0, log_total - target, 0.0)), 0.0
    )
    count_sum = jnp.sum(all_counts)
    dlogits = (jnp.exp(logits - log_total[:, None]) - hit.astype(F32)) * all_counts[:, None]
    dlogits = jnp.where(sec == 3, dlogits, 0.0).astype(BF16)
    d_table = tn(dlogits, af)
    if fast:
        daf = unpick(nn(dlogits, table))
    else:
        daf = lax.psum(nn(dlogits, table), "dp")
        daf = lax.dynamic_slice_in_dim(daf, d * 2 * PICKS, 2 * PICKS).reshape(2, PICKS, D)
        daf = jnp.where(sec == 3, daf[1], lax.ppermute(daf[0], "section", [(3, 2)]))
    d_own, dg_f = rms_pull(picked.astype(F32), g_f, daf)
    dg_f = jnp.where(sec >= 2, dg_f, 0.0)
    spread = (jnp.arange(SP)[:, None] == my_picks[None, :]).astype(F32)
    d_top = jnp.dot(spread, d_own, precision=lax.Precision.HIGHEST).astype(BF16)
    dx1 = backward_call(False, d_top, x, weights, *around, kept)
    dy = jnp.where(sec < 2, lax.ppermute(dx1, "section", [(2, 0), (3, 1)]), d_top)
    dx0, grads = backward_call(True, dy, x, weights, *around, kept)

    if fast:
        grad, squares = reduce_and_scatter(grads, d_table, dx0, local[None, :])
        squares = jnp.sum(squares) + jnp.sum(d_table * d_table)
    else:
        grads = grads.astype(F32) + lax.ppermute(grads, "section", beside).astype(F32)
        grads = jnp.pad(grads.astype(BF16), ((0, own * n_dp - WROWS), (0, 0)))
        grad = lax.psum_scatter(grads, "dp", scatter_dimension=0, tiled=True).astype(F32)
        grad = jnp.where(sec == 3, d_table, grad)
        pair = jnp.stack([dx0, lax.ppermute(dx0, "section", [(1, 0)])])
        all_dx = lax.all_gather(pair, "dp", axis=0, tiled=True).reshape(-1, D)
        grad = jnp.where(sec == 0, tn(onehot, all_dx) * embed_factor, grad)
        squares = jnp.sum(grad * grad)

    if fast:
        block = jnp.concatenate([dg_f, jnp.stack([squares, loss_part]), jnp.zeros((254,), F32)])
        totals = jnp.sum(share(block.reshape(8, 128), n_sec, n_dp, 8, "share_norm"), axis=0)
        totals = totals.reshape(-1)
        dg_f, squares, loss_sum = totals[:D], totals[D], totals[D + 1]
    else:
        dg_f, squares, loss_sum = lax.psum((dg_f, squares, loss_part), ("section", "dp"))
    grad_norm = jnp.sqrt(squares + jnp.sum(dg_f * dg_f))
    gain_here = (jnp.arange(own) == VOCAB % own)[:, None] & (sec == 3) & (d == gain_at)
    grad = grad + jnp.where(gain_here, dg_f[None, :], 0.0)
    clipped = grad * jnp.minimum(1.0, clip_limit / (grad_norm + norm_eps))
    new_momentum = momentum_decay * momentum + clipped
    new_master = master - learn_rate * (clipped + momentum_decay * new_momentum)
    new_average = average_decay * average + (1.0 - average_decay) * new_master
    return loss_sum, count_sum, grad_norm, new_master, new_momentum, new_average


def solution(mesh):
    split = P("dp", None)
    whole = P(("section", "dp"), None)
    return jax.shard_map(
        shards,
        mesh=mesh,
        in_specs=(split,) * 6 + (whole,) * 3,
        out_specs=(P(), P(), P(), whole, whole, whole),
        check_vma=False,
    )
```

time: 3030 us -> 535 us (0.18)
  waiting for transfers between devices: 1460 us -> 38.7 us
  other arithmetic: 504 us -> 38.7 us
  local copies, waits for them, and re-layouts: 448 us -> 23 us
  Pallas kernels: 0 us -> 402 us
  starting transfers between devices: 315 us -> 2.82 us
  loops' own time: 219 us -> 0 us
  blocking collectives: 38 us -> 0 us
    reduce_scatter x1 -> x0, waiting for transfers between devices: 688 us -> none  [shards(): lax.psum_scatter(grad_acc, 'dp', scatter_dimension=0, tiled=True)]
    ppermute x8 -> x2, waiting for transfers between devices: 544 us -> 38.7 us  [the longest x1 32.3 us: shards(): lax.ppermute(dx1, 'section', [(2, 0), (3, 1)])]
    pallas_call x0 -> x11, Pallas kernels: none -> 402 us  [the longest x1 137 us: reduce_and_scatter(): pl.pallas_call(close_kernel, out_shape=(jax.ShapeDtypeStruct((2 * HALF, D...]
    ppermute x8 -> x2, starting transfers between devices: 315 us -> 2.82 us  [the longest x1 1.5 us: shards(): lax.ppermute(dx1, 'section', [(2, 0), (3, 1)])]
    all_gather x1 -> x0, waiting for transfers between devices: 230 us -> none  [shards(): lax.all_gather(master.astype(jnp.bfloat16), 'dp', axis=0, tiled=True)]
    scatter x99 -> x0, other arithmetic: 202 us -> none  [the longest x95 195 us: shards(): stash.at[slot_mb].set(jnp.where(active, fresh, stash[slot_mb]))]
    scatter-add x5 -> x0, other arithmetic: 183 us -> none  [embed_backward(): grad_acc.at[row_index].add(grad_in.astype(jnp.float32) * embed_factor)]
    dynamic_slice x104 -> x1, local copies, waits for them, and re-layouts: 141 us -> 0.02 us  [shards(): segment = jnp.pad(segment[par], (0, SP - SLOTS), constant_values=SEGS + 2)]
  transfers between devices with their start and end apart: 10 -> 2, of which waited for: 6 -> 2; matrix products, arithmetic and copies ran while one was open for 10% -> 1% of each run, Pallas kernels for 0% -> 0%
where the time goes in v1:
time: 535 us; the launch traced here: 526 us
  Pallas kernels  402 us (75%)
  other arithmetic  38.7 us (7%)
  waiting for transfers between devices  38.7 us (7%)
  local copies, waits for them, and re-layouts  23 us (4%)
  matrix products  15.2 us (3%)
  between operations  6.06 us (1%)
    pallas_call x1, Pallas kernels, reduce_and_scatter(): pl.pallas_call(close_kernel, out_shape=(jax.ShapeDtypeStruct((2 * HALF, D...  137 us
    pallas_call x1, Pallas kernels, gather_and_embed(): pl.pallas_call(open_kernel, out_shape=(jax.ShapeDtypeStruct((WROWS, D), B...  126 us
    pallas_call x2, Pallas kernels, backward_call(): pl.pallas_call(functools.partial(backward_kernel, with_weights), out_shap...  62 us
    ppermute x1, waiting for transfers between devices, shards(): lax.ppermute(dx1, 'section', [(2, 0), (3, 1)])  32.3 us
    pallas_call x2, Pallas kernels, forward_call(): pl.pallas_call(forward_kernel, out_shape=(low, low, low, low, low, jax.Sh...  31.7 us
    pallas_call x2, Pallas kernels, share(): pl.pallas_call(functools.partial(share_kernel, n_sec, n_dp), out_shape=ja...  26.2 us
    add x1, other arithmetic, shards(): new_average = average_decay * average + (1.0 - average_decay) * new_master  16.7 us
    pallas_call x1, Pallas kernels, share_row(): pl.pallas_call(functools.partial(share_row_kernel, n_dp), out_shape=jax.S...  14.6 us
  transfers between devices with their start and end apart: 2, of which 2 were waited for; matrix products, arithmetic and copies ran while one was open for 1% of the time, Pallas kernels for 0%

profile of v1, /device:TPU:0, one launch (start us, length us, event | category | flops | bytes accessed | tf_op | source)
XLA Modules:
  0.0 526.0 jit_solution(18061157718187670525)
XLA Ops:
  10.0 3.3 convert_element_type.65.table
  13.3 1.7 copy-done.16
  15.7 15.2 %share_info.1 = f32[32,16,128]{2,1,0:T(8,128)} custom-call(f32[16,128]{1,0:T(8,128)} %fusion.36.block), custom_call_target="tpu_custom_call" | custom-call | tf_op jit(solution)/shard_map/share_info/pallas_call | solution.py:807
  32.0 2.4 sub.94.index
  34.4 125.6 %gather_and_embed.1 = (bf16[9232,768]{1,0:T(8,128)(2,1)}, bf16[272,768]{1,0:T(8,128)(2,1)}) custom-call(bf16[2176,768]{1,0:T(8,128)(2,1)} %copy-done.16, s32[4352,1]{1,0:T(8,128)} %sub.94.index), custom_call_target="tpu_custom_call" | custom-call | tf_op jit(solution)/shard_map/gather_and_embed/pallas_call | solution.py:410
  161.0 16.6 %layer_forward.2 = (bf16[272,768]{1,0:T(8,128)(2,1)S(1)}, bf16[272,768]{1,0:T(8,128)(2,1)}, bf16[272,768]{1,0:T(8,128)(2,1)}, bf16[272,768]{1,0:T(8,128)(2,1)}, ...) custom-call(bf16[272,768]{1,0:T(8,128)(2,1)S(1)} %copy-done.8, ...), custom_call_target="tpu_custom_call" | custom-call | tf_op jit(solution)/shard_map/layer_forward/pallas_call | solution.py:1223
  180.0 6.4 %collective-permute-done = bf16[272,768]{1,0:T(8,128)(2,1)S(1)} collective-permute-done((bf16[272,768]{1,0:T(8,128)(2,1)S(1)}, bf16[272,768]{1,0:T(8,128)(2,1)S(1)}, u32[]{:S(2)}, u32[]{:S(2)}) %collective-permute-start) | collective-permute-done | bytes 417824 | tf_op jit(solution)/shard_map/ppermute | solution.py:1433
  186.5 15.1 %layer_forward.3 = (bf16[272,768]{1,0:T(8,128)(2,1)S(1)}, bf16[272,768]{1,0:T(8,128)(2,1)S(1)}, bf16[272,768]{1,0:T(8,128)(2,1)S(1)}, bf16[272,768]{1,0:T(8,128)...) custom-call(bf16[272,768]{1,0:T(8,128)(2,1)S(1)} %broadcast_select_f, ...), custom_call_target="tpu_custom_call" | custom-call | tf_op jit(solution)/shard_map/layer_forward/pallas_call | solution.py:1223
  208.4 2.0 share_picked.1
  211.8 4.4 fusion.49
  216.2 2.1 copy-done.15
  220.1 14.6 %share_sums.1 = f32[8,16,128]{2,1,0:T(8,128)} custom-call(f32[16,128]{1,0:T(8,128)} %pad.24.block), custom_call_target="tpu_custom_call" | custom-call | tf_op jit(solution)/shard_map/share_sums/pallas_call | solution.py:856
  235.7 3.3 fusion.4
  240.3 3.2 fusion.50.part
  243.5 2.1 unpick.1
  247.5 2.2 convolution_convert_fusion.dy
  249.7 24.3 %layer_backward.1 = bf16[272,768]{1,0:T(8,128)(2,1)} custom-call(bf16[272,768]{1,0:T(8,128)(2,1)} %convolution_convert_fusion.dy, bf16[272,768]{1,0:T(8,128)(2,1)} %copy-done.3, bf16[9232,768]{1,0:T(8,128)(2,1)} %get-tuple-element.22.w_any, f32[272,128]{1,0:T(8,128)} %copy-done.6, f32[272,128]{1,0:T(8,128)} %copy-done.5, s32[272,1]{1,0:T(8,128)} %copy-done.4, ...), custom_call_target="tpu_custom_call" | custom-call | tf_op jit(solution)/shard_map/layer_backward/pallas_call | solution.py:1355
  274.0 1.5 collective-permute-start.1
  276.2 5.4 %multiply_reduce_fusion = (f32[]{:T(128)}, f32[2176,768]{1,0:T(8,128)}) fusion(bf16[512,2176]{1,0:T(8,128)(2,1)S(1)} %copy-done.21, bf16[512,768]{1,0:T(8,128)(2,1)S(1)} %copy-done.19, f32[768]{0:T(1024)S(1)} %slice_reduce_fusion.1, f32[512]{0:T(512)S(1)} %add_rsqrt_fusion, pred[]{:T(512)S(6)} %eq.88), kind=kOutput, calls=%fused_computation.7 | convolution fusion | flops 1716584448 | bytes 9704453 | tf_op jit(solution)/shard_map/dot_general | solution.py:40
  281.6 32.3 %collective-permute-done.1 = bf16[272,768]{1,0:T(8,128)(2,1)S(1)} collective-permute-done((bf16[272,768]{1,0:T(8,128)(2,1)}, bf16[272,768]{1,0:T(8,128)(2,1)S(1)}, u32[]{:S(2)}, u32[]{:S(2)}) %collective-permute-start.1) | collective-permute-done | bytes 417824 | tf_op jit(solution)/shard_map/ppermute | solution.py:1483
  314.7 37.7 %layer_backward_weights.1 = (bf16[272,768]{1,0:T(8,128)(2,1)}, bf16[9232,768]{1,0:T(8,128)(2,1)}) custom-call(bf16[272,768]{1,0:T(8,128)(2,1)} %broadcast_select_fusion.dy, bf16[272,768]{1,0:T(8,128)(2,1)} %copy-done.3, bf16[9232,768]{1,0:T(8,128)(2,1)} %get-tuple-element.22.w_any, f32[272,128]{1,0:T(8,128)} %copy-done.6, f32[272,128]{1,0:T(8,128)} %copy-done.5, ...), custom_call_target="tpu_custom_call" | custom-call | tf_op jit(solution)/shard_map/layer_backward_weights/pallas_call | solution.py:1355
  352.4 137.4 %reduce_and_scatter.1 = (f32[2176,768]{1,0:T(8,128)}, f32[8,768]{1,0:T(8,128)}) custom-call(bf16[9232,768]{1,0:T(8,128)(2,1)} %get-tuple-element.32.grads, f32[2176,768]{1,0:T(8,128)} %get-tuple-element.69.start, bf16[272,768]{1,0:T(8,128)(2,1)} %get-tuple-element.33.block, s32[1,4352]{1,0:T(1,128)} %sub.90.index), custom_call_target="tpu_custom_call", output_to_operand_aliasing={{0}: (1, {})} | custom-call | tf_op jit(solution)/shard_map/reduce_and_scatter/pallas_call | solution.py:725
  493.2 11.0 %share_norm.1 = f32[32,8,128]{2,1,0:T(8,128)} custom-call(f32[8,128]{1,0:T(8,128)} %maximum_bitcast_fusion.block), custom_call_target="tpu_custom_call" | custom-call | tf_op jit(solution)/shard_map/share_norm/pallas_call | solution.py:807
  507.7 16.7 %multiply_add_fusion = (f32[2176,768]{1,0:T(8,128)}, f32[2176,768]{1,0:T(8,128)}, f32[2176,768]{1,0:T(8,128)}) fusion(f32[2176,768]{1,0:T(8,128)} %param.17, f32[2176,768]{1,0:T(8,128)} %param.15, f32[]{:T(128)S(6)} %min.15, f32[2176,768]{1,0:T(8,128)} %get-tuple-element.35, f32[768]{0:T(1024)S(1)} %get-tuple-element.57, pred[2176]{0:T(1024)(128)(4,1)S(1)} %fusion.33, ...), kind=kLoop, calls=%fused_computation.3 | loop fusion | flops 20054016 | bytes 46797956 | tf_op jit(solution)/shard_map/add | solution.py:1512
  (125 shorter events, 33.6 us)
Async XLA Ops:
  0.6 5.3 %copy-start = (s32[2,264]{1,0:T(2,128)S(1)}, s32[2,264]{1,0:T(2,128)}, u32[]{:S(2)}) copy-start(s32[2,264]{1,0:T(2,128)} %param.10) | copy-start | bytes 6340
  5.0 181.4 %copy-start.14 = (s32[1,272]{1,0:T(1,128)}, s32[1,272]{1,0:T(1,128)S(1)}, u32[]{:S(2)}) copy-start(s32[1,272]{1,0:T(1,128)S(1)} %broadcast_in_dim.149.seg_cols) | copy-start | bytes 3268
  5.1 181.3 %copy-start.4 = (s32[272,1]{1,0:T(8,128)}, s32[272,1]{1,0:T(8,128)S(1)}, u32[]{:S(2)}) copy-start(s32[272,1]{1,0:T(8,128)S(1)} %broadcast_in_dim.160.seg_rows) | copy-start | bytes 3268
  9.9 176.6 %copy-start.5 = (f32[272,128]{1,0:T(8,128)}, f32[272,128]{1,0:T(8,128)S(1)}, u32[]{:S(2)}) copy-start(f32[272,128]{1,0:T(8,128)S(1)} %copy.35.sine) | copy-start | bytes 417796
  10.0 176.5 %copy-start.6 = (f32[272,128]{1,0:T(8,128)}, f32[272,128]{1,0:T(8,128)S(1)}, u32[]{:S(2)}) copy-start(f32[272,128]{1,0:T(8,128)S(1)} %copy.34.cosine) | copy-start | bytes 417796
  13.3 1.7 copy-start.16
  159.9 1.0 copy-start.8
  160.9 17.9 %copy-start.23 = (s32[2,32]{1,0:T(2,128)S(1)}, s32[2,32]{1,0:T(2,128)}, u32[]{:S(2)}) copy-start(s32[2,32]{1,0:T(2,128)} %param.11) | copy-start | bytes 772
  161.0 25.4 %copy-start.9 = (bf16[272,768]{1,0:T(8,128)(2,1)S(1)}, bf16[272,768]{1,0:T(8,128)(2,1)}, u32[]{:S(2)}) copy-start(bf16[272,768]{1,0:T(8,128)(2,1)} %get-tuple-element.21.x) | copy-start | bytes 1253380
  177.5 8.8 %collective-permute-start = (bf16[272,768]{1,0:T(8,128)(2,1)S(1)}, bf16[272,768]{1,0:T(8,128)(2,1)S(1)}, u32[]{:S(2)}, u32[]{:S(2)}) collective-permute-start(bf16[272,768]{1,0:T(8,128)(2,1)S(1)} %get-tuple-element.23), channel_id=1, source_target_pairs={{0,16},{8,24},{1,17},{9,25},{2,18},{10,26},{3,19},{11,27},{4,20},{... | collective-permute-start | bytes 1253384 | tf_op jit(solution)/shard_map/ppermute | solution.py:1433
  186.5 15.1 %copy-start.3 = (bf16[272,768]{1,0:T(8,128)(2,1)}, bf16[272,768]{1,0:T(8,128)(2,1)S(1)}, u32[]{:S(2)}) copy-start(bf16[272,768]{1,0:T(8,128)(2,1)S(1)} %broadcast_select_fusion.1.x) | copy-start | bytes 1253380
  201.6 1.3 copy-start.2
  202.9 0.9 copy-start.7
  203.9 0.8 copy-start.10
  206.2 0.8 copy-start.13
  216.2 2.1 copy-start.15
  219.5 20.8 %copy-start.17 = (bf16[2176,768]{1,0:T(8,128)(2,1)S(1)}, bf16[2176,768]{1,0:T(8,128)(2,1)}, u32[]{:S(2)}) copy-start(bf16[2176,768]{1,0:T(8,128)(2,1)} %copy-done.16) | copy-start | bytes 10027012
  238.9 1.4 copy-start.20
  240.3 5.3 %copy-start.22 = (bf16[32,768]{1,0:T(8,128)(2,1)S(1)}, bf16[32,768]{1,0:T(8,128)(2,1)}, u32[]{:S(2)}) copy-start(bf16[32,768]{1,0:T(8,128)(2,1)} %get-tuple-element.48.block) | copy-start | bytes 147460
  249.7 26.5 %copy-start.19 = (bf16[512,768]{1,0:T(8,128)(2,1)S(1)}, bf16[512,768]{1,0:T(8,128)(2,1)}, u32[]{:S(2)}) copy-start(bf16[512,768]{1,0:T(8,128)(2,1)} %share_picked.1) | copy-start | bytes 2359300
  249.7 26.5 %copy-start.21 = (bf16[512,2176]{1,0:T(8,128)(2,1)S(1)}, bf16[512,2176]{1,0:T(8,128)(2,1)}, u32[]{:S(2)}) copy-start(bf16[512,2176]{1,0:T(8,128)(2,1)} %copy-done.20) | copy-start | bytes 6684676
  274.0 39.9 %collective-permute-start.1 = (bf16[272,768]{1,0:T(8,128)(2,1)}, bf16[272,768]{1,0:T(8,128)(2,1)S(1)}, u32[]{:S(2)}, u32[]{:S(2)}) collective-permute-start(bf16[272,768]{1,0:T(8,128)(2,1)} %layer_backward.1), channel_id=1, source_target_pairs={{16,0},{24,8},{17,1},{25,9},{18,2},{26,10},{19,3},{27,11},{20,4},{... | collective-permute-start | bytes 1253384 | tf_op jit(solution)/shard_map/ppermute | solution.py:1483
  276.2 37.7 %copy-start.18 = (bf16[272,768]{1,0:T(8,128)(2,1)S(1)}, bf16[272,768]{1,0:T(8,128)(2,1)}, u32[]{:S(2)}) copy-start(bf16[272,768]{1,0:T(8,128)(2,1)} %convolution_convert_fusion.dy) | copy-start | bytes 1253380
  507.7 16.8 %copy-start.1 = (s32[2,264]{1,0:T(2,128)S(1)}, s32[2,264]{1,0:T(2,128)}, u32[]{:S(2)}) copy-start(s32[2,264]{1,0:T(2,128)} %param.10) | copy-start | bytes 6340
  (2 other events, 1.5 us)

commit v2 on v1

--- a/solution.py
+++ b/solution.py
@@ -81,6 +81,7 @@
 MESH = pl.DeviceIdType.MESH
 ANY = pl.BlockSpec(memory_space=pl.ANY)
 VMEM = pl.BlockSpec(memory_space=pltpu.VMEM)
+SMEM = pl.BlockSpec(memory_space=pltpu.SMEM)
 
 HALF = 1088
 CH = 64
@@ -88,9 +89,10 @@
 CC = 48
 NCC = 11
 LANE = 4 * HALF
-LAG = 2
+LAG = 3
 WINDOW = 2
 HOP = 3
+TURN = 6
 
 
 def place():
@@ -103,7 +105,7 @@
     return sec, dp, z, c, par, home
 
 
-def greet_neighbours(sec, dp, z, c, par):
+def greet_neighbours(sec, dp, z, c, par, turns):
     barrier = pltpu.get_barrier_semaphore()
 
     def greet(s, e):
@@ -113,7 +115,11 @@
     greet(sec + 1 - 2 * par, dp)
     pl.when(z > 0)(lambda: greet(sec, dp - 2))
     pl.when(z < 3)(lambda: greet(sec, dp + 2))
-    pl.semaphore_wait(barrier, 2 + (z > 0).astype(jnp.int32) + (z < 3).astype(jnp.int32))
+    count = 2 + (z > 0).astype(jnp.int32) + (z < 3).astype(jnp.int32)
+    for sender, receiver in turns:
+        pl.when(sec == receiver)(lambda sender=sender: greet(sender, dp))
+        count = count + (sec == sender).astype(jnp.int32)
+    pl.semaphore_wait(barrier, count)
 
 
 def hop_targets(sec, dp, c, par):
@@ -131,57 +137,165 @@
 def tree(z, c, home):
     both = jnp.logical_and
     either = jnp.logical_or
+    no = jnp.logical_not
     far = z >= 2
     mid = both(z >= 1, z <= 2)
     never = z < 0
+    away = no(home)
+    as_int = lambda flag: flag.astype(jnp.int32)
     out = []
     for block in (0, 1):
         for half in (0, 1):
-            mine = home if half == 0 else jnp.logical_not(home)
-            other = jnp.logical_not(mine)
+            mine = home if half == 0 else away
+            other = no(mine)
             source = both(z == block, home)
-            at_owner_col = both(z == block, jnp.logical_not(home))
+            if half == 0:
+                early = (lambda j: j < TURN) if block == 0 else (lambda j: j < 0)
+                near_x = lambda j, block=block, early=early: both(z == 1 - block, early(j))
+                hop_x = lambda j, near_x=near_x: both(home, near_x(j))
+                got_x = lambda j, near_x=near_x: both(away, near_x(j))
+                along = lambda j, early=early: either(home, no(early(j)))
+            else:
+                hop_x = lambda j, block=block: both(away, z == 1 - block)
+                got_x = lambda j, block=block: both(home, z == 1 - block)
+                along = lambda j: away
+            at_owner = both(z == block, away)
             if block == 0:
-                sends = dict(up=either(z == 0, both(mid, mine)), down=never)
-                from_up = never
+                up = lambda j, along=along, mine=mine: either(both(z == 0, along(j)), both(mid, mine))
+                down = lambda j: never
+                from_up = lambda j: never
             else:
-                sends = dict(up=both(mid, mine), down=z == 1)
-                from_up = z == 0
-            sends["x"] = either(source, both(far, mine))
-            from_x = either(at_owner_col, both(far, other))
-            from_down = jnp.logical_not(either(source, either(from_x, from_up)))
-            aside = 1 - home.astype(jnp.int32)
-            turn = jnp.logical_and(far, other).astype(jnp.int32) + far.astype(jnp.int32) * half
-            near = 1 - far.astype(jnp.int32)
-            depth = jnp.abs(z - block) + near * aside + turn
-            out.append((source, sends, dict(up=from_up, down=from_down, x=from_x), depth))
+                up = lambda j, mine=mine: both(mid, mine)
+                down = lambda j, along=along: both(z == 1, along(j))
+                from_up = lambda j, got_x=got_x: both(z == 0, no(got_x(j)))
+            send_x = lambda j, source=source, mine=mine, hop_x=hop_x: either(
+                either(source, both(far, mine)), hop_x(j)
+            )
+            from_x = lambda j, at_owner=at_owner, other=other, got_x=got_x: either(
+                either(at_owner, both(far, other)), got_x(j)
+            )
+            from_down = lambda j, source=source, from_x=from_x, from_up=from_up: no(
+                either(source, either(from_x(j), from_up(j)))
+            )
+            depth = jnp.abs(z - block) + as_int(far) * (half + as_int(other))
+            if half == 0:
+                depth = depth + (1 - as_int(far)) * as_int(away)
+            else:
+                depth = depth + (1 - as_int(far)) * jnp.where(
+                    away, 1, 2 * as_int(z == 1 - block)
+                )
+            out.append(
+                (source, dict(up=up, down=down, x=send_x), dict(up=from_up, down=from_down, x=from_x), depth)
+            )
     lane0 = c == 0
     source = both(both(z == 2, home), lane0)
     sends = dict(
-        up=both(z == 2, lane0),
-        down=both(mid, lane0),
-        x=source,
-        core=lane0,
+        up=lambda j: both(z == 2, lane0),
+        down=lambda j: both(mid, lane0),
+        x=lambda j: source,
     )
     parents = dict(
-        up=both(z <= 1, lane0),
-        down=both(z == 3, lane0),
-        x=both(both(z == 2, jnp.logical_not(home)), lane0),
+        up=lambda j: both(z <= 1, lane0),
+        down=lambda j: both(z == 3, lane0),
+        x=lambda j: both(both(z == 2, away), lane0),
     )
-    depth = jnp.abs(z - 2) + 1 - home.astype(jnp.int32)
-    out.append((source, sends, parents, depth))
+    out.append((source, sends, parents, jnp.abs(z - 2) + as_int(away)))
     return out
 
 
+def segment_of(starts, r, slot):
+    bounds = [starts[r, j] for j in range(SEGS + 1)]
+    count = lambda at: functools.reduce(
+        jnp.add, [(at >= bounds[j]).astype(jnp.int32) for j in range(1, SEGS + 1)]
+    )
+    segment = count(slot)
+    begin = jnp.where(
+        segment == 0, bounds[0], jnp.where(segment == 1, bounds[1], jnp.where(segment == 2, bounds[2], bounds[3]))
+    )
+    counted = jnp.logical_and(count(slot + 1) == segment, slot + 1 < bounds[SEGS])
+    return segment, slot - begin, counted, slot < bounds[SEGS]
+
+
 def open_kernel(
-    table, index, out, x0, own_sem, recv_sem, recv_c, core_sem, send_sem,
-    sent, mine, rx_core, rx_up, rx_down, swap_send, swap_recv, x_send, x_recv, line_send,
-    up_recv, down_recv,
+    table, codes, labels, picks, starts, classes, nulls, frequency, out, x0, info, gain, cosine,
+    sine, own_sem, recv_sem, recv_c, core_sem, send_sem, sent, mine, rx_core, rx_up, rx_down,
+    swap_send, swap_recv, x_send, x_recv, line_send, up_recv, down_recv, last_send, last_recv,
+    note, note_send, note_recv, gain_send, gain_recv,
 ):
     sec, dp, z, c, par, home = place()
     targets = hop_targets(sec, dp, c, par)
-    classes = tree(z, c, home)
-    greet_neighbours(sec, dp, z, c, par)
+    classes_of = tree(z, c, home)
+    gain_dp = VOCAB // (2 * HALF)
+    holds_gain = jnp.logical_and(sec == 3, dp == gain_dp)
+
+    barrier = pltpu.get_barrier_semaphore()
+
+    def greet(s, e):
+        pl.semaphore_signal(barrier, 1, device_id=(s, e), device_id_type=MESH)
+
+    for k in range(1, 8):
+        greet(sec, lax.rem(dp + k, 8))
+    greet(sec + 1 - 2 * par, dp)
+    pl.when(sec == 2)(lambda: greet(0, dp))
+    pl.when(sec == 1)(lambda: greet(2, dp))
+    pl.when(jnp.logical_and(sec == 2, dp != gain_dp))(lambda: greet(3, gain_dp))
+
+    slot_row = lax.broadcasted_iota(jnp.int32, (1, SLOTS), 1)
+    note[...] = jnp.full(note.shape, -1, jnp.int32)
+    for r in range(2):
+        segment, position, _, live = segment_of(starts, r, slot_row)
+        names = [classes[r, j] + (CLASSES - 1 - classes[r, j]) * nulls[r, j] for j in range(SEGS)]
+        name = jnp.where(segment == 0, names[0], jnp.where(segment == 1, names[1], names[2]))
+        opens = jnp.logical_and(position == 0, live)
+        note[r : r + 1, :SLOTS] = jnp.where(opens, VOCAB + name, codes[r : r + 1, :])
+        chosen = picks[r : r + 1, :]
+        ids = lax.broadcasted_iota(jnp.int32, (SLOTS, PICKS), 0)
+        label_col = column(labels[r : r + 1, :], SLOTS)
+        note[2 + r : 3 + r, :PICKS] = jnp.sum(
+            jnp.where(ids == chosen, label_col, 0), axis=0, keepdims=True
+        )
+        note[4 + r : 5 + r, :PICKS] = segment_of(starts, r, chosen)[2].astype(jnp.int32)
+    info[dp] = note[...]
+    count = 8 + jnp.logical_or(sec == 0, sec == 2).astype(jnp.int32)
+    pl.semaphore_wait(barrier, count + 7 * holds_gain.astype(jnp.int32))
+    for k in range(1, 8):
+        pltpu.make_async_remote_copy(
+            src_ref=note,
+            dst_ref=info.at[dp],
+            send_sem=note_send,
+            recv_sem=note_recv,
+            device_id=(sec, lax.rem(dp + k, 8)),
+            device_id_type=MESH,
+        ).start()
+    noted = pltpu.make_async_remote_copy(
+        src_ref=info.at[pl.ds(0, 7)],
+        dst_ref=info.at[pl.ds(0, 7)],
+        send_sem=note_send,
+        recv_sem=note_recv,
+        device_id=targets["core"],
+        device_id_type=MESH,
+    )
+
+    gain_rows = table.at[pl.ds(VOCAB % (2 * HALF), 16)]
+
+    def gain_to(s, e):
+        return pltpu.make_async_remote_copy(
+            src_ref=gain_rows,
+            dst_ref=gain,
+            send_sem=gain_send,
+            recv_sem=gain_recv,
+            device_id=(s, e),
+            device_id_type=MESH,
+        )
+
+    def send_gain():
+        for e in range(8):
+            gain_to(2, e).start()
+            if e != gain_dp:
+                gain_to(3, e).start()
+        gain[...] = gain_rows[...]
+
+    pl.when(holds_gain)(send_gain)
 
     def keep(rows):
         return pltpu.make_async_copy(
@@ -199,7 +313,7 @@
         keep(NCC * CC).wait()
 
     pl.when(jnp.logical_and(home, z < 2))(keep_all)
-    pl.when(classes[4][0])(keep_few)
+    pl.when(classes_of[4][0])(keep_few)
 
     def base(k, lane):
         if k == 4:
@@ -218,26 +332,27 @@
         )
 
     def piece(k, j, rows):
-        source, sends, _, _ = classes[k]
+        source, sends, _, _ = classes_of[k]
         recv = recv_c.at[j] if k == 4 else recv_sem.at[k, j]
         slot = lax.rem(j, WINDOW)
 
         def send(hop):
             to = core_sem.at[k] if hop == "core" else recv
             one = copy(k, hop, j, rows, to, slot)
-            pl.when(j >= WINDOW)(one.wait_send)
+            before = True if hop == "core" else sends[hop](j - WINDOW)
+            pl.when(jnp.logical_and(j >= WINDOW, before))(one.wait_send)
             one.start()
 
         pl.when(jnp.logical_not(source))(copy(k, "x", j, rows, recv, slot).wait_recv)
         for hop in HOPS[:3]:
-            pl.when(sends[hop])(lambda hop=hop: send(hop))
+            pl.when(sends[hop](j))(lambda hop=hop: send(hop))
         send("core")
 
     def counts(k):
         return (NCC, CC) if k == 4 else (NCH, CH)
 
     first = sec == 0
-    second = sec == 1
+    second = sec == 2
 
     def slot(k):
         return pl.ds(pl.multiple_of(k * SP, 16), SP)
@@ -262,7 +377,7 @@
             dst_ref=mine.at[slot(zz)],
             send_sem=x_send,
             recv_sem=x_recv.at[zz],
-            device_id=targets["x"],
+            device_id=(2, dp),
             device_id_type=MESH,
         )
 
@@ -291,29 +406,21 @@
         mine[there, :] = (mine[there, :].astype(F32) + ref[there, :].astype(F32)).astype(BF16)
 
     def look(row):
-        local = index[pl.ds(pl.multiple_of(row * SP, 16), SP), :]
+        local = column(info[row // 2, pl.ds(lax.rem(row, 2), 1), :][:, :SP], SP) - dp * 2 * HALF
         ids = lax.broadcasted_iota(jnp.int32, (SP, 2 * HALF), 1)
         onehot = jnp.where(ids == local, 1.0, 0.0).astype(BF16)
         return (nn(onehot, table[...]) * math.sqrt(D)).astype(BF16)
 
-    def lookup(i):
-        b = i // 2
+    def lookup(b):
         zz = order(b // 2)
         p = 1 - lax.rem(b, 2)
         k = 4 * p + zz
-
-        def for_other():
-            sent[slot(k), :] = look(2 * (2 * zz + 1 - c) + p)
-            swap(k).start()
-
-        def for_self():
-            mine[slot(k), :] = look(2 * (2 * zz + c) + p)
-            swap(k).wait_recv()
-            add(k, rx_core)
-            pl.when(p == 1)(lambda: cross(zz).start())
-
-        pl.when(lax.rem(i, 2) == 0)(for_other)
-        pl.when(lax.rem(i, 2) == 1)(for_self)
+        sent[slot(k), :] = look(2 * (2 * zz + 1 - c) + p)
+        swap(k).start()
+        mine[slot(k), :] = look(2 * (2 * zz + c) + p)
+        swap(k).wait_recv()
+        add(k, rx_core)
+        pl.when(p == 1)(lambda: cross(zz).start())
 
     def chain(zz):
         def from_below():
@@ -336,21 +443,41 @@
             hops = jnp.maximum(
                 z * (zz >= z).astype(jnp.int32), (3 - z) * (zz <= z).astype(jnp.int32)
             )
-            pl.when(i == 4 * o + 3 + 2 * sec + HOP * hops)(lambda zz=zz: chain(zz))
+            pl.when(i == 2 * o + 2 + sec + HOP * hops)(lambda zz=zz: chain(zz))
+
+    segment, position, _, _ = segment_of(starts, par, lax.broadcasted_iota(jnp.int32, (SP, 128), 0))
+    angles = position.astype(F32) * frequency[...]
+    lanes = lax.broadcasted_iota(jnp.int32, (SP, 128), 1)
+    cosine[...] = jnp.cos(angles)
+    sine[...] = jnp.where(lax.rem(lanes, 64) < 32, -1.0, 1.0) * jnp.sin(angles)
+    noted.wait_recv()
 
     def step(i, carry):
         for k in range(5):
             count, rows = counts(k)
-            j = i - LAG * classes[k][3]
+            j = i - LAG * classes_of[k][3]
             now = jnp.logical_and(j >= 0, j < count)
             if k == 4:
                 now = jnp.logical_and(now, c == 0)
             pl.when(now)(lambda k=k, j=j, rows=rows: piece(k, j, rows))
-        pl.when(jnp.logical_and(first, i < 16))(lambda: lookup(i))
-        pl.when(sec < 2)(lambda: chains(i))
+        pl.when(jnp.logical_and(first, i < 8))(lambda: lookup(i))
+        pl.when(jnp.logical_or(first, second))(lambda: chains(i))
+        pl.when(jnp.logical_and(second, i == last_step))(lambda: last().start())
         return carry
 
-    lax.fori_loop(0, max(NCH + 5 * LAG, 12 + 3 + 2 + 3 * HOP + 1), step, 0)
+    last_step = 6 + 2 + 2 + 3 * HOP + 1
+
+    def last():
+        return pltpu.make_async_remote_copy(
+            src_ref=mine.at[slot(z)],
+            dst_ref=x0,
+            send_sem=last_send,
+            recv_sem=last_recv,
+            device_id=(1, dp),
+            device_id_type=MESH,
+        )
+
+    lax.fori_loop(0, max(NCH + 5 * LAG, last_step + 1), step, 0)
 
     def blocks(count, sem):
         return pltpu.make_async_remote_copy(
@@ -362,29 +489,46 @@
             device_id_type=MESH,
         )
 
-    def finish():
+    def end_first():
+        blocks(8, swap_send).wait_send()
+        blocks(4, x_send).wait_send()
+        blocks(3, line_send).wait_send()
         x0[...] = mine[slot(z), :]
+
+    def end_second():
         blocks(3, line_send).wait_send()
+        last().wait_send()
 
     def none():
         x0[...] = jnp.zeros_like(x0)
 
-    def sent_first():
-        blocks(8, swap_send).wait_send()
-        blocks(4, x_send).wait_send()
-
-    pl.when(first)(sent_first)
-    pl.when(sec < 2)(finish)
+    pl.when(first)(end_first)
+    pl.when(second)(end_second)
+    pl.when(sec == 1)(last().wait_recv)
     pl.when(sec >= 2)(none)
+
+    noted.wait_send()
+
+    def gain_sent():
+        for e in range(15):
+            gain_to(2, 0).wait_send()
+
+    pl.when(holds_gain)(gain_sent)
+    pl.when(jnp.logical_and(sec >= 2, jnp.logical_not(holds_gain)))(gain_to(2, dp).wait_recv)
 
     def drain(k):
         count, rows = counts(k)
-        _, sends, _, _ = classes[k]
+        _, sends, _, _ = classes_of[k]
         for j in range(count - WINDOW, count):
             for hop in HOPS[:3]:
                 one = copy(k, hop, j, rows, core_sem.at[k], j % WINDOW)
-                pl.when(sends[hop])(one.wait_send)
+                pl.when(sends[hop](j))(one.wait_send)
             copy(k, "core", j, rows, core_sem.at[k], j % WINDOW).wait_send()
+        if k == 0:
+            for j in range(TURN - WINDOW, TURN):
+                one = copy(k, "x", j, rows, core_sem.at[k], j % WINDOW)
+                last_one = jnp.logical_not(sends["x"](j + WINDOW))
+                pl.when(jnp.logical_and(sends["x"](j), last_one))(one.wait_send)
 
     def came(k):
         count, rows = counts(k)
@@ -405,16 +549,20 @@
     pl.when(c == 1)(lambda: came(4))
 
 
-def gather_and_embed(table, index):
+def gather_and_embed(table, codes, labels, picks, starts, classes, nulls, frequency):
     rows = lambda n: pltpu.VMEM((n * SP, D), BF16)
     return pl.pallas_call(
         open_kernel,
         out_shape=(
             jax.ShapeDtypeStruct((WROWS, D), BF16),
             jax.ShapeDtypeStruct((SP, D), BF16),
+            jax.ShapeDtypeStruct((8, 8, 384), jnp.int32),
+            jax.ShapeDtypeStruct((16, D), BF16),
+            jax.ShapeDtypeStruct((SP, 128), F32),
+            jax.ShapeDtypeStruct((SP, 128), F32),
         ),
-        in_specs=[VMEM, VMEM],
-        out_specs=(VMEM, VMEM),
+        in_specs=[VMEM] * 4 + [SMEM] * 3 + [VMEM],
+        out_specs=(VMEM,) * 6,
         scratch_shapes=[
             pltpu.SemaphoreType.DMA,
             pltpu.SemaphoreType.DMA((4, NCH)),
@@ -433,18 +581,22 @@
             pltpu.SemaphoreType.DMA,
             pltpu.SemaphoreType.DMA((4,)),
             pltpu.SemaphoreType.DMA((4,)),
-        ],
+            pltpu.SemaphoreType.DMA,
+            pltpu.SemaphoreType.DMA,
+            pltpu.VMEM((8, 384), jnp.int32),
+        ]
+        + [pltpu.SemaphoreType.DMA] * 4,
         compiler_params=pltpu.CompilerParams(
             collective_id=0, has_side_effects=True, vmem_limit_bytes=56 * 2**20
         ),
         name="gather_and_embed",
-    )(table, index)
+    )(table, codes, labels, picks, starts, classes, nulls, frequency)
 
 
 def close_kernel(
     grads, start, block, index, out, squares, loc, rx_core, rx_up, rx_down, rx_x, total, summed,
     all_dx, load_sem, core_sem, core_c, recv_sem, recv_c, core_send, send_sem, out_sem,
-    dx_own, dx_send, line_recv, cross_recv, dx_core_send, dx_core_recv,
+    dx_own, dx_send, line_recv, cross_recv, turn_recv, dx_core_send, dx_core_recv,
 ):
     sec, dp, z, c, par, home = place()
     targets = hop_targets(sec, dp, c, par)
@@ -470,7 +622,7 @@
 
     for k in range(5):
         load(k).start()
-    greet_neighbours(sec, dp, z, c, par)
+    greet_neighbours(sec, dp, z, c, par, ((1, 2), (2, 0)))
 
     def to_core(k, j, rows):
         sem = core_c.at[j] if k == 4 else core_sem.at[k, j]
@@ -538,13 +690,13 @@
                 landed(k, hop, j, rows).wait_recv()
                 acc[...] += rx[hop][part, :].astype(F32)
 
-            pl.when(classes[k][1][hop])(add)
+            pl.when(classes[k][1][hop](j))(add)
         return part, acc
 
     def pass_on(k, j, rows, part, acc):
         loc[part, :] = acc[...].astype(BF16)
         for hop in HOPS[:3]:
-            pl.when(classes[k][2][hop])(lambda hop=hop: onward(k, hop, j, rows).start())
+            pl.when(classes[k][2][hop](j))(lambda hop=hop: onward(k, hop, j, rows).start())
 
     def relay(k, j, rows):
         part, acc = gathered(k, j, rows)
@@ -559,8 +711,9 @@
         count_squares(value)
 
     first = sec == 0
-    second = sec == 1
-    in_line = sec < 2
+    second = sec == 2
+    in_line = jnp.logical_or(first, second)
+    p_line = second.astype(jnp.int32)
     both = jnp.logical_and
 
     def dx_part(p, zz):
@@ -577,10 +730,10 @@
         )
 
     def line(zz, hop):
-        return move(par, zz, dx_send, line_recv.at[zz], targets[hop])
+        return move(p_line, zz, dx_send, line_recv.at[zz], targets[hop])
 
     def cross(zz):
-        return move(1, zz, dx_send, cross_recv.at[zz], targets["x"])
+        return move(1, zz, dx_send, cross_recv.at[zz], (0, dp))
 
     def dx_to_core(p, zz):
         return move(p, zz, dx_core_send, dx_core_recv, targets["core"])
@@ -603,15 +756,32 @@
             device_id_type=MESH,
         )
 
-    def own_block():
-        own = pltpu.make_async_copy(block, dx_part(par, z), dx_own)
-        own.start()
-        own.wait()
+    turned = pltpu.make_async_remote_copy(
+        src_ref=block,
+        dst_ref=dx_part(1, z),
+        send_sem=dx_send,
+        recv_sem=turn_recv,
+        device_id=(2, dp),
+        device_id_type=MESH,
+    )
+    pl.when(sec == 1)(turned.start)
+
+    def pass_own():
         pl.when(z < 3)(lambda: line(z, "up").start())
         pl.when(z > 0)(lambda: line(z, "down").start())
         aside(z)
 
-    pl.when(in_line)(own_block)
+    def own_first():
+        own = pltpu.make_async_copy(block, dx_part(0, z), dx_own)
+        own.start()
+        own.wait()
+        pass_own()
+
+    def own_second():
+        turned.wait_recv()
+        pass_own()
+
+    pl.when(first)(own_first)
 
     def from_below(k):
         line(z - k, "up").wait_recv()
@@ -633,16 +803,18 @@
         count_squares(value)
 
     def collect(i):
+        pl.when(both(second, i == HOP))(own_second)
         for k in range(1, 4):
-            pl.when(both(i == HOP * k, z >= k))(lambda k=k: from_below(k))
-            pl.when(both(i == HOP * k, z + k <= 3))(lambda k=k: from_above(k))
+            now = i == HOP * (k + p_line)
+            pl.when(both(now, z >= k))(lambda k=k: from_below(k))
+            pl.when(both(now, z + k <= 3))(lambda k=k: from_above(k))
 
     def embed(i):
-        pl.when(i == HOP)(lambda: crossed(z))
+        pl.when(i == 2 * HOP)(lambda: crossed(z))
         for k in range(1, 4):
-            pl.when(both(i == HOP * (k + 1), z >= k))(lambda k=k: crossed(z - k))
-            pl.when(both(i == HOP * (k + 1), z + k <= 3))(lambda k=k: crossed(z + k))
-        begin = 4 * HOP + 2
+            pl.when(both(i == HOP * (k + 2), z >= k))(lambda k=k: crossed(z - k))
+            pl.when(both(i == HOP * (k + 2), z + k <= 3))(lambda k=k: crossed(z + k))
+        begin = 5 * HOP + 1
         pl.when(i == begin)(lambda: blocks(8, dx_core_send, dx_core_recv).wait_recv())
         for half in range(2):
             t = 2 * (i - begin) + half
@@ -675,7 +847,7 @@
         pl.when(first)(lambda: embed(i))
         return carry
 
-    lax.fori_loop(0, max(NCH + 5 * LAG, 4 * HOP + 2 + 9), step, 0)
+    lax.fori_loop(0, max(NCH + 5 * LAG, 5 * HOP + 1 + 9), step, 0)
     pl.when(first)(lambda: blocks(8, dx_core_send, dx_core_recv).wait_send())
 
     def dx_sent(count):
@@ -683,7 +855,7 @@
 
     middle = both(z >= 1, z <= 2)
     ends = jnp.logical_not(middle)
-    pl.when(both(first, ends))(lambda: dx_sent(1))
+    pl.when(jnp.logical_or(sec == 1, both(first, ends)))(lambda: dx_sent(1))
     pl.when(both(first, middle))(lambda: dx_sent(5))
     pl.when(both(second, ends))(lambda: dx_sent(5))
     pl.when(both(second, middle))(lambda: dx_sent(9))
@@ -750,6 +922,7 @@
             pltpu.SemaphoreType.DMA((4,)),
             pltpu.SemaphoreType.DMA,
             pltpu.SemaphoreType.DMA,
+            pltpu.SemaphoreType.DMA,
         ],
         compiler_params=pltpu.CompilerParams(
             collective_id=1, has_side_effects=True, vmem_limit_bytes=60 * 2**20
@@ -819,302 +992,6 @@
     )(block)
 
 
-def share_row_kernel(n_dp, block, out, send_sem, recv_sem, own_sem):
-    sec = lax.axis_index("section")
-    me = lax.axis_index("dp")
-    barrier = pltpu.get_barrier_semaphore()
-    own = pltpu.make_async_copy(block, out.at[me], own_sem)
-    own.start()
-    for k in range(1, n_dp):
-        pl.semaphore_signal(
-            barrier, 1, device_id=(sec, lax.rem(me + k, n_dp)), device_id_type=MESH
-        )
-    pl.semaphore_wait(barrier, n_dp - 1)
-    for k in range(1, n_dp):
-        pltpu.make_async_remote_copy(
-            src_ref=block,
-            dst_ref=out.at[me],
-            send_sem=send_sem,
-            recv_sem=recv_sem,
-            device_id=(sec, lax.rem(me + k, n_dp)),
-            device_id_type=MESH,
-        ).start()
-    every = pltpu.make_async_remote_copy(
-        src_ref=out.at[pl.ds(0, n_dp - 1)],
-        dst_ref=out.at[pl.ds(0, n_dp - 1)],
-        send_sem=send_sem,
-        recv_sem=recv_sem,
-        device_id=(sec, lax.rem(me + 1, n_dp)),
-        device_id_type=MESH,
-    )
-    own.wait()
-    every.wait_send()
-    every.wait_recv()
-
-
-def share_row(block, n_dp, cid, name):
-    return pl.pallas_call(
-        functools.partial(share_row_kernel, n_dp),
-        out_shape=jax.ShapeDtypeStruct((n_dp,) + block.shape, block.dtype),
-        in_specs=[VMEM],
-        out_specs=VMEM,
-        scratch_shapes=[
-            pltpu.SemaphoreType.DMA,
-            pltpu.SemaphoreType.DMA,
-            pltpu.SemaphoreType.DMA,
-        ],
-        compiler_params=pltpu.CompilerParams(collective_id=cid, has_side_effects=True),
-        name=name,
-    )(block)
-
-
-def picked_kernel(block, out, own_sem, send_sem, recv_sem, core_send, core_recv):
-    sec, dp, z, c, par, home = place()
-    last = sec == 3
-    upper = sec >= 2
-    barrier = pltpu.get_barrier_semaphore()
-
-    def greet(s, e):
-        pl.semaphore_signal(barrier, 1, device_id=(s, e), device_id_type=MESH)
-
-    def rows(p, zz, lane):
-        return pl.ds(pl.multiple_of((2 * (2 * zz + lane) + p) * PICKS, PICKS), PICKS)
-
-    def greet_senders():
-        for k in range(4):
-            greet(2, 2 * k + c)
-        for k in range(1, 4):
-            greet(3, 2 * lax.rem(z + k, 4) + c)
-        greet(3, dp + 1 - 2 * c)
-
-    pl.when(last)(greet_senders)
-
-    def to(k):
-        zz = lax.rem(z + k, 4)
-        return pltpu.make_async_remote_copy(
-            src_ref=block,
-            dst_ref=out.at[rows(par, z, c)],
-            send_sem=send_sem,
-            recv_sem=recv_sem.at[par, z],
-            device_id=(3, 2 * zz + c),
-            device_id_type=MESH,
-        )
-
-    def forward(p, k):
-        zz = lax.rem(z + k, 4)
-        return pltpu.make_async_remote_copy(
-            src_ref=out.at[rows(p, zz, c)],
-            dst_ref=out.at[rows(p, zz, c)],
-            send_sem=core_send,
-            recv_sem=core_recv,
-            device_id=(3, dp + 1 - 2 * c),
-            device_id_type=MESH,
-        )
-
-    def came(p, k):
-        zz = lax.rem(z + k, 4)
-        return pltpu.make_async_remote_copy(
-            src_ref=block,
-            dst_ref=out.at[rows(p, zz, c)],
-            send_sem=send_sem,
-            recv_sem=recv_sem.at[p, zz],
-            device_id=(3, dp),
-            device_id_type=MESH,
-        )
-
-    def every(count):
-        return pltpu.make_async_remote_copy(
-            src_ref=out.at[pl.ds(0, count * PICKS)],
-            dst_ref=out.at[pl.ds(0, count * PICKS)],
-            send_sem=core_send,
-            recv_sem=core_recv,
-            device_id=(3, dp),
-            device_id_type=MESH,
-        )
-
-    def all_sent(count):
-        return pltpu.make_async_remote_copy(
-            src_ref=out.at[pl.ds(0, count * PICKS)],
-            dst_ref=out.at[pl.ds(0, count * PICKS)],
-            send_sem=send_sem,
-            recv_sem=core_recv,
-            device_id=(3, dp),
-            device_id_type=MESH,
-        )
-
-    def second():
-        pl.semaphore_wait(barrier, 4)
-        for k in range(4):
-            to(k).start()
-        all_sent(4).wait_send()
-
-    def third():
-        own = pltpu.make_async_copy(block, out.at[rows(1, z, c)], own_sem)
-        own.start()
-        pl.semaphore_wait(barrier, 4)
-        for k in range(1, 4):
-            to(k).start()
-        own.wait()
-        forward(1, 0).start()
-        for k in range(4):
-            came(0, k).wait_recv()
-            forward(0, k).start()
-            if k:
-                came(1, k).wait_recv()
-                forward(1, k).start()
-        all_sent(3).wait_send()
-        every(8).wait_send()
-        every(8).wait_recv()
-
-    def none():
-        out[...] = jnp.zeros_like(out)
-
-    pl.when(sec == 2)(second)
-    pl.when(last)(third)
-    pl.when(jnp.logical_not(last))(none)
-
-
-def share_picked(block):
-    return pl.pallas_call(
-        picked_kernel,
-        out_shape=jax.ShapeDtypeStruct((16 * PICKS, D), BF16),
-        in_specs=[VMEM],
-        out_specs=VMEM,
-        scratch_shapes=[
-            pltpu.SemaphoreType.DMA,
-            pltpu.SemaphoreType.DMA,
-            pltpu.SemaphoreType.DMA((2, 4)),
-            pltpu.SemaphoreType.DMA,
-            pltpu.SemaphoreType.DMA,
-        ],
-        compiler_params=pltpu.CompilerParams(collective_id=4, has_side_effects=True),
-        name="share_picked",
-    )(block)
-
-
-def unpick_kernel(part, out, rx_core, low, rx, core_send, core_recv, send_sem, recv_sem):
-    sec, dp, z, c, par, home = place()
-    barrier = pltpu.get_barrier_semaphore()
-
-    def greet(s, e):
-        pl.semaphore_signal(barrier, 1, device_id=(s, e), device_id_type=MESH)
-
-    def greet_senders():
-        for k in range(4):
-            pl.when(jnp.logical_or(sec == 2, 2 * k + c != dp))(lambda k=k: greet(3, 2 * k + c))
-
-    pl.when(sec >= 2)(greet_senders)
-    pl.when(sec == 3)(lambda: greet(3, dp + 1 - 2 * c))
-
-    def row(p, zz, lane):
-        return (2 * (2 * zz + lane) + p) * PICKS
-
-    def swap(p, zz):
-        place_there = (2 * zz + p) * PICKS
-        return pltpu.make_async_remote_copy(
-            src_ref=part.at[pl.ds(pl.multiple_of(row(p, zz, 1 - c), PICKS), PICKS)],
-            dst_ref=rx_core.at[pl.ds(place_there, PICKS)],
-            send_sem=core_send,
-            recv_sem=core_recv,
-            device_id=(3, dp + 1 - 2 * c),
-            device_id_type=MESH,
-        )
-
-    def to(p, k):
-        zz = lax.rem(z + k, 4)
-        return pltpu.make_async_remote_copy(
-            src_ref=low.at[pl.ds(pl.multiple_of((2 * zz + p) * PICKS, PICKS), PICKS)],
-            dst_ref=rx.at[z],
-            send_sem=send_sem,
-            recv_sem=recv_sem,
-            device_id=(2 + p, 2 * zz + c),
-            device_id_type=MESH,
-        )
-
-    def third():
-        pl.semaphore_wait(barrier, 8)
-        for zz in range(4):
-            for p in range(2):
-                swap(p, zz).start()
-        whole = pltpu.make_async_remote_copy(
-            src_ref=rx_core,
-            dst_ref=rx_core,
-            send_sem=core_send,
-            recv_sem=core_recv,
-            device_id=(3, dp),
-            device_id_type=MESH,
-        )
-        whole.wait_recv()
-        for zz in range(4):
-            for p in range(2):
-                there = pl.ds((2 * zz + p) * PICKS, PICKS)
-                mine = part[pl.ds(pl.multiple_of(row(p, zz, c), PICKS), PICKS), :]
-                low[there, :] = (mine + rx_core[there, :]).astype(BF16)
-        for k in range(4):
-            to(0, k).start()
-            if k:
-                to(1, k).start()
-        whole.wait_send()
-        pltpu.make_async_remote_copy(
-            src_ref=low.at[pl.ds(0, 7 * PICKS)],
-            dst_ref=low.at[pl.ds(0, 7 * PICKS)],
-            send_sem=send_sem,
-            recv_sem=recv_sem,
-            device_id=(3, dp),
-            device_id_type=MESH,
-        ).wait_send()
-        pltpu.make_async_remote_copy(
-            src_ref=rx.at[pl.ds(0, 3)],
-            dst_ref=rx.at[pl.ds(0, 3)],
-            send_sem=send_sem,
-            recv_sem=recv_sem,
-            device_id=(3, dp),
-            device_id_type=MESH,
-        ).wait_recv()
-        rx[z] = low[pl.ds(pl.multiple_of((2 * z + 1) * PICKS, PICKS), PICKS), :]
-
-    def second():
-        pltpu.make_async_remote_copy(
-            src_ref=rx,
-            dst_ref=rx,
-            send_sem=send_sem,
-            recv_sem=recv_sem,
-            device_id=(3, dp),
-            device_id_type=MESH,
-        ).wait_recv()
-
-    def none():
-        rx[...] = jnp.zeros_like(rx)
-
-    pl.when(sec == 3)(third)
-    pl.when(sec == 2)(second)
-    pl.when(sec < 2)(none)
-    summed = rx[0].astype(F32)
-    for k in range(1, 4):
-        summed = summed + rx[k].astype(F32)
-    out[...] = summed
-
-
-def unpick(part):
-    return pl.pallas_call(
-        unpick_kernel,
-        out_shape=jax.ShapeDtypeStruct((PICKS, D), F32),
-        in_specs=[VMEM],
-        out_specs=VMEM,
-        scratch_shapes=[
-            pltpu.VMEM((8 * PICKS, D), F32),
-            pltpu.VMEM((8 * PICKS, D), BF16),
-            pltpu.VMEM((4, PICKS, D), BF16),
-            pltpu.SemaphoreType.DMA,
-            pltpu.SemaphoreType.DMA,
-            pltpu.SemaphoreType.DMA,
-            pltpu.SemaphoreType.DMA,
-        ],
-        compiler_params=pltpu.CompilerParams(collective_id=5, has_side_effects=True),
-        name="unpick",
-    )(part)
-
-
 NEG = -1e30
 FT = 256
 
@@ -1125,10 +1002,12 @@
     return block * cosine + jnp.where(lax.rem(lanes, 64) < 32, ahead, behind) * sine
 
 
-def see(seg_rows, seg_cols):
+def see(starts):
+    par = lax.rem(lax.axis_index("section"), 2)
     rows = lax.broadcasted_iota(jnp.int32, (SP, SP), 0)
     cols = lax.broadcasted_iota(jnp.int32, (SP, SP), 1)
-    allowed = jnp.logical_and(seg_rows[...] == seg_cols[...], cols <= rows)
+    same = segment_of(starts, par, rows)[0] == segment_of(starts, par, cols)[0]
+    allowed = jnp.logical_and(same, cols <= rows)
     return jnp.where(allowed, 0.0, NEG)
 
 
@@ -1149,12 +1028,12 @@
 
 
 def forward_kernel(
-    x, w_any, cosine, sine, seg_rows, seg_cols, y, q, k, v, o, h, gate, up, w, m, unseen, sems
+    x, w_any, cosine, sine, starts, y, q, k, v, o, h, gate, up, w, m, unseen, sems
 ):
     copies = weight_copies(w_any, w, sems)
     for i in (5, 0, 1, 2, 3, 4):
         copies[i].start()
-    unseen[...] = see(seg_rows, seg_cols)
+    unseen[...] = see(starts)
     lanes = lax.broadcasted_iota(jnp.int32, (SP, 128), 1)
     first = lanes < 64
     copies[5].wait()
@@ -1217,13 +1096,13 @@
     lax.fori_loop(0, 3, narrow, 0)
 
 
-def forward_call(x, weights, cosine, sine, seg_rows, seg_cols):
+def forward_call(x, weights, cosine, sine, starts):
     low = jax.ShapeDtypeStruct((SP, D), BF16)
     wide = jax.ShapeDtypeStruct((SP, FF), F32)
     return pl.pallas_call(
         forward_kernel,
         out_shape=(low, low, low, low, low, jax.ShapeDtypeStruct((SP, D), F32), wide, wide),
-        in_specs=[VMEM, ANY, VMEM, VMEM, VMEM, VMEM],
+        in_specs=[VMEM, ANY, VMEM, VMEM, SMEM],
         out_specs=(VMEM,) * 8,
         scratch_shapes=[
             pltpu.VMEM((WROWS, D), BF16),
@@ -1233,7 +1112,7 @@
         ],
         compiler_params=pltpu.CompilerParams(vmem_limit_bytes=48 * 2**20),
         name="layer_forward",
-    )(x, weights, cosine, sine, seg_rows, seg_cols)
+    )(x, weights, cosine, sine, starts)
 
 
 def rms_back(value_in, gain, grad):
@@ -1245,7 +1124,7 @@
 
 
 def backward_kernel(
-    with_weights, dy, x, w_any, cosine, sine, seg_rows, seg_cols, q, k, v, o, h, gate, up, *refs
+    with_weights, dy, x, w_any, cosine, sine, starts, q, k, v, o, h, gate, up, *refs
 ):
     if with_weights:
         dx, grads, w, dgate, dup, m, da, do, dq, dk, dv, unseen, sems = refs
@@ -1254,7 +1133,7 @@
     copies = weight_copies(w_any, w, sems)
     for i in (4, 5, 2, 3, 1, 0):
         copies[i].start()
-    unseen[...] = see(seg_rows, seg_cols)
+    unseen[...] = see(starts)
     lanes = lax.broadcasted_iota(jnp.int32, (SP, 128), 1)
     first = lanes < 64
     copies[4].wait()
@@ -1347,7 +1226,7 @@
     ).astype(BF16)
 
 
-def backward_call(with_weights, dy, x, weights, cosine, sine, seg_rows, seg_cols, kept):
+def backward_call(with_weights, dy, x, weights, cosine, sine, starts, kept):
     low = jax.ShapeDtypeStruct((SP, D), BF16)
     out_shape = (low, jax.ShapeDtypeStruct((WROWS, D), BF16)) if with_weights else low
     wide = pltpu.VMEM((SP, FF), BF16)
@@ -1355,7 +1234,7 @@
     return pl.pallas_call(
         functools.partial(backward_kernel, with_weights),
         out_shape=out_shape,
-        in_specs=[VMEM, VMEM, ANY] + [VMEM] * 11,
+        in_specs=[VMEM, VMEM, ANY, VMEM, VMEM, SMEM] + [VMEM] * 7,
         out_specs=(VMEM, VMEM) if with_weights else VMEM,
         scratch_shapes=[
             pltpu.VMEM((WROWS, D), BF16),
@@ -1372,78 +1251,417 @@
         ],
         compiler_params=pltpu.CompilerParams(vmem_limit_bytes=60 * 2**20),
         name="layer_backward_weights" if with_weights else "layer_backward",
-    )(dy, x, weights, cosine, sine, seg_rows, seg_cols, *kept)
-
-
-def shards(codes, labels, picks, classes, null_mask, starts, master, momentum, average):
+    )(dy, x, weights, cosine, sine, starts, *kept)
+
+
+HEAD_T = 256
+
+
+def column(row, size):
+    there = lax.broadcasted_iota(jnp.int32, (size, size), 0)
+    here = lax.broadcasted_iota(jnp.int32, (size, size), 1)
+    zero = jnp.zeros((), row.dtype)
+    return jnp.sum(jnp.where(there == here, row, zero), axis=1, keepdims=True)
+
+
+def as_rows(values):
+    there = lax.broadcasted_iota(jnp.int32, (128, 128), 0)
+    here = lax.broadcasted_iota(jnp.int32, (128, 128), 1)
+    return [
+        jnp.sum(
+            jnp.where(there == here, values[k * 128 : (k + 1) * 128], 0.0), axis=0, keepdims=True
+        )
+        for k in range(4)
+    ]
+
+
+def head_kernel(
+    y, picks, info, gain, table, d_top, d_table, small, mine, picked, af, scores, dlow, labels,
+    counts, stat, stats, daf, rx_core, low, rx, fresh, zero_sem, own_sem, pick_send, pick_recv,
+    core_send, core_recv, stat_send, stat_recv, swap_send, swap_recv, daf_send, daf_recv,
+):
+    sec, dp, z, c, par, home = place()
+    last = sec == 3
+    upper = sec >= 2
+    barrier = pltpu.get_barrier_semaphore()
+    other_core = (3, dp + 1 - 2 * c)
+
+    def greet(s, e):
+        pl.semaphore_signal(barrier, 1, device_id=(s, e), device_id_type=MESH)
+
+    def greet_second():
+        for k in range(4):
+            greet(3, 2 * k + c)
+        pl.semaphore_wait(barrier, 4)
+
+    def greet_third():
+        for k in range(4):
+            greet(2, 2 * k + c)
+        for k in range(1, 8):
+            greet(3, lax.rem(dp + k, 8))
+        pl.semaphore_wait(barrier, 11)
+
+    all_zero = pltpu.make_async_copy(fresh, d_table, zero_sem)
+
+    def zeros():
+        fresh[...] = jnp.zeros_like(fresh)
+        all_zero.start()
+
+    pl.when(jnp.logical_not(last))(zeros)
+    small[...] = jnp.zeros_like(small)
+    pick_row = picks[pl.ds(par, 1), :]
+    pick_col = column(pick_row, PICKS)
+
+    def choose():
+        ids = lax.broadcasted_iota(jnp.int32, (PICKS, SP), 1)
+        mine[...] = nn(jnp.where(ids == pick_col, 1.0, 0.0).astype(BF16), y[...]).astype(BF16)
+
+    pl.when(upper)(choose)
+    pl.when(sec == 2)(greet_second)
+    pl.when(last)(greet_third)
+
+    def rows(p, zz, lane):
+        return pl.ds(pl.multiple_of((2 * (2 * zz + lane) + p) * PICKS, PICKS), PICKS)
+
+    def pick_to(k):
+        zz = lax.rem(z + k, 4)
+        return pltpu.make_async_remote_copy(
+            src_ref=mine,
+            dst_ref=picked.at[rows(par, z, c)],
+            send_sem=pick_send,
+            recv_sem=pick_recv.at[par, z],
+            device_id=(3, 2 * zz + c),
+            device_id_type=MESH,
+        )
+
+    def came(p, k):
+        zz = lax.rem(z + k, 4)
+        return pltpu.make_async_remote_copy(
+            src_ref=mine,
+            dst_ref=picked.at[rows(p, zz, c)],
+            send_sem=pick_send,
+            recv_sem=pick_recv.at[p, zz],
+            device_id=other_core,
+            device_id_type=MESH,
+        )
+
+    def forward(p, k):
+        part = picked.at[rows(p, lax.rem(z + k, 4), c)]
+        return pltpu.make_async_remote_copy(
+            src_ref=part,
+            dst_ref=part,
+            send_sem=core_send,
+            recv_sem=core_recv,
+            device_id=other_core,
+            device_id_type=MESH,
+        )
+
+    def span(ref, count, send, recv):
+        part = ref.at[pl.ds(0, count)]
+        return pltpu.make_async_remote_copy(
+            src_ref=part,
+            dst_ref=part,
+            send_sem=send,
+            recv_sem=recv,
+            device_id=other_core,
+            device_id_type=MESH,
+        )
+
+    def pick_second():
+        for k in (1, 2, 3, 0):
+            pick_to(k).start()
+
+    def pick_third():
+        own = pltpu.make_async_copy(mine, picked.at[rows(1, z, c)], own_sem)
+        own.start()
+        for k in range(1, 4):
+            pick_to(k).start()
+        for e in range(8):
+            for p in range(2):
+                at = pl.ds((2 * e + p) * PICKS, PICKS)
+                labels[at, :] = column(info[e, 2 + p : 3 + p, :][:, :PICKS], PICKS)
+                counts[at, :] = column(info[e, 4 + p : 5 + p, :][:, :PICKS].astype(F32), PICKS)
+        own.wait()
+        forward(1, 0).start()
+        for k in range(4):
+            came(0, k).wait_recv()
+            forward(0, k).start()
+            if k:
+                came(1, k).wait_recv()
+                forward(1, k).start()
+        span(picked, 8 * PICKS, core_send, core_recv).wait_recv()
+
+    pl.when(sec == 2)(pick_second)
+    pl.when(last)(pick_third)
+    g_f = gain[...].astype(F32)[0:1]
+    own = 2 * HALF
+    tiles = [(t * HEAD_T, HEAD_T) for t in range(own // HEAD_T)] + [
+        (own - own % HEAD_T, own % HEAD_T)
+    ]
+
+    def over_tiles(body):
+        def step(t, carry):
+            body(pl.multiple_of(t * HEAD_T, HEAD_T), HEAD_T)
+            return carry
+
+        lax.fori_loop(0, own // HEAD_T, step, 0)
+        body(own - own % HEAD_T, own % HEAD_T)
+
+    def forward_part():
+        af[...] = rms_scale(picked[...].astype(F32), g_f).astype(BF16)
+        fold = lambda op, block: functools.reduce(
+            op, [block[:, k * 128 : (k + 1) * 128] for k in range(block.shape[1] // 128)]
+        )
+        top = daf.at[:, pl.ds(0, 128)]
+        top[...] = jnp.full((16 * PICKS, 128), NEG, F32)
+
+        def product(start, size):
+            ids = lax.broadcasted_iota(jnp.int32, (16 * PICKS, size), 1) + (dp * own + start)
+            block = nt(af[...], table[pl.ds(start, size), :])
+            block = jnp.where(ids < VOCAB, block, NEG)
+            scores[:, pl.ds(start, size)] = block
+            top[...] = jnp.maximum(top[...], fold(jnp.maximum, block))
+
+        over_tiles(product)
+        top_col = jnp.max(top[...], axis=1, keepdims=True)
+        total = daf.at[:, pl.ds(128, 128)]
+        target = daf.at[:, pl.ds(256, 128)]
+        total[...] = jnp.zeros((16 * PICKS, 128), F32)
+        target[...] = jnp.zeros((16 * PICKS, 128), F32)
+
+        def exponents(start, size):
+            ids = lax.broadcasted_iota(jnp.int32, (16 * PICKS, size), 1) + (dp * own + start)
+            block = scores[:, pl.ds(start, size)]
+            grown = jnp.exp(block - top_col)
+            scores[:, pl.ds(start, size)] = grown
+            total[...] += fold(jnp.add, grown)
+            target[...] += fold(jnp.add, jnp.where(ids == labels[...], block, 0.0))
+
+        over_tiles(exponents)
+        stat[...] = jnp.zeros_like(stat)
+        columns = (
+            top_col,
+            jnp.sum(total[...], axis=1, keepdims=True),
+            jnp.sum(target[...], axis=1, keepdims=True),
+        )
+        for k, values in enumerate(columns):
+            for i, row in enumerate(as_rows(values)):
+                stat[4 * k + i : 4 * k + i + 1, :] = row
+        stats[dp] = stat[...]
+        for k in range(1, 8):
+            pltpu.make_async_remote_copy(
+                src_ref=stat,
+                dst_ref=stats.at[dp],
+                send_sem=stat_send,
+                recv_sem=stat_recv,
+                device_id=(3, lax.rem(dp + k, 8)),
+                device_id_type=MESH,
+            ).start()
+        every = span(stats, 7, stat_send, stat_recv)
+        every.wait_recv()
+        tops = [stats[e, 0:4, :] for e in range(8)]
+        best = functools.reduce(jnp.maximum, tops)
+        sums = sum(stats[e, 4:8, :] * jnp.exp(tops[e] - best) for e in range(8))
+        hits = sum(stats[e, 8:12, :] for e in range(8))
+        log_total = best + jnp.log(sums)
+        log_col = jnp.concatenate([column(log_total[k : k + 1], 128) for k in range(4)], axis=0)
+        hit_col = jnp.concatenate([column(hits[k : k + 1], 128) for k in range(4)], axis=0)
+        loss = jnp.sum(
+            jnp.where(counts[...] > 0, log_col - hit_col, 0.0), axis=0, keepdims=True
+        )
+        lane = lax.broadcasted_iota(jnp.int32, (1, 128), 1)
+        small[6:7, :] = jnp.where(jnp.logical_and(lane == 0, dp == 0), loss, 0.0)
+        shrink = jnp.exp(top_col - log_col)
+
+        def slopes(start, size):
+            ids = lax.broadcasted_iota(jnp.int32, (16 * PICKS, size), 1) + (dp * own + start)
+            hit = jnp.where(ids == labels[...], 1.0, 0.0)
+            block = (scores[:, pl.ds(start, size)] * shrink - hit) * counts[...]
+            dlow[:, pl.ds(start, size)] = block.astype(BF16)
+
+        over_tiles(slopes)
+        for b in range(3):
+            cols = pl.ds(b * 256, 256)
+            daf[:, cols] = nn(dlow[...], table[:, cols])
+        every.wait_send()
+        span(picked, 3 * PICKS, pick_send, core_recv).wait_send()
+        span(picked, 8 * PICKS, core_send, core_recv).wait_send()
+
+    def swap(p, zz):
+        return pltpu.make_async_remote_copy(
+            src_ref=daf.at[rows(p, zz, 1 - c)],
+            dst_ref=rx_core.at[pl.ds((2 * zz + p) * PICKS, PICKS)],
+            send_sem=swap_send,
+            recv_sem=swap_recv,
+            device_id=other_core,
+            device_id_type=MESH,
+        )
+
+    def back_to(p, k):
+        zz = lax.rem(z + k, 4)
+        return pltpu.make_async_remote_copy(
+            src_ref=low.at[pl.ds(pl.multiple_of((2 * zz + p) * PICKS, PICKS), PICKS)],
+            dst_ref=rx.at[z],
+            send_sem=daf_send,
+            recv_sem=daf_recv,
+            device_id=(2 + p, 2 * zz + c),
+            device_id_type=MESH,
+        )
+
+    def table_part(start, size):
+        there = pl.ds(start, size)
+        value = tn(dlow[:, there], af[...])
+        fresh[there, :] = value
+        pltpu.make_async_copy(fresh.at[there], d_table.at[there], zero_sem).start()
+        folded = jnp.sum(value * value, axis=0, keepdims=True)
+        small[7:8, :] += functools.reduce(
+            jnp.add, [folded[:, k * 128 : (k + 1) * 128] for k in range(6)]
+        )
+
+    def third():
+        forward_part()
+        for zz in range(4):
+            for p in range(2):
+                swap(p, zz).start()
+        table_part(own - own % HEAD_T, own % HEAD_T)
+        span(rx_core, 8 * PICKS, swap_send, swap_recv).wait_recv()
+        for zz in range(4):
+            for p in range(2):
+                there = pl.ds((2 * zz + p) * PICKS, PICKS)
+                low[there, :] = (daf[rows(p, zz, c), :] + rx_core[there, :]).astype(BF16)
+        for k in (1, 2, 3, 0):
+            back_to(0, k).start()
+            if k:
+                back_to(1, k).start()
+
+        def step(t, carry):
+            table_part(pl.multiple_of(t * HEAD_T, HEAD_T), HEAD_T)
+            return carry
+
+        lax.fori_loop(0, own // HEAD_T, step, 0)
+        rx[z] = low[pl.ds(pl.multiple_of((2 * z + 1) * PICKS, PICKS), PICKS), :]
+        span(rx_core, 8 * PICKS, swap_send, swap_recv).wait_send()
+        span(low, 7 * PICKS, daf_send, daf_recv).wait_send()
+        span(rx, 3, daf_send, daf_recv).wait_recv()
+
+    def second():
+        span(picked, 4 * PICKS, pick_send, core_recv).wait_send()
+        span(rx, 4, daf_send, daf_recv).wait_recv()
+
+    pl.when(last)(third)
+    pl.when(sec == 2)(second)
+
+    def finish():
+        summed = rx[0].astype(F32)
+        for k in range(1, 4):
+            summed = summed + rx[k].astype(F32)
+        grad, dg_f = rms_back(mine[...].astype(F32), g_f, summed)
+        for k in range(6):
+            small[k : k + 1, :] = dg_f[:, k * 128 : (k + 1) * 128]
+        ids = lax.broadcasted_iota(jnp.int32, (SP, PICKS), 0)
+        spread = jnp.where(ids == pick_row, 1.0, 0.0).astype(BF16)
+        rest = grad
+        out = jnp.zeros((SP, D), F32)
+        for _ in range(3):
+            part = rest.astype(BF16)
+            out = out + nn(spread, part)
+            rest = rest - part.astype(F32)
+        d_top[...] = out.astype(BF16)
+
+    def none():
+        d_top[...] = jnp.zeros_like(d_top)
+
+    pl.when(upper)(finish)
+    pl.when(jnp.logical_not(upper))(none)
+    all_zero.wait()
+
+
+def head_call(y, picks, info, gain, table):
+    low = lambda *shape: pltpu.VMEM(shape, BF16)
+    wide = lambda *shape: pltpu.VMEM(shape, F32)
+    n = 16 * PICKS
+    return pl.pallas_call(
+        head_kernel,
+        out_shape=(
+            jax.ShapeDtypeStruct((SP, D), BF16),
+            jax.ShapeDtypeStruct((2 * HALF, D), F32),
+            jax.ShapeDtypeStruct((8, 128), F32),
+        ),
+        in_specs=[VMEM] * 5,
+        out_specs=(VMEM, ANY, VMEM),
+        scratch_shapes=[
+            low(PICKS, D),
+            low(n, D),
+            low(n, D),
+            wide(n, 2 * HALF),
+            low(n, 2 * HALF),
+            pltpu.VMEM((n, 1), jnp.int32),
+            wide(n, 1),
+            wide(16, 128),
+            wide(8, 16, 128),
+            wide(n, D),
+            wide(8 * PICKS, D),
+            low(8 * PICKS, D),
+            low(4, PICKS, D),
+            wide(2 * HALF, D),
+            pltpu.SemaphoreType.DMA,
+            pltpu.SemaphoreType.DMA,
+            pltpu.SemaphoreType.DMA,
+            pltpu.SemaphoreType.DMA((2, 4)),
+        ]
+        + [pltpu.SemaphoreType.DMA] * 8,
+        compiler_params=pltpu.CompilerParams(
+            collective_id=3, has_side_effects=True, vmem_limit_bytes=56 * 2**20
+        ),
+        name="head",
+    )(y, picks, info, gain, table)
+
+
+def open_anywhere(codes, labels, picks, classes, null_mask, starts, table, frequency):
     sec = lax.axis_index("section")
     d = lax.axis_index("dp")
-    n_dp = lax.axis_size("dp")
-    n_sec = lax.axis_size("section")
     par = lax.rem(sec, 2)
-    own = master.shape[0]
-    learn_rate = rate_factor * math.sqrt(own * n_sec * n_dp)
-    embed_factor = math.sqrt(D)
-    beside = [(0, 1), (1, 0), (2, 3), (3, 2)]
-    fast = n_sec == 4 and n_dp == 8 and own == 2 * HALF
-    table = master.astype(BF16)
-    gain_row = lax.slice_in_dim(table, VOCAB % own, VOCAB % own + 1)[0].astype(F32)
-    gain_at = VOCAB // own
-
-    row_index, counted, segment, position = jax.vmap(row_layout)(starts, classes, null_mask, codes)
+    own = table.shape[0]
+    row_index, counted, _, position = jax.vmap(row_layout)(starts, classes, null_mask, codes)
     picked_labels = jnp.take_along_axis(labels, picks, axis=1)
     picked_counts = jnp.take_along_axis(counted, picks, axis=1).astype(jnp.int32)
     row_index = jnp.pad(row_index, ((0, 0), (0, SP - SLOTS)), constant_values=-1)
     info = jnp.concatenate([row_index, picked_labels, picked_counts], axis=1)
-    if fast:
-        block = jnp.concatenate([info.reshape(-1).astype(F32), gain_row])
-        block = jnp.pad(block, (0, 2048 - block.shape[0])).reshape(16, 128)
-        info = share(block, n_sec, n_dp, 2, "share_info").reshape(n_sec, n_dp, 2048)
-        g_f = info[3, gain_at, 2 * (SP + 2 * PICKS) :][:D]
-        info = info[0, :, : 2 * (SP + 2 * PICKS)].reshape(2 * n_dp, -1).astype(jnp.int32)
-    else:
-        info = lax.all_gather(info, "dp", axis=0, tiled=True)
-        holds = (sec == 3) & (d == gain_at)
-        g_f = lax.psum(jnp.where(holds, gain_row, 0.0), ("section", "dp"))
-    all_index = info[:, :SP].reshape(-1)
+    info = lax.all_gather(info, "dp", axis=0, tiled=True)
     all_labels = info[:, SP : SP + PICKS].reshape(-1)
     all_counts = info[:, SP + PICKS :].reshape(-1).astype(F32)
-    segment = jnp.pad(segment[par], (0, SP - SLOTS), constant_values=SEGS + 2)
+    gain_row = lax.slice_in_dim(table, VOCAB % own, VOCAB % own + 1)[0].astype(F32)
+    holds = (sec == 3) & (d == VOCAB // own)
+    g_f = lax.psum(jnp.where(holds, gain_row, 0.0), ("section", "dp"))
     position = jnp.pad(position[par], (0, SP - SLOTS))
-    frequency = rope_base ** (-jnp.arange(HD // 2, dtype=F32) * 2.0 / HD)
     angles = position.astype(F32)[:, None] * frequency[None, :]
     cosine = jnp.tile(jnp.cos(angles), (1, 4))
     sine = jnp.tile(jnp.concatenate([-jnp.sin(angles), jnp.sin(angles)], axis=1), (1, 2))
-    around = (cosine, sine, segment[:, None], segment[None, :])
-
-    local = jnp.where(sec == 0, all_index, -1) - d * own
-    if fast:
-        weights, x0 = gather_and_embed(table, local[:, None])
-    else:
-        gathered = lax.all_gather(table, "dp", axis=0, tiled=True)[:WROWS]
-        other = lax.ppermute(gathered, "section", beside)
-        weights = jnp.where((sec == 1) | (sec == 2), gathered, other)
-        onehot = (local[:, None] == jnp.arange(own)[None, :]).astype(BF16)
-        looked = (nn(onehot, table) * embed_factor).astype(BF16)
-        looked = lax.psum_scatter(looked, "dp", scatter_dimension=0, tiled=True).reshape(2, SP, D)
-        from_first = lax.ppermute(looked[1], "section", [(0, 1)])
-        x0 = jnp.where(sec == 0, looked[0], from_first)
-
-    y0 = forward_call(x0, weights, *around)[0]
-    x = jnp.where(sec < 2, x0, lax.ppermute(y0, "section", [(0, 2), (1, 3)]))
-    y, *kept = forward_call(x, weights, *around)
-
-    my_picks = picks[par]
+    gathered = lax.all_gather(table, "dp", axis=0, tiled=True)[:WROWS]
+    other = lax.ppermute(gathered, "section", [(0, 1), (1, 0), (2, 3), (3, 2)])
+    weights = jnp.where((sec == 1) | (sec == 2), gathered, other)
+    local = jnp.where(sec == 0, info[:, :SP].reshape(-1), -1) - d * own
+    onehot = (local[:, None] == jnp.arange(own)[None, :]).astype(BF16)
+    looked = (nn(onehot, table) * math.sqrt(D)).astype(BF16)
+    looked = lax.psum_scatter(looked, "dp", scatter_dimension=0, tiled=True).reshape(2, SP, D)
+    from_first = lax.ppermute(looked[1], "section", [(0, 1)])
+    x0 = jnp.where(sec == 0, looked[0], from_first)
+    return weights, x0, local, all_labels, all_counts, g_f, cosine, sine
+
+
+def head_anywhere(y, my_picks, all_labels, all_counts, g_f, table):
+    sec = lax.axis_index("section")
+    d = lax.axis_index("dp")
+    n_sec = lax.axis_size("section")
+    n_dp = lax.axis_size("dp")
+    own = table.shape[0]
     picked = jnp.take(y, my_picks, axis=0)
-    if fast:
-        all_picked = share_picked(picked)
-    else:
-        all_picked = lax.all_gather(picked, ("section", "dp"), axis=0, tiled=False)
-        all_picked = all_picked.reshape(n_sec, n_dp, PICKS, D)[2:].transpose(1, 0, 2, 3)
+    all_picked = lax.all_gather(picked, ("section", "dp"), axis=0, tiled=False)
+    all_picked = all_picked.reshape(n_sec, n_dp, PICKS, D)[2:].transpose(1, 0, 2, 3)
     all_picked = all_picked.reshape(-1, D).astype(F32)
     af = jnp.where(sec == 3, rms_scale(all_picked, g_f), 0.0).astype(BF16)
     vocab_ids = d * own + jnp.arange(own)
-    logits = jnp.where(vocab_ids[None, :] < VOCAB, nt(af, table), -1e30)
+    logits = jnp.where(vocab_ids[None, :] < VOCAB, nt(af, table), NEG)
     local_max = jnp.max(logits, axis=1)
     hit = vocab_ids[None, :] == all_labels[:, None]
     sums = jnp.stack(
@@ -1453,11 +1671,7 @@
             jnp.sum(jnp.where(hit, logits, 0.0), axis=1),
         ]
     )
-    if fast:
-        block = jnp.pad(sums.reshape(-1, 128), ((0, 4), (0, 0)))
-        every = share_row(block, n_dp, 3, "share_sums")[:, :12].reshape(n_dp, 3, -1)
-    else:
-        every = lax.all_gather(sums, "dp", axis=0, tiled=False)
+    every = lax.all_gather(sums, "dp", axis=0, tiled=False)
     top = jnp.max(every[:, 0], axis=0)
     total = jnp.sum(every[:, 1] * jnp.exp(every[:, 0] - top), axis=0)
     target = jnp.sum(every[:, 2], axis=0)
@@ -1465,27 +1679,67 @@
     loss_part = jnp.where(
         (sec == 3) & (d == 0), jnp.sum(jnp.where(all_counts > 0, log_total - target, 0.0)), 0.0
     )
-    count_sum = jnp.sum(all_counts)
     dlogits = (jnp.exp(logits - log_total[:, None]) - hit.astype(F32)) * all_counts[:, None]
     dlogits = jnp.where(sec == 3, dlogits, 0.0).astype(BF16)
     d_table = tn(dlogits, af)
-    if fast:
-        daf = unpick(nn(dlogits, table))
-    else:
-        daf = lax.psum(nn(dlogits, table), "dp")
-        daf = lax.dynamic_slice_in_dim(daf, d * 2 * PICKS, 2 * PICKS).reshape(2, PICKS, D)
-        daf = jnp.where(sec == 3, daf[1], lax.ppermute(daf[0], "section", [(3, 2)]))
+    daf = lax.psum(nn(dlogits, table), "dp")
+    daf = lax.dynamic_slice_in_dim(daf, d * 2 * PICKS, 2 * PICKS).reshape(2, PICKS, D)
+    daf = jnp.where(sec == 3, daf[1], lax.ppermute(daf[0], "section", [(3, 2)]))
     d_own, dg_f = rms_pull(picked.astype(F32), g_f, daf)
     dg_f = jnp.where(sec >= 2, dg_f, 0.0)
     spread = (jnp.arange(SP)[:, None] == my_picks[None, :]).astype(F32)
     d_top = jnp.dot(spread, d_own, precision=lax.Precision.HIGHEST).astype(BF16)
+    return d_top, d_table, dg_f, loss_part
+
+
+def shards(codes, labels, picks, classes, null_mask, starts, master, momentum, average):
+    sec = lax.axis_index("section")
+    d = lax.axis_index("dp")
+    n_dp = lax.axis_size("dp")
+    n_sec = lax.axis_size("section")
+    par = lax.rem(sec, 2)
+    own = master.shape[0]
+    learn_rate = rate_factor * math.sqrt(own * n_sec * n_dp)
+    beside = [(0, 1), (1, 0), (2, 3), (3, 2)]
+    fast = n_sec == 4 and n_dp == 8 and own == 2 * HALF
+    table = master.astype(BF16)
+    gain_at = VOCAB // own
+    frequency = rope_base ** (-jnp.arange(HD // 2, dtype=F32) * 2.0 / HD)
+
+    if fast:
+        wide = jnp.tile(frequency[None, :], (1, 4))
+        weights, x0, info, gain, cosine, sine = gather_and_embed(
+            table, codes, labels, picks, starts, classes, null_mask, wide
+        )
+        all_index = info[:, :2, :SP].reshape(-1)
+        local = jnp.where(sec == 0, all_index, -1) - d * own
+    else:
+        opened = open_anywhere(codes, labels, picks, classes, null_mask, starts, table, frequency)
+        weights, x0, local, all_labels, all_counts, g_f, cosine, sine = opened
+    around = (cosine, sine, starts)
+
+    y0 = forward_call(x0, weights, *around)[0]
+    x = jnp.where(sec < 2, x0, lax.ppermute(y0, "section", [(0, 2), (1, 3)]))
+    y, *kept = forward_call(x, weights, *around)
+
+    if fast:
+        d_top, d_table, small = head_call(y, picks, info, gain, table)
+    else:
+        d_top, d_table, dg_f, loss_part = head_anywhere(
+            y, picks[par], all_labels, all_counts, g_f, table
+        )
+
     dx1 = backward_call(False, d_top, x, weights, *around, kept)
     dy = jnp.where(sec < 2, lax.ppermute(dx1, "section", [(2, 0), (3, 1)]), d_top)
     dx0, grads = backward_call(True, dy, x, weights, *around, kept)
 
     if fast:
         grad, squares = reduce_and_scatter(grads, d_table, dx0, local[None, :])
-        squares = jnp.sum(squares) + jnp.sum(d_table * d_table)
+        squares = squares.reshape(-1, 6, 128).sum(axis=(0, 1))
+        small = small + jnp.where(jnp.arange(8)[:, None] == 7, squares[None, :], 0.0)
+        totals = jnp.sum(share(small, n_sec, n_dp, 8, "share_norm"), axis=0)
+        dg_f, loss_sum, squares = totals[:6].reshape(-1), totals[6, 0], jnp.sum(totals[7])
+        count_sum = jnp.sum(info[:, 4:6, :PICKS].astype(F32))
     else:
         grads = grads.astype(F32) + lax.ppermute(grads, "section", beside).astype(F32)
         grads = jnp.pad(grads.astype(BF16), ((0, own * n_dp - WROWS), (0, 0)))
@@ -1493,16 +1747,11 @@
         grad = jnp.where(sec == 3, d_table, grad)
         pair = jnp.stack([dx0, lax.ppermute(dx0, "section", [(1, 0)])])
         all_dx = lax.all_gather(pair, "dp", axis=0, tiled=True).reshape(-1, D)
-        grad = jnp.where(sec == 0, tn(onehot, all_dx) * embed_factor, grad)
-        squares = jnp.sum(grad * grad)
-
-    if fast:
-        block = jnp.concatenate([dg_f, jnp.stack([squares, loss_part]), jnp.zeros((254,), F32)])
-        totals = jnp.sum(share(block.reshape(8, 128), n_sec, n_dp, 8, "share_norm"), axis=0)
-        totals = totals.reshape(-1)
-        dg_f, squares, loss_sum = totals[:D], totals[D], totals[D + 1]
-    else:
-        dg_f, squares, loss_sum = lax.psum((dg_f, squares, loss_part), ("section", "dp"))
+        onehot = (jnp.arange(own)[:, None] == local[None, :]).astype(BF16)
+        grad = jnp.where(sec == 0, nn(onehot, all_dx) * math.sqrt(D), grad)
+        totals = (dg_f, jnp.sum(grad * grad), loss_part)
+        dg_f, squares, loss_sum = lax.psum(totals, ("section", "dp"))
+        count_sum = jnp.sum(all_counts)
     grad_norm = jnp.sqrt(squares + jnp.sum(dg_f * dg_f))
     gain_here = (jnp.arange(own) == VOCAB % own)[:, None] & (sec == 3) & (d == gain_at)
     grad = grad + jnp.where(gain_here, dg_f[None, :], 0.0)

time: 535 us -> 476 us (0.89); the launches traced: 526 us -> 476 us
  Pallas kernels: 402 us -> 363 us
  waiting for transfers between devices: 38.7 us -> 67 us
  matrix products: 15.2 us -> 0 us
  local copies, waits for them, and re-layouts: 23 us -> 10.7 us
  other arithmetic: 38.7 us -> 28.4 us
    ppermute x1, waiting for transfers between devices: 32.3 us -> 58.7 us  [shards(): lax.ppermute(dx1, 'section', [(2, 0), (3, 1)])]
    pallas_call x1, Pallas kernels: 137 us -> 119 us  [reduce_and_scatter(): pl.pallas_call(close_kernel, out_shape=(jax.ShapeDtypeStruct((2 * HALF, D...]
    dot_general x4 -> x0, matrix products: 15.2 us -> none  [the longest x1 5.43 us: tn(): lax.dot_general(left, right, (((0,), (0,)), ((), ())), preferred_element_...]
    pallas_call x3 -> x1, Pallas kernels: 18.7 us -> 6.26 us  [head_call(): pl.pallas_call(head_kernel, out_shape=(jax.ShapeDtypeStruct((SP, D), BF16...]
    pallas_call x2 -> x1, Pallas kernels: 26.2 us -> 17.1 us  [share(): pl.pallas_call(functools.partial(share_kernel, n_sec, n_dp), out_shape=ja...]
    unnamed x48 -> x34, local copies, waits for them, and re-layouts: 11.6 us -> 8.92 us
where the time goes in v2:
time: 476 us
  Pallas kernels  363 us (76%)
  waiting for transfers between devices  67 us (14%)
  other arithmetic  28.4 us (6%)
  local copies, waits for them, and re-layouts  10.7 us (2%)
    pallas_call x1, Pallas kernels, gather_and_embed(): pl.pallas_call(open_kernel, out_shape=(jax.ShapeDtypeStruct((WROWS, D), B...  127 us
    pallas_call x1, Pallas kernels, reduce_and_scatter(): pl.pallas_call(close_kernel, out_shape=(jax.ShapeDtypeStruct((2 * HALF, D...  119 us
    pallas_call x2, Pallas kernels, backward_call(): pl.pallas_call(functools.partial(backward_kernel, with_weights), out_shap...  61.7 us
    ppermute x1, waiting for transfers between devices, shards(): lax.ppermute(dx1, 'section', [(2, 0), (3, 1)])  58.7 us
    pallas_call x2, Pallas kernels, forward_call(): pl.pallas_call(forward_kernel, out_shape=(low, low, low, low, low, jax.Sh...  32.4 us
    pallas_call x1, Pallas kernels, share(): pl.pallas_call(functools.partial(share_kernel, n_sec, n_dp), out_shape=ja...  17.1 us
    add x1, other arithmetic, shards(): new_average = average_decay * average + (1.0 - average_decay) * new_master  16.7 us
  transfers between devices with their start and end apart: 2, of which 2 were waited for; matrix products, arithmetic and copies ran while one was open for 1% of the time, Pallas kernels for 0%

profile of v2, /device:TPU:0, one launch (start us, length us, event | category | flops | bytes accessed | tf_op | source)
XLA Modules:
  0.0 475.8 jit_solution(1196331966124570469)
XLA Ops:
  1.3 5.0 %convert_element_type.6.table = bf16[2176,768]{1,0:T(8,128)(2,1)} convert(f32[2176,768]{1,0:T(8,128)} %param.15) | non-fusion elementwise | flops 1671168 | bytes 10027008 | tf_op jit(solution)/shard_map/convert_element_type | solution.py:1705
  6.2 127.3 %gather_and_embed.1 = (bf16[9232,768]{1,0:T(8,128)(2,1)}, bf16[272,768]{1,0:T(8,128)(2,1)}, s32[8,8,384]{2,1,0:T(8,128)}, bf16[16,768]{1,0:T(8,128)(2,1)}, f32[272,128]{1,0:T(8,128)}, /*index=5*/f32[272,128]{1,0:T(8,128)}) custom-call(bf16[2176,768]{1,0:T(8,128)(2,1)} %convert_element_type.6.table, s32[2,264]{1,0:T(2,128)} %codes.1, s32[2,264]{1,0:T(2,128)} %labels.1, ...), custom_call_target="tpu_custom_call" | custom-call | tf_op jit(solution)/shard_map/gather_and_embed/pallas_call | solution.py:554
  133.6 0.9 copy-done.3
  134.5 0.9 copy-done.5
  135.4 1.0 copy-done.7
  136.4 17.0 %layer_forward.2 = (bf16[272,768]{1,0:T(8,128)(2,1)S(1)}, bf16[272,768]{1,0:T(8,128)(2,1)}, bf16[272,768]{1,0:T(8,128)(2,1)}, bf16[272,768]{1,0:T(8,128)(2,1)}, ...) custom-call(bf16[272,768]{1,0:T(8,128)(2,1)S(1)} %copy-done.7, ...), custom_call_target="tpu_custom_call" | custom-call | tf_op jit(solution)/shard_map/layer_forward/pallas_call | solution.py:1102
  153.4 1.3 collective-permute-start
  154.7 8.4 %collective-permute-done = bf16[272,768]{1,0:T(8,128)(2,1)S(1)} collective-permute-done((bf16[272,768]{1,0:T(8,128)(2,1)S(1)}, bf16[272,768]{1,0:T(8,128)(2,1)S(1)}, u32[]{:S(2)}, u32[]{:S(2)}) %collective-permute-start) | collective-permute-done | bytes 417824 | tf_op jit(solution)/shard_map/ppermute | solution.py:1722
  163.2 15.5 %layer_forward.3 = (bf16[272,768]{1,0:T(8,128)(2,1)S(1)}, bf16[272,768]{1,0:T(8,128)(2,1)S(1)}, bf16[272,768]{1,0:T(8,128)(2,1)S(1)}, bf16[272,768]{1,0:T(8,128)...) custom-call(bf16[272,768]{1,0:T(8,128)(2,1)S(1)} %broadcast_select_f, ...), custom_call_target="tpu_custom_call" | custom-call | tf_op jit(solution)/shard_map/layer_forward/pallas_call | solution.py:1102
  178.6 1.4 copy-done
  180.0 0.9 copy-done.2
  184.0 0.8 copy-done.13
  184.7 6.3 %head.1 = (bf16[272,768]{1,0:T(8,128)(2,1)}, f32[2176,768]{1,0:T(8,128)}, f32[8,128]{1,0:T(8,128)}) custom-call(bf16[272,768]{1,0:T(8,128)(2,1)} %copy-done.13, s32[2,32]{1,0:T(2,128)} %picks.3, s32[8,8,384]{2,1,0:T(8,128)} %get-tuple-element.34.info, bf16[16,768]{1,0:T(8,128)(2,1)} %get-tuple-element.35.gain, bf16[2176,768]{1,0:T(8,128)(2,1)} %convert_element_type.6.table), custom_call_target="tpu_custom_call" | custom-call | tf_op jit(solution)/shard_map/head/pallas_call | solution.py:1583
  191.0 24.1 %layer_backward.1 = bf16[272,768]{1,0:T(8,128)(2,1)} custom-call(bf16[272,768]{1,0:T(8,128)(2,1)} %get-tuple-element.37.dy, bf16[272,768]{1,0:T(8,128)(2,1)} %copy-done.1, bf16[9232,768]{1,0:T(8,128)(2,1)} %get-tuple-element.29.w_any, f32[272,128]{1,0:T(8,128)} %get-tuple-element.30.cosine, f32[272,128]{1,0:T(8,128)} %get-tuple-element.31.sine, ...), custom_call_target="tpu_custom_call" | custom-call | tf_op jit(solution)/shard_map/layer_backward/pallas_call | solution.py:1234
  215.1 1.5 collective-permute-start.1
  216.7 0.9 select_subtract_fusion
  218.3 1.4 convert_reduce_fusion
  219.7 58.7 %collective-permute-done.1 = bf16[272,768]{1,0:T(8,128)(2,1)S(1)} collective-permute-done((bf16[272,768]{1,0:T(8,128)(2,1)}, bf16[272,768]{1,0:T(8,128)(2,1)S(1)}, u32[]{:S(2)}, u32[]{:S(2)}) %collective-permute-start.1) | collective-permute-done | bytes 417824 | tf_op jit(solution)/shard_map/ppermute | solution.py:1733
  278.4 0.8 broadcast_select_fusion.dy
  279.2 37.5 %layer_backward_weights.1 = (bf16[272,768]{1,0:T(8,128)(2,1)}, bf16[9232,768]{1,0:T(8,128)(2,1)}) custom-call(bf16[272,768]{1,0:T(8,128)(2,1)} %broadcast_select_fusion.dy, bf16[272,768]{1,0:T(8,128)(2,1)} %copy-done.1, bf16[9232,768]{1,0:T(8,128)(2,1)} %get-tuple-element.29.w_any, f32[272,128]{1,0:T(8,128)} %get-tuple-element.30.cosine, ...), custom_call_target="tpu_custom_call" | custom-call | tf_op jit(solution)/shard_map/layer_backward_weights/pallas_call | solution.py:1234
  316.7 118.6 %reduce_and_scatter.1 = (f32[2176,768]{1,0:T(8,128)}, f32[8,768]{1,0:T(8,128)}) custom-call(bf16[9232,768]{1,0:T(8,128)(2,1)} %get-tuple-element.45.grads, f32[2176,768]{1,0:T(8,128)} %get-tuple-element.46.start, bf16[272,768]{1,0:T(8,128)(2,1)} %get-tuple-element.47.block, s32[1,4352]{1,0:T(1,128)} %sub.21.index), custom_call_target="tpu_custom_call", output_to_operand_aliasing={{0}: (1, {})} | custom-call | tf_op jit(solution)/shard_map/reduce_and_scatter/pallas_call | solution.py:897
  436.8 17.1 %share_norm.1 = f32[32,8,128]{2,1,0:T(8,128)} custom-call(f32[8,128]{1,0:T(8,128)} %select_add_fusion.block), custom_call_target="tpu_custom_call" | custom-call | tf_op jit(solution)/shard_map/share_norm/pallas_call | solution.py:980
  453.9 0.9 reduce_sum.55
  457.9 16.7 %multiply_add_fusion = (f32[2176,768]{1,0:T(8,128)}, f32[2176,768]{1,0:T(8,128)}, f32[2176,768]{1,0:T(8,128)}) fusion(f32[2176,768]{1,0:T(8,128)} %param.17, f32[2176,768]{1,0:T(8,128)} %param.15, f32[]{:T(128)S(6)} %min.3, f32[2176,768]{1,0:T(8,128)} %get-tuple-element.49, f32[768]{0:T(1024)S(1)} %get-tuple-element.53, pred[2176]{0:T(1024)(128)(4,1)S(1)} %fusion.1, ...), kind=kLoop, calls=%fused_computation | loop fusion | flops 20054016 | bytes 46797956 | tf_op jit(solution)/shard_map/add | solution.py:1761
  (41 shorter events, 7.6 us)
Async XLA Ops:
  1.2 132.3 %copy-start.14 = (s32[2,4]{1,0:T(2,128)S(1)}, s32[2,4]{1,0:T(2,128)}, u32[]{:S(2)}) copy-start(s32[2,4]{1,0:T(2,128)} %starts.9) | copy-start | bytes 100
  133.5 0.9 copy-start.3
  134.5 0.9 copy-start.5
  135.4 1.0 copy-start.7
  136.4 26.7 %copy-start.8 = (bf16[272,768]{1,0:T(8,128)(2,1)S(1)}, bf16[272,768]{1,0:T(8,128)(2,1)}, u32[]{:S(2)}) copy-start(bf16[272,768]{1,0:T(8,128)(2,1)} %get-tuple-element.28.x) | copy-start | bytes 1253380
  136.4 26.8 %copy-start.4 = (f32[272,128]{1,0:T(8,128)S(1)}, f32[272,128]{1,0:T(8,128)}, u32[]{:S(2)}) copy-start(f32[272,128]{1,0:T(8,128)} %get-tuple-element.30.cosine) | copy-start | bytes 417796
  136.4 26.8 %copy-start.6 = (f32[272,128]{1,0:T(8,128)S(1)}, f32[272,128]{1,0:T(8,128)}, u32[]{:S(2)}) copy-start(f32[272,128]{1,0:T(8,128)} %get-tuple-element.31.sine) | copy-start | bytes 417796
  153.4 9.7 %collective-permute-start = (bf16[272,768]{1,0:T(8,128)(2,1)S(1)}, bf16[272,768]{1,0:T(8,128)(2,1)S(1)}, u32[]{:S(2)}, u32[]{:S(2)}) collective-permute-start(bf16[272,768]{1,0:T(8,128)(2,1)S(1)} %get-tuple-element.32), channel_id=1, source_target_pairs={{0,16},{8,24},{1,17},{9,25},{2,18},{10,26},{3,19},{11,27},{4,20},{... | collective-permute-start | bytes 1253384 | tf_op jit(solution)/shard_map/ppermute | solution.py:1722
  163.1 15.5 %copy-start.1 = (bf16[272,768]{1,0:T(8,128)(2,1)}, bf16[272,768]{1,0:T(8,128)(2,1)S(1)}, u32[]{:S(2)}) copy-start(bf16[272,768]{1,0:T(8,128)(2,1)S(1)} %broadcast_select_fusion.1.x) | copy-start | bytes 1253380
  178.6 1.4 copy-start
  180.0 0.9 copy-start.2
  180.9 0.7 copy-start.9
  181.6 0.8 copy-start.10
  182.4 0.8 copy-start.11
  183.2 0.8 copy-start.12
  184.0 0.8 copy-start.13
  191.0 87.4 %copy-start.15 = (bf16[272,768]{1,0:T(8,128)(2,1)S(1)}, bf16[272,768]{1,0:T(8,128)(2,1)}, u32[]{:S(2)}) copy-start(bf16[272,768]{1,0:T(8,128)(2,1)} %get-tuple-element.37.dy) | copy-start | bytes 1253380
  215.1 63.2 %collective-permute-start.1 = (bf16[272,768]{1,0:T(8,128)(2,1)}, bf16[272,768]{1,0:T(8,128)(2,1)S(1)}, u32[]{:S(2)}, u32[]{:S(2)}) collective-permute-start(bf16[272,768]{1,0:T(8,128)(2,1)} %layer_backward.1), channel_id=1, source_target_pairs={{16,0},{24,8},{17,1},{25,9},{18,2},{26,10},{19,3},{27,11},{20,4},{... | collective-permute-start | bytes 1253384 | tf_op jit(solution)/shard_map/ppermute | solution.py:1733
  316.7 119.4 %copy-start.16 = (f32[8,128]{1,0:T(8,128)S(1)}, f32[8,128]{1,0:T(8,128)}, u32[]{:S(2)}) copy-start(f32[8,128]{1,0:T(8,128)} %get-tuple-element.36) | copy-start | bytes 12292

commit v3 on v2

--- a/solution.py
+++ b/solution.py
@@ -83,16 +83,26 @@
 VMEM = pl.BlockSpec(memory_space=pltpu.VMEM)
 SMEM = pl.BlockSpec(memory_space=pltpu.SMEM)
 
-HALF = 1088
-CH = 64
-NCH = HALF // CH
-CC = 48
-NCC = 11
-LANE = 4 * HALF
-LAG = 3
+OWN = 2176
+SPLIT = 1152
+COUNT = (18, 16, 18, 16, 11)
+ROWS = (64, 64, 64, 64, 48)
+HELD = (0, SPLIT, OWN, OWN + SPLIT, 2 * OWN)
+LANE = 2 * OWN + 11 * 48
+LAG = 2
 WINDOW = 2
-HOP = 3
+HOP = 2
+PIECES = ((0, 64), (64, 64), (128, 64), (192, 64), (256, 16))
 TURN = 6
+CHOP = 4
+CLAG = 3
+AHEAD = 4
+
+
+def class_base(k, lane):
+    if k == 4:
+        return 4 * OWN
+    return OWN * (2 * (k // 2) + lane) + SPLIT * (k % 2)
 
 
 def place():
@@ -217,16 +227,24 @@
 
 
 def open_kernel(
-    table, codes, labels, picks, starts, classes, nulls, frequency, out, x0, info, gain, cosine,
-    sine, own_sem, recv_sem, recv_c, core_sem, send_sem, sent, mine, rx_core, rx_up, rx_down,
+    master, codes, labels, picks, starts, classes, nulls, frequency, out, x0, info, gain, cosine,
+    sine, table, exact, master_sem, own_sem, recv_sem, recv_c, core_sem, send_sem, sent, mine, rx_core, rx_up, rx_down,
     swap_send, swap_recv, x_send, x_recv, line_send, up_recv, down_recv, last_send, last_recv,
     note, note_send, note_recv, gain_send, gain_recv,
 ):
     sec, dp, z, c, par, home = place()
     targets = hop_targets(sec, dp, c, par)
     classes_of = tree(z, c, home)
-    gain_dp = VOCAB // (2 * HALF)
+    gain_dp = VOCAB // (OWN)
     holds_gain = jnp.logical_and(sec == 3, dp == gain_dp)
+
+    parts = [pl.ds(k * (OWN // 4), OWN // 4) for k in range(4)]
+    fetch = [
+        pltpu.make_async_copy(master.at[part], exact.at[part], master_sem.at[k])
+        for k, part in enumerate(parts)
+    ]
+    for one in fetch:
+        one.start()
 
     barrier = pltpu.get_barrier_semaphore()
 
@@ -256,6 +274,9 @@
         )
         note[4 + r : 5 + r, :PICKS] = segment_of(starts, r, chosen)[2].astype(jnp.int32)
     info[dp] = note[...]
+    for one, part in zip(fetch, parts):
+        one.wait()
+        table[part, :] = exact[part, :].astype(BF16)
     count = 8 + jnp.logical_or(sec == 0, sec == 2).astype(jnp.int32)
     pl.semaphore_wait(barrier, count + 7 * holds_gain.astype(jnp.int32))
     for k in range(1, 8):
@@ -276,7 +297,7 @@
         device_id_type=MESH,
     )
 
-    gain_rows = table.at[pl.ds(VOCAB % (2 * HALF), 16)]
+    gain_rows = table.at[pl.ds(VOCAB % (OWN), 16)]
 
     def gain_to(s, e):
         return pltpu.make_async_remote_copy(
@@ -300,28 +321,23 @@
     def keep(rows):
         return pltpu.make_async_copy(
             table.at[pl.ds(0, rows)],
-            out.at[pl.ds(pl.multiple_of(dp * 2 * HALF, 16), rows)],
+            out.at[pl.ds(pl.multiple_of(dp * OWN, 16), rows)],
             own_sem,
         )
 
     def keep_all():
-        keep(2 * HALF).start()
-        keep(2 * HALF).wait()
+        keep(OWN).start()
+        keep(OWN).wait()
 
     def keep_few():
-        keep(NCC * CC).start()
-        keep(NCC * CC).wait()
+        keep(11 * 48).start()
+        keep(11 * 48).wait()
 
     pl.when(jnp.logical_and(home, z < 2))(keep_all)
     pl.when(classes_of[4][0])(keep_few)
 
-    def base(k, lane):
-        if k == 4:
-            return 4 * 2 * HALF
-        return 2 * HALF * (2 * (k // 2) + lane) + HALF * (k % 2)
-
     def copy(k, hop, j, rows, recv, slot):
-        part = out.at[pl.ds(pl.multiple_of(base(k, c) + j * rows, 16), rows)]
+        part = out.at[pl.ds(pl.multiple_of(class_base(k, c) + j * rows, 16), rows)]
         return pltpu.make_async_remote_copy(
             src_ref=part,
             dst_ref=part,
@@ -349,7 +365,7 @@
         send("core")
 
     def counts(k):
-        return (NCC, CC) if k == 4 else (NCH, CH)
+        return COUNT[k], ROWS[k]
 
     first = sec == 0
     second = sec == 2
@@ -381,33 +397,32 @@
             device_id_type=MESH,
         )
 
-    def go_up(zz):
+    def piece_of(k, q):
+        start, size = PIECES[q]
+        return pl.ds(pl.multiple_of(k * SP + start, 16), size)
+
+    def go(zz, q, ref, recv, hop):
         return pltpu.make_async_remote_copy(
-            src_ref=mine.at[slot(zz)],
-            dst_ref=rx_down.at[slot(zz)],
+            src_ref=mine.at[piece_of(zz, q)],
+            dst_ref=ref.at[piece_of(zz, q)],
             send_sem=line_send,
-            recv_sem=down_recv.at[zz],
-            device_id=targets["up"],
-            device_id_type=MESH,
-        )
-
-    def go_down(zz):
-        return pltpu.make_async_remote_copy(
-            src_ref=mine.at[slot(zz)],
-            dst_ref=rx_up.at[slot(zz)],
-            send_sem=line_send,
-            recv_sem=up_recv.at[zz],
-            device_id=targets["down"],
-            device_id_type=MESH,
-        )
-
-    def add(k, ref):
-        there = slot(k)
+            recv_sem=recv.at[zz, q],
+            device_id=targets[hop],
+            device_id_type=MESH,
+        )
+
+    def go_up(zz, q):
+        return go(zz, q, rx_down, down_recv, "up")
+
+    def go_down(zz, q):
+        return go(zz, q, rx_up, up_recv, "down")
+
+    def add(there, ref):
         mine[there, :] = (mine[there, :].astype(F32) + ref[there, :].astype(F32)).astype(BF16)
 
     def look(row):
-        local = column(info[row // 2, pl.ds(lax.rem(row, 2), 1), :][:, :SP], SP) - dp * 2 * HALF
-        ids = lax.broadcasted_iota(jnp.int32, (SP, 2 * HALF), 1)
+        local = column(info[row // 2, pl.ds(lax.rem(row, 2), 1), :][:, :SP], SP) - dp * OWN
+        ids = lax.broadcasted_iota(jnp.int32, (SP, OWN), 1)
         onehot = jnp.where(ids == local, 1.0, 0.0).astype(BF16)
         return (nn(onehot, table[...]) * math.sqrt(D)).astype(BF16)
 
@@ -419,23 +434,24 @@
         swap(k).start()
         mine[slot(k), :] = look(2 * (2 * zz + c) + p)
         swap(k).wait_recv()
-        add(k, rx_core)
+        add(slot(k), rx_core)
         pl.when(p == 1)(lambda: cross(zz).start())
 
-    def chain(zz):
+    def chain(zz, q):
         def from_below():
-            go_up(zz).wait_recv()
-            add(zz, rx_down)
+            go_up(zz, q).wait_recv()
+            add(piece_of(zz, q), rx_down)
 
         def from_above():
-            go_down(zz).wait_recv()
-            add(zz, rx_up)
-
-        pl.when(second)(cross(zz).wait_recv)
+            go_down(zz, q).wait_recv()
+            add(piece_of(zz, q), rx_up)
+
+        if q == 0:
+            pl.when(second)(cross(zz).wait_recv)
         pl.when(jnp.logical_and(zz >= z, z > 0))(from_below)
         pl.when(jnp.logical_and(zz <= z, z < 3))(from_above)
-        pl.when(zz > z)(lambda: go_up(zz).start())
-        pl.when(zz < z)(lambda: go_down(zz).start())
+        pl.when(zz > z)(lambda: go_up(zz, q).start())
+        pl.when(zz < z)(lambda: go_down(zz, q).start())
 
     def chains(i):
         for o in range(4):
@@ -443,7 +459,9 @@
             hops = jnp.maximum(
                 z * (zz >= z).astype(jnp.int32), (3 - z) * (zz <= z).astype(jnp.int32)
             )
-            pl.when(i == 2 * o + 2 + sec + HOP * hops)(lambda zz=zz: chain(zz))
+            for q in range(5):
+                now = i == 2 * o + 2 + sec + HOP * hops + q
+                pl.when(now)(lambda zz=zz, q=q: chain(zz, q))
 
     segment, position, _, _ = segment_of(starts, par, lax.broadcasted_iota(jnp.int32, (SP, 128), 0))
     angles = position.astype(F32) * frequency[...]
@@ -465,7 +483,7 @@
         pl.when(jnp.logical_and(second, i == last_step))(lambda: last().start())
         return carry
 
-    last_step = 6 + 2 + 2 + 3 * HOP + 1
+    last_step = 6 + 2 + 2 + 3 * HOP + 4 + 1
 
     def last():
         return pltpu.make_async_remote_copy(
@@ -477,7 +495,7 @@
             device_id_type=MESH,
         )
 
-    lax.fori_loop(0, max(NCH + 5 * LAG, last_step + 1), step, 0)
+    lax.fori_loop(0, max(18 + 5 * LAG, last_step + 1), step, 0)
 
     def blocks(count, sem):
         return pltpu.make_async_remote_copy(
@@ -532,7 +550,7 @@
 
     def came(k):
         count, rows = counts(k)
-        part = out.at[pl.ds(pl.multiple_of(base(k, 1 - c), 16), count * rows)]
+        part = out.at[pl.ds(pl.multiple_of(class_base(k, 1 - c), 16), count * rows)]
         pltpu.make_async_remote_copy(
             src_ref=part,
             dst_ref=part,
@@ -549,7 +567,7 @@
     pl.when(c == 1)(lambda: came(4))
 
 
-def gather_and_embed(table, codes, labels, picks, starts, classes, nulls, frequency):
+def gather_and_embed(master, codes, labels, picks, starts, classes, nulls, frequency):
     rows = lambda n: pltpu.VMEM((n * SP, D), BF16)
     return pl.pallas_call(
         open_kernel,
@@ -560,13 +578,16 @@
             jax.ShapeDtypeStruct((16, D), BF16),
             jax.ShapeDtypeStruct((SP, 128), F32),
             jax.ShapeDtypeStruct((SP, 128), F32),
+            jax.ShapeDtypeStruct((OWN, D), BF16),
         ),
-        in_specs=[VMEM] * 4 + [SMEM] * 3 + [VMEM],
-        out_specs=(VMEM,) * 6,
+        in_specs=[ANY] + [VMEM] * 3 + [SMEM] * 3 + [VMEM],
+        out_specs=(VMEM,) * 7,
         scratch_shapes=[
+            pltpu.VMEM((OWN, D), F32),
+            pltpu.SemaphoreType.DMA((4,)),
             pltpu.SemaphoreType.DMA,
-            pltpu.SemaphoreType.DMA((4, NCH)),
-            pltpu.SemaphoreType.DMA((NCC,)),
+            pltpu.SemaphoreType.DMA((4, 18)),
+            pltpu.SemaphoreType.DMA((11,)),
             pltpu.SemaphoreType.DMA((5,)),
             pltpu.SemaphoreType.DMA((5, 4, WINDOW)),
             rows(8),
@@ -579,8 +600,8 @@
             pltpu.SemaphoreType.DMA,
             pltpu.SemaphoreType.DMA((4,)),
             pltpu.SemaphoreType.DMA,
-            pltpu.SemaphoreType.DMA((4,)),
-            pltpu.SemaphoreType.DMA((4,)),
+            pltpu.SemaphoreType.DMA((4, 5)),
+            pltpu.SemaphoreType.DMA((4, 5)),
             pltpu.SemaphoreType.DMA,
             pltpu.SemaphoreType.DMA,
             pltpu.VMEM((8, 384), jnp.int32),
@@ -590,124 +611,151 @@
             collective_id=0, has_side_effects=True, vmem_limit_bytes=56 * 2**20
         ),
         name="gather_and_embed",
-    )(table, codes, labels, picks, starts, classes, nulls, frequency)
+    )(master, codes, labels, picks, starts, classes, nulls, frequency)
 
 
 def close_kernel(
-    grads, start, block, index, out, squares, loc, rx_core, rx_up, rx_down, rx_x, total, summed,
-    all_dx, load_sem, core_sem, core_c, recv_sem, recv_c, core_send, send_sem, out_sem,
-    dx_own, dx_send, line_recv, cross_recv, turn_recv, dx_core_send, dx_core_recv,
+    left_any, right_any, tail, start, block, index, out, squares, left, right, loc, sent, rx_core,
+    rx_up, rx_down, rx_x, summed, ring, all_dx, load_sem, core_sem, recv_sem, recv_c, core_send,
+    send_sem, ring_sem, dx_own, dx_send, line_recv, cross_recv, turn_recv, dx_core_send,
+    dx_core_recv, ready,
 ):
     sec, dp, z, c, par, home = place()
     targets = hop_targets(sec, dp, c, par)
     classes = tree(z, c, home)
-    rx = dict(up=rx_up, down=rx_down, x=rx_x)
+    loads = [
+        pltpu.make_async_copy(left_any, left, load_sem.at[0]),
+        pltpu.make_async_copy(right_any, right, load_sem.at[1]),
+    ]
+    for one in loads:
+        one.start()
     del start
-
-    def base(k, lane):
-        if k == 4:
-            return 4 * 2 * HALF
-        return 2 * HALF * (2 * (k // 2) + lane) + HALF * (k % 2)
-
-    def held(k):
-        return k * HALF
-
-    def load(k):
-        rows = NCC * CC if k == 4 else HALF
-        return pltpu.make_async_copy(
-            grads.at[pl.ds(pl.multiple_of(base(k, c), 16), rows)],
-            loc.at[pl.ds(held(k), rows)],
-            load_sem.at[k],
-        )
-
-    for k in range(5):
-        load(k).start()
-    greet_neighbours(sec, dp, z, c, par, ((1, 2), (2, 0)))
-
-    def to_core(k, j, rows):
-        sem = core_c.at[j] if k == 4 else core_sem.at[k, j]
+    greet_neighbours(sec, dp, z, c, par, ((1, 2), (0, 2)))
+    pl.when(sec == 0)(
+        lambda: pl.semaphore_signal(ready, 1, device_id=(2, dp), device_id_type=MESH)
+    )
+    for one in loads:
+        one.wait()
+
+    def place_of(hop, k, j):
+        offset = j * ROWS[k]
+        if hop == "down":
+            base = (0, 0, 0, SPLIT, OWN)[k]
+        elif hop == "up":
+            base = (0, SPLIT, OWN, OWN, OWN + SPLIT)[k]
+        else:
+            base = HELD[k]
+        return pl.ds(pl.multiple_of(base + offset, 16), ROWS[k])
+
+    def gradient(first_row, size):
+        first_row = jnp.int32(first_row)
+        bounds = (D, 2 * D, 3 * D, 4 * D, 4 * D + 2 * FF)
+        matrix = functools.reduce(
+            jnp.add, [(first_row >= bound).astype(jnp.int32) for bound in bounds]
+        )
+        cols = pl.ds(pl.multiple_of(first_row, 128), size)
+        return tn(left[:, cols], right[matrix]).astype(BF16)
+
+    def core_copy(k, offset, rows, sem):
+        part = pl.ds(pl.multiple_of(HELD[k] + offset, 16), rows)
         return pltpu.make_async_remote_copy(
-            src_ref=grads.at[pl.ds(pl.multiple_of(base(k, 1 - c) + j * rows, 16), rows)],
-            dst_ref=rx_core.at[pl.ds(pl.multiple_of(held(k) + j * rows, 16), rows)],
-            send_sem=core_send.at[k],
+            src_ref=sent.at[part],
+            dst_ref=rx_core.at[part],
+            send_sem=core_send,
             recv_sem=sem,
             device_id=targets["core"],
             device_id_type=MESH,
         )
 
-    def start_core(j, carry):
-        for k in range(4):
-            to_core(k, j, CH).start()
-        pl.when(jnp.logical_and(j < NCC, c == 1))(lambda: to_core(4, j, CC).start())
-        return carry
-
-    lax.fori_loop(0, NCH, start_core, 0)
-    for k in range(5):
-        load(k).wait()
-
-    def onward(k, hop, j, rows):
+    def form(k, t):
+        there = pl.ds(pl.multiple_of(HELD[k] + 128 * t, 128), 128)
+        sent[there, :] = gradient(class_base(k, 1 - c) + 128 * t, 128)
+        core_copy(k, 128 * t, 128, core_sem.at[k, t]).start()
+        loc[there, :] = gradient(class_base(k, c) + 128 * t, 128)
+
+    last_rows = 11 * 48
+
+    def form_last(into):
+        for t in range(4):
+            into[pl.ds(HELD[4] + 128 * t, 128), :] = gradient(4 * OWN + 128 * t, 128)
+        into[pl.ds(HELD[4] + 512, 16), :] = tail[...]
+
+    def form_for_other():
+        form_last(sent)
+        core_copy(4, 0, last_rows, core_sem.at[4, 0]).start()
+
+    squares[...] = jnp.zeros_like(squares)
+
+    def count_squares(value):
+        folded = value * value
+        size = folded.shape[0]
+        while size > 8 and size % 16 == 0:
+            size //= 2
+            folded = folded[:size] + folded[size:]
+        for part in range(size // 8):
+            for n in range(D // 128):
+                squares[...] += folded[part * 8 : (part + 1) * 8, n * 128 : (n + 1) * 128]
+
+    rx = dict(up=rx_up, down=rx_down, x=rx_x)
+
+    def onward(k, hop, j):
         back = dict(up="down", down="up", x="x")[hop]
+        return landing(k, back, hop, j)
+
+    def landing(k, back, hop, j):
         index = ("up", "down", "x").index(back)
-        part = pl.ds(pl.multiple_of(held(k) + j * rows, 16), rows)
+        part = pl.ds(pl.multiple_of(HELD[k] + j * ROWS[k], 16), ROWS[k])
         return pltpu.make_async_remote_copy(
             src_ref=loc.at[part],
-            dst_ref=rx[back].at[part],
+            dst_ref=rx[back].at[place_of(back, k, j)],
             send_sem=send_sem.at[k],
             recv_sem=recv_c.at[index, j] if k == 4 else recv_sem.at[index, k, j],
             device_id=targets[hop],
             device_id_type=MESH,
         )
 
-    def landed(k, hop, j, rows):
-        index = ("up", "down", "x").index(hop)
-        part = pl.ds(pl.multiple_of(held(k) + j * rows, 16), rows)
-        return pltpu.make_async_remote_copy(
-            src_ref=loc.at[part],
-            dst_ref=rx[hop].at[part],
-            send_sem=send_sem.at[k],
-            recv_sem=recv_c.at[index, j] if k == 4 else recv_sem.at[index, k, j],
-            device_id=targets[hop],
-            device_id_type=MESH,
-        )
-
-    def write_out(k, j, rows):
-        offset = j * rows if k == 4 else HALF * (k % 2) + j * rows
-        part = pl.ds(pl.multiple_of(offset, 16), rows)
-        return pltpu.make_async_copy(total.at[part], out.at[part], out_sem)
-
-    def start_of(k, j, rows):
-        part = pl.ds(pl.multiple_of(held(k) + j * rows, 16), rows)
-        to_core(k, j, rows).wait_recv()
-        acc = summed.at[pl.ds(0, rows)]
+    def gathered(k, j):
+        part = pl.ds(pl.multiple_of(HELD[k] + j * ROWS[k], 16), ROWS[k])
+        if k == 4:
+            pl.when(j == 0)(lambda: core_copy(4, 0, last_rows, core_sem.at[4, 0]).wait_recv())
+        else:
+            pl.when(lax.rem(j, 2) == 0)(
+                lambda: core_copy(k, 64 * j, 128, core_sem.at[k, j // 2]).wait_recv()
+            )
+        acc = summed.at[pl.ds(0, ROWS[k])]
         acc[...] = loc[part, :].astype(F32) + rx_core[part, :].astype(F32)
-        return part, acc
-
-    def gathered(k, j, rows):
-        part, acc = start_of(k, j, rows)
         for hop in HOPS[:3]:
+            if (hop, k) in (("down", 0), ("down", 1)):
+                continue
 
             def add(hop=hop):
-                landed(k, hop, j, rows).wait_recv()
-                acc[...] += rx[hop][part, :].astype(F32)
+                landing(k, hop, hop, j).wait_recv()
+                acc[...] += rx[hop][place_of(hop, k, j), :].astype(F32)
 
             pl.when(classes[k][1][hop](j))(add)
         return part, acc
 
-    def pass_on(k, j, rows, part, acc):
+    def relay(k, j):
+        part, acc = gathered(k, j)
         loc[part, :] = acc[...].astype(BF16)
         for hop in HOPS[:3]:
-            pl.when(classes[k][2][hop](j))(lambda hop=hop: onward(k, hop, j, rows).start())
-
-    def relay(k, j, rows):
-        part, acc = gathered(k, j, rows)
-        pass_on(k, j, rows, part, acc)
-
-    def finish(k, j, rows):
-        _, acc = gathered(k, j, rows)
-        offset = j * rows if k == 4 else HALF * (k % 2) + j * rows
+            pl.when(classes[k][2][hop](j))(lambda hop=hop: onward(k, hop, j).start())
+
+    def write(slot, rows, offset):
+        return pltpu.make_async_copy(
+            ring.at[pl.ds(pl.multiple_of(slot * 64, 64), rows)],
+            out.at[pl.ds(pl.multiple_of(offset, 16), rows)],
+            ring_sem.at[slot],
+        )
+
+    def finish(k, j):
+        _, acc = gathered(k, j)
+        slot = 4 * (k % 2) + lax.rem(j, 4)
+        copy = write(slot, ROWS[k], SPLIT * (k % 2) + j * ROWS[k])
+        pl.when(j >= 4)(copy.wait)
         value = acc[...]
-        total[pl.ds(pl.multiple_of(offset, 16), rows), :] = value
-        write_out(k, j, rows).start()
+        ring[pl.ds(pl.multiple_of(slot * 64, 64), ROWS[k]), :] = value
+        copy.start()
         count_squares(value)
 
     first = sec == 0
@@ -779,6 +827,7 @@
 
     def own_second():
         turned.wait_recv()
+        pl.semaphore_wait(ready, 1)
         pass_own()
 
     pl.when(first)(own_first)
@@ -794,60 +843,59 @@
         aside(z + k)
 
     def tile(t):
-        there = pl.ds(pl.multiple_of(t * 128, 128), 128)
-        ids = lax.broadcasted_iota(jnp.int32, (128, 16 * SP), 0) + t * 128
+        ids = lax.broadcasted_iota(jnp.int32, (SP, 16 * SP), 0) + t * SP
         onehot = jnp.where(ids == index[...], 1.0, 0.0).astype(BF16)
         value = nn(onehot, all_dx[...]) * math.sqrt(D)
-        total[there, :] = value
-        pltpu.make_async_copy(total.at[there], out.at[there], out_sem).start()
+        slot = lax.rem(t, 2)
+        copy = write_tile(slot, t)
+        pl.when(t >= 2)(copy.wait)
+        ring[pl.ds(pl.multiple_of(slot * SP, 16), SP), :] = value
+        copy.start()
         count_squares(value)
 
+    def write_tile(slot, t):
+        return pltpu.make_async_copy(
+            ring.at[pl.ds(pl.multiple_of(slot * SP, 16), SP)],
+            out.at[pl.ds(pl.multiple_of(t * SP, 16), SP)],
+            ring_sem.at[slot],
+        )
+
     def collect(i):
-        pl.when(both(second, i == HOP))(own_second)
+        pl.when(both(second, i == CHOP + AHEAD))(own_second)
         for k in range(1, 4):
-            now = i == HOP * (k + p_line)
+            now = i == CHOP * (k + p_line) + AHEAD * p_line
             pl.when(both(now, z >= k))(lambda k=k: from_below(k))
             pl.when(both(now, z + k <= 3))(lambda k=k: from_above(k))
 
+    begin = 5 * CHOP + 1
+
     def embed(i):
-        pl.when(i == 2 * HOP)(lambda: crossed(z))
+        pl.when(i == 2 * CHOP)(lambda: crossed(z))
         for k in range(1, 4):
-            pl.when(both(i == HOP * (k + 2), z >= k))(lambda k=k: crossed(z - k))
-            pl.when(both(i == HOP * (k + 2), z + k <= 3))(lambda k=k: crossed(z + k))
-        begin = 5 * HOP + 1
+            pl.when(both(i == CHOP * (k + 2), z >= k))(lambda k=k: crossed(z - k))
+            pl.when(both(i == CHOP * (k + 2), z + k <= 3))(lambda k=k: crossed(z + k))
         pl.when(i == begin)(lambda: blocks(8, dx_core_send, dx_core_recv).wait_recv())
-        for half in range(2):
-            t = 2 * (i - begin) + half
-            pl.when(both(t >= 0, t < 17))(lambda t=t: tile(t))
-
-    squares[...] = jnp.zeros_like(squares)
-
-    def count_squares(value):
-        folded = value * value
-        size = folded.shape[0]
-        while size > 8 and size % 16 == 0:
-            size //= 2
-            folded = folded[:size] + folded[size:]
-        for part in range(size // 8):
-            squares[...] += folded[part * 8 : (part + 1) * 8]
+        t = i - begin
+        pl.when(both(t >= 0, t < OWN // SP))(lambda: tile(t))
 
     def step(i, carry):
+        for k in range(4):
+            pl.when(both(lax.rem(i, 2) == 0, i < COUNT[k]))(lambda k=k: form(k, i // 2))
+        pl.when(both(i == 1, c == 0))(lambda: form_last(loc))
+        pl.when(both(i == 1, c == 1))(form_for_other)
         for k in range(5):
-            count, rows = (NCC, CC) if k == 4 else (NCH, CH)
             source, _, _, depth = classes[k]
-            j = i - LAG * ((5, 5, 4, 4, 3)[k] - depth)
-            now = jnp.logical_and(j >= 0, j < count)
+            j = i - CLAG * ((5, 5, 4, 4, 3)[k] - depth) - (2 if k == 4 else 0)
+            now = both(j >= 0, j < COUNT[k])
             if k == 4:
-                now = jnp.logical_and(now, c == 0)
-            pl.when(jnp.logical_and(now, jnp.logical_not(source)))(
-                lambda k=k, j=j, rows=rows: relay(k, j, rows)
-            )
-            pl.when(jnp.logical_and(now, source))(lambda k=k, j=j, rows=rows: finish(k, j, rows))
+                now = both(now, c == 0)
+            pl.when(both(now, jnp.logical_not(source)))(lambda k=k, j=j: relay(k, j))
+            pl.when(both(now, source))(lambda k=k, j=j: finish(k, j))
         pl.when(in_line)(lambda: collect(i))
         pl.when(first)(lambda: embed(i))
         return carry
 
-    lax.fori_loop(0, max(NCH + 5 * LAG, 5 * HOP + 1 + 9), step, 0)
+    lax.fori_loop(0, max(18 + 5 * CLAG, begin + OWN // SP), step, 0)
     pl.when(first)(lambda: blocks(8, dx_core_send, dx_core_recv).wait_send())
 
     def dx_sent(count):
@@ -859,86 +907,98 @@
     pl.when(both(first, middle))(lambda: dx_sent(5))
     pl.when(both(second, ends))(lambda: dx_sent(5))
     pl.when(both(second, middle))(lambda: dx_sent(9))
+    def sent_core(rows):
+        part = pl.ds(0, rows)
+        pltpu.make_async_remote_copy(
+            src_ref=sent.at[part],
+            dst_ref=rx_core.at[part],
+            send_sem=core_send,
+            recv_sem=core_sem.at[4, 0],
+            device_id=targets["core"],
+            device_id_type=MESH,
+        ).wait_send()
+
+    pl.when(c == 0)(lambda: sent_core(2 * OWN))
+    pl.when(c == 1)(lambda: sent_core(LANE))
     for k in range(5):
-        rows = NCC * CC if k == 4 else HALF
-        source, _, parents, _ = classes[k]
-        whole = pl.ds(held(k), rows)
-        sent_core = pltpu.make_async_remote_copy(
-            src_ref=grads.at[pl.ds(0, rows)],
-            dst_ref=rx_core.at[whole],
-            send_sem=core_send.at[k],
-            recv_sem=core_c.at[0],
-            device_id=targets["core"],
-            device_id_type=MESH,
-        )
-        sent = pltpu.make_async_remote_copy(
-            src_ref=loc.at[whole],
-            dst_ref=rx_x.at[whole],
+        part = pl.ds(HELD[k], COUNT[k] * ROWS[k])
+        gone = pltpu.make_async_remote_copy(
+            src_ref=loc.at[part],
+            dst_ref=rx_x.at[part],
             send_sem=send_sem.at[k],
-            recv_sem=core_c.at[0],
+            recv_sem=core_sem.at[4, 0],
             device_id=targets["x"],
             device_id_type=MESH,
         )
-        if k == 4:
-            pl.when(c == 1)(sent_core.wait_send)
-            pl.when(jnp.logical_and(jnp.logical_not(source), c == 0))(sent.wait_send)
-        else:
-            sent_core.wait_send()
-            pl.when(jnp.logical_not(source))(sent.wait_send)
-    done_all = pltpu.make_async_copy(total, out, out_sem)
-    part = pl.ds(0, NCC * CC)
-    done_few = pltpu.make_async_copy(total.at[part], out.at[part], out_sem)
-    pl.when(jnp.logical_or(jnp.logical_and(home, z < 2), sec == 0))(done_all.wait)
-    pl.when(classes[4][0])(done_few.wait)
-
-
-def reduce_and_scatter(grads, start, block, index):
-    rows = LANE + NCC * CC
+        away = jnp.logical_not(classes[k][0])
+        pl.when(both(away, c == 0) if k == 4 else away)(gone.wait_send)
+
+    def drain_half(k):
+        for j in range(COUNT[k] - 4, COUNT[k]):
+            write(4 * (k % 2) + j % 4, ROWS[k], 0).wait()
+
+    def drain_tiles():
+        for slot in range(2):
+            write_tile(slot, 0).wait()
+
+    for k in range(5):
+        pl.when(classes[k][0])(lambda k=k: drain_half(k))
+    pl.when(first)(drain_tiles)
+
+
+def reduce_and_scatter(left, right, tail, start, block, index):
+    low = lambda *shape: pltpu.VMEM(shape, BF16)
+    dma = pltpu.SemaphoreType.DMA
     return pl.pallas_call(
         close_kernel,
         out_shape=(
-            jax.ShapeDtypeStruct((2 * HALF, D), F32),
-            jax.ShapeDtypeStruct((8, D), F32),
+            jax.ShapeDtypeStruct((OWN, D), F32),
+            jax.ShapeDtypeStruct((8, 128), F32),
         ),
-        in_specs=[ANY, ANY, VMEM, VMEM],
+        in_specs=[ANY, ANY, VMEM, ANY, VMEM, VMEM],
         out_specs=(ANY, VMEM),
-        input_output_aliases={1: 0},
-        scratch_shapes=[pltpu.VMEM((rows, D), BF16)] * 5
-        + [
-            pltpu.VMEM((2 * HALF, D), F32),
-            pltpu.VMEM((CH, D), F32),
-            pltpu.VMEM((16 * SP, D), BF16),
-            pltpu.SemaphoreType.DMA((5,)),
-            pltpu.SemaphoreType.DMA((4, NCH)),
-            pltpu.SemaphoreType.DMA((NCC,)),
-            pltpu.SemaphoreType.DMA((3, 4, NCH)),
-            pltpu.SemaphoreType.DMA((3, NCC)),
-            pltpu.SemaphoreType.DMA((5,)),
-            pltpu.SemaphoreType.DMA((5,)),
-            pltpu.SemaphoreType.DMA,
-            pltpu.SemaphoreType.DMA,
-            pltpu.SemaphoreType.DMA,
-            pltpu.SemaphoreType.DMA((4,)),
-            pltpu.SemaphoreType.DMA((4,)),
-            pltpu.SemaphoreType.DMA,
-            pltpu.SemaphoreType.DMA,
-            pltpu.SemaphoreType.DMA,
+        input_output_aliases={3: 0},
+        scratch_shapes=[
+            low(SP, MATS),
+            low(6, SP, D),
+            low(LANE, D),
+            low(LANE, D),
+            low(LANE, D),
+            low(OWN + SPLIT + 11 * 48, D),
+            low(OWN + 11 * 48, D),
+            low(LANE, D),
+            pltpu.VMEM((64, D), F32),
+            pltpu.VMEM((2 * SP, D), F32),
+            low(16 * SP, D),
+            dma((2,)),
+            dma((5, 9)),
+            dma((3, 4, 18)),
+            dma((3, 11)),
+            dma,
+            dma((5,)),
+            dma((8,)),
+            dma,
+            dma,
+            dma((4,)),
+            dma((4,)),
+            dma,
+            dma,
+            dma,
+            pltpu.SemaphoreType.REGULAR,
         ],
         compiler_params=pltpu.CompilerParams(
-            collective_id=1, has_side_effects=True, vmem_limit_bytes=60 * 2**20
+            collective_id=1, has_side_effects=True, vmem_limit_bytes=63 * 2**20
         ),
         name="reduce_and_scatter",
-    )(grads, start, block, index)
-
-
-def share_kernel(n_sec, n_dp, block, out, send_sem, recv_sem, own_sem):
+    )(left, right, tail, start, block, index)
+
+
+def norm_kernel(n_sec, n_dp, small, squares, out, block, every, send_sem, recv_sem):
     sec = lax.axis_index("section")
     dp = lax.axis_index("dp")
     n = n_sec * n_dp
     me = sec * n_dp + dp
     barrier = pltpu.get_barrier_semaphore()
-    own = pltpu.make_async_copy(block, out.at[me], own_sem)
-    own.start()
 
     def peer(k):
         other = lax.rem(me + k, n)
@@ -949,12 +1009,15 @@
         return carry
 
     lax.fori_loop(1, n, greet, 0)
+    block[...] = small[...]
+    block[7:8, :] += jnp.sum(squares[...], axis=0, keepdims=True)
+    every[me] = block[...]
     pl.semaphore_wait(barrier, n - 1)
 
     def send(k, carry):
         pltpu.make_async_remote_copy(
             src_ref=block,
-            dst_ref=out.at[me],
+            dst_ref=every.at[me],
             send_sem=send_sem,
             recv_sem=recv_sem,
             device_id=peer(k),
@@ -963,33 +1026,40 @@
         return carry
 
     lax.fori_loop(1, n, send, 0)
-    every = pltpu.make_async_remote_copy(
-        src_ref=out.at[pl.ds(0, n - 1)],
-        dst_ref=out.at[pl.ds(0, n - 1)],
+    others = pltpu.make_async_remote_copy(
+        src_ref=every.at[pl.ds(0, n - 1)],
+        dst_ref=every.at[pl.ds(0, n - 1)],
         send_sem=send_sem,
         recv_sem=recv_sem,
         device_id=peer(1),
         device_id_type=MESH,
     )
-    own.wait()
-    every.wait_send()
-    every.wait_recv()
-
-
-def share(block, n_sec, n_dp, cid, name):
+    others.wait_recv()
+    total = every[0]
+    for k in range(1, n):
+        total = total + every[k]
+    gains = jnp.sum(total[0:6] * total[0:6], axis=0, keepdims=True)
+    norm = jnp.sqrt(jnp.sum(gains + total[7:8], axis=1, keepdims=True))
+    out[0:8, :] = total
+    out[8:16, :] = jnp.broadcast_to(norm, (8, 128))
+    others.wait_send()
+
+
+def share_norm(small, squares, n_sec, n_dp):
     return pl.pallas_call(
-        functools.partial(share_kernel, n_sec, n_dp),
-        out_shape=jax.ShapeDtypeStruct((n_sec * n_dp,) + block.shape, block.dtype),
-        in_specs=[VMEM],
+        functools.partial(norm_kernel, n_sec, n_dp),
+        out_shape=jax.ShapeDtypeStruct((16, 128), F32),
+        in_specs=[VMEM, VMEM],
         out_specs=VMEM,
         scratch_shapes=[
-            pltpu.SemaphoreType.DMA,
+            pltpu.VMEM((8, 128), F32),
+            pltpu.VMEM((n_sec * n_dp, 8, 128), F32),
             pltpu.SemaphoreType.DMA,
             pltpu.SemaphoreType.DMA,
         ],
-        compiler_params=pltpu.CompilerParams(collective_id=cid, has_side_effects=True),
-        name=name,
-    )(block)
+        compiler_params=pltpu.CompilerParams(collective_id=8, has_side_effects=True),
+        name="share_norm",
+    )(small, squares)
 
 
 NEG = -1e30
@@ -1011,6 +1081,14 @@
     return jnp.where(allowed, 0.0, NEG)
 
 
+def hide(starts):
+    par = lax.rem(lax.axis_index("section"), 2)
+    rows = lax.broadcasted_iota(jnp.int32, (SP, SP), 0)
+    cols = lax.broadcasted_iota(jnp.int32, (SP, SP), 1)
+    same = segment_of(starts, par, rows)[0] == segment_of(starts, par, cols)[0]
+    return jnp.where(jnp.logical_and(same, rows <= cols), 0.0, NEG)
+
+
 def softmax_of(scores, unseen):
     masked = scores + unseen
     grown = jnp.exp(masked - jnp.max(masked, axis=-1, keepdims=True))
@@ -1027,9 +1105,14 @@
     ]
 
 
-def forward_kernel(
-    x, w_any, cosine, sine, starts, y, q, k, v, o, h, gate, up, w, m, unseen, sems
-):
+def forward_kernel(keep, x, w_any, cosine, sine, starts, y, *refs):
+    kept = refs[:7] if keep else ()
+    q, k, v, o, h, gate, up, w, m, unseen, sems, keep_sems = refs[len(kept) :]
+
+    def put(i):
+        if keep:
+            pltpu.make_async_copy((q, k, v, o, h, gate, up)[i], kept[i], keep_sems.at[i]).start()
+
     copies = weight_copies(w_any, w, sems)
     for i in (5, 0, 1, 2, 3, 4):
         copies[i].start()
@@ -1056,7 +1139,9 @@
             k[:, there] = turn(raw_k[:, here], cosine[...], sine[...], lanes).astype(BF16)
         return carry
 
-    lax.fori_loop(0, D // 256, project, 0)
+    lax.fori_loop(0, D // 256, project, 0, unroll=True)
+    for i in range(3):
+        put(i)
 
     def attend(b, carry):
         cols = pl.ds(pl.multiple_of(b * 128, 128), 128)
@@ -1067,11 +1152,13 @@
         o[:, cols] = jnp.where(first, nn(p0, vb), nn(p1, vb)).astype(BF16)
         return carry
 
-    lax.fori_loop(0, HEADS // 2, attend, 0)
+    lax.fori_loop(0, HEADS // 2, attend, 0, unroll=True)
+    put(3)
     copies[1].wait()
     for b in range(3):
         cols = pl.ds(b * 256, 256)
         h[:, cols] = x[:, cols].astype(F32) + nn(o[...], w[pl.ds(3 * D, D), cols])
+    put(4)
     a2 = rms_scale(h[...], gains[1:2]).astype(BF16)
     copies[2].wait()
     copies[3].wait()
@@ -1085,7 +1172,9 @@
         m[:, cols] = (g / (1.0 + jnp.exp(-g)) * u).astype(BF16)
         return carry
 
-    lax.fori_loop(0, FF // FT, widen, 0)
+    lax.fori_loop(0, FF // FT, widen, 0, unroll=True)
+    put(5)
+    put(6)
     copies[4].wait()
 
     def narrow(b, carry):
@@ -1093,25 +1182,32 @@
         y[:, cols] = (h[:, cols] + nn(m[...], w[pl.ds(4 * D + 2 * FF, FF), cols])).astype(BF16)
         return carry
 
-    lax.fori_loop(0, 3, narrow, 0)
-
-
-def forward_call(x, weights, cosine, sine, starts):
+    lax.fori_loop(0, 3, narrow, 0, unroll=True)
+    for i, part in enumerate(kept):
+        pltpu.make_async_copy((q, k, v, o, h, gate, up)[i], part, keep_sems.at[i]).wait()
+
+
+KEPT = ((D, BF16), (D, BF16), (D, BF16), (D, BF16), (D, F32), (FF, F32), (FF, F32))
+
+
+def forward_call(keep, x, weights, cosine, sine, starts):
     low = jax.ShapeDtypeStruct((SP, D), BF16)
-    wide = jax.ShapeDtypeStruct((SP, FF), F32)
+    kept = tuple(jax.ShapeDtypeStruct((SP, n), t) for n, t in KEPT) if keep else ()
     return pl.pallas_call(
-        forward_kernel,
-        out_shape=(low, low, low, low, low, jax.ShapeDtypeStruct((SP, D), F32), wide, wide),
+        functools.partial(forward_kernel, keep),
+        out_shape=(low,) + kept,
         in_specs=[VMEM, ANY, VMEM, VMEM, SMEM],
-        out_specs=(VMEM,) * 8,
-        scratch_shapes=[
+        out_specs=(VMEM,) + (ANY,) * len(kept),
+        scratch_shapes=[pltpu.VMEM((SP, n), t) for n, t in KEPT]
+        + [
             pltpu.VMEM((WROWS, D), BF16),
             pltpu.VMEM((SP, FF), BF16),
             pltpu.VMEM((SP, SP), F32),
             pltpu.SemaphoreType.DMA((6,)),
+            pltpu.SemaphoreType.DMA((7,)),
         ],
-        compiler_params=pltpu.CompilerParams(vmem_limit_bytes=48 * 2**20),
-        name="layer_forward",
+        compiler_params=pltpu.CompilerParams(vmem_limit_bytes=56 * 2**20),
+        name="layer_forward_kept" if keep else "layer_forward",
     )(x, weights, cosine, sine, starts)
 
 
@@ -1123,20 +1219,33 @@
     return grad_in, jnp.sum(grad * unit, axis=0, keepdims=True)
 
 
-def backward_kernel(
-    with_weights, dy, x, w_any, cosine, sine, starts, q, k, v, o, h, gate, up, *refs
-):
-    if with_weights:
-        dx, grads, w, dgate, dup, m, da, do, dq, dk, dv, unseen, sems = refs
-    else:
-        dx, w, dgate, dup, m, da, do, dq, dk, dv, unseen, sems = refs
+def backward_kernel(dy, x, w_any, cosine, sine, starts, *refs):
+    kept, refs = refs[:7], refs[7:]
+    dx, left, right, tail, refs = *refs[:4], refs[4:]
+    q, k, v, o, h, gate, up, w, dgate, dup, m, da, do, dq, dk, dv, a1, a2, db, *refs = refs
+    unseen, sems, keep_sems, out_sems = refs
+    outs = []
+
+    def put(source, target):
+        copy = pltpu.make_async_copy(source, target, out_sems.at[len(outs)])
+        copy.start()
+        outs.append(copy)
     copies = weight_copies(w_any, w, sems)
-    for i in (4, 5, 2, 3, 1, 0):
-        copies[i].start()
-    unseen[...] = see(starts)
+    taken = [
+        pltpu.make_async_copy(part, (q, k, v, o, h, gate, up)[i], keep_sems.at[i])
+        for i, part in enumerate(kept)
+    ]
+    for one in (
+        copies[4], taken[5], taken[6], copies[5], copies[2], copies[3], taken[4], copies[1],
+        taken[0], taken[1], taken[2], copies[0], taken[3],
+    ):
+        one.start()
+    unseen[...] = hide(starts)
     lanes = lax.broadcasted_iota(jnp.int32, (SP, 128), 1)
     first = lanes < 64
     copies[4].wait()
+    taken[5].wait()
+    taken[6].wait()
 
     def open_mlp(b, carry):
         cols = pl.ds(pl.multiple_of(b * FT, FT), FT)
@@ -1146,11 +1255,13 @@
         sig = 1.0 / (1.0 + jnp.exp(-g))
         dgate[:, cols] = (dm * u * sig * (1.0 + g * (1.0 - sig))).astype(BF16)
         dup[:, cols] = (dm * g * sig).astype(BF16)
-        if with_weights:
-            m[:, cols] = (g * sig * u).astype(BF16)
+        m[:, cols] = (g * sig * u).astype(BF16)
         return carry
 
-    lax.fori_loop(0, FF // FT, open_mlp, 0)
+    lax.fori_loop(0, FF // FT, open_mlp, 0, unroll=True)
+    for i, part in enumerate((dgate, dup, m)):
+        put(part, left.at[:, pl.ds(4 * D + i * FF, FF)])
+    put(dy, right.at[5])
     copies[5].wait()
     gains = w[pl.ds(MATS, 16), :].astype(F32)
     copies[2].wait()
@@ -1163,13 +1274,20 @@
         )
         return carry
 
-    lax.fori_loop(0, 3, close_mlp, 0)
+    lax.fori_loop(0, 3, close_mlp, 0, unroll=True)
+    taken[4].wait()
     dh, dg_mlp = rms_back(h[...], gains[1:2], da[...])
     dh = dh + dy[...].astype(F32)
-    db = dh.astype(BF16)
+    db[...] = dh.astype(BF16)
+    a2[...] = rms_scale(h[...], gains[1:2]).astype(BF16)
+    put(db, right.at[3])
+    put(a2, right.at[4])
     copies[1].wait()
     for b in range(3):
-        do[:, pl.ds(b * 256, 256)] = nt(db, w[pl.ds(3 * D + b * 256, 256), :]).astype(BF16)
+        do[:, pl.ds(b * 256, 256)] = nt(db[...], w[pl.ds(3 * D + b * 256, 256), :]).astype(BF16)
+
+    for i in range(3):
+        taken[i].wait()
 
     def attend(b, carry):
         cols = pl.ds(pl.multiple_of(b * 128, 128), 128)
@@ -1178,11 +1296,13 @@
         parts = []
         for head in range(2):
             keep = first if head == 0 else jnp.logical_not(first)
-            probs = softmax_of(nt(jnp.where(keep, qb, zero), kb), unseen[...])
-            dprobs = nt(jnp.where(keep, dob, zero), vb)
-            along = jnp.sum(probs * dprobs, axis=-1, keepdims=True)
+            masked = nt(jnp.where(keep, kb, zero), qb) + unseen[...]
+            grown = jnp.exp(masked - jnp.max(masked, axis=0, keepdims=True))
+            probs = grown / jnp.sum(grown, axis=0, keepdims=True)
+            dprobs = nt(jnp.where(keep, vb, zero), dob)
+            along = jnp.sum(probs * dprobs, axis=0, keepdims=True)
             dscores = (probs * (dprobs - along)).astype(BF16)
-            parts.append((nn(dscores, kb), tn(dscores, qb), tn(probs.astype(BF16), dob)))
+            parts.append((tn(dscores, kb), nn(dscores, qb), nn(probs.astype(BF16), dob)))
         dqb = jnp.where(first, parts[0][0], parts[1][0]) * HD ** (-0.5)
         dkb = jnp.where(first, parts[0][1], parts[1][1])
         dq[:, cols] = turn(dqb, cosine[...], -sine[...], lanes).astype(BF16)
@@ -1190,7 +1310,9 @@
         dv[:, cols] = jnp.where(first, parts[0][2], parts[1][2]).astype(BF16)
         return carry
 
-    lax.fori_loop(0, HEADS // 2, attend, 0)
+    lax.fori_loop(0, HEADS // 2, attend, 0, unroll=True)
+    for i, part in enumerate((dq, dk, dv)):
+        put(part, right.at[i])
     copies[0].wait()
     for b in range(3):
         rows = lambda i, b=b: w[pl.ds(i * D + b * 256, 256), :]
@@ -1198,60 +1320,59 @@
             nt(dq[...], rows(0)) + nt(dk[...], rows(1)) + nt(dv[...], rows(2))
         )
     stream = x[...].astype(F32)
+    a1[...] = rms_scale(stream, gains[0:1]).astype(BF16)
+    for i in range(3):
+        put(a1, left.at[:, pl.ds(i * D, D)])
+    taken[3].wait()
+    put(o, left.at[:, pl.ds(3 * D, D)])
     dstream, dg_attn = rms_back(stream, gains[0:1], da[...])
     dx[...] = (dstream + dh).astype(BF16)
-    if not with_weights:
-        return
-    a1 = rms_scale(stream, gains[0:1]).astype(BF16)
-    a2 = rms_scale(h[...], gains[1:2]).astype(BF16)
-    for b in range(3):
-        cols = slice(b * 256, (b + 1) * 256)
-        piece = a1[:, cols]
-        for i, right in enumerate((dq, dk, dv)):
-            grads[pl.ds(i * D + b * 256, 256), :] = tn(piece, right[...]).astype(BF16)
-        grads[pl.ds(3 * D + b * 256, 256), :] = tn(o[:, cols], db).astype(BF16)
-
-    def outer(b, carry):
-        cols = pl.ds(pl.multiple_of(b * FT, FT), FT)
-        base = 4 * D + b * FT
-        for i, (left, right) in enumerate(((dgate, a2), (dup, a2), (m, dy))):
-            there = pl.ds(pl.multiple_of(base + i * FF, FT), FT)
-            grads[there, :] = tn(left[:, cols], right[...]).astype(BF16)
-        return carry
-
-    lax.fori_loop(0, FF // FT, outer, 0)
-    tail = lax.broadcasted_iota(jnp.int32, (16, D), 0)
-    grads[pl.ds(MATS, 16), :] = jnp.where(
-        tail == 0, dg_attn, jnp.where(tail == 1, dg_mlp, 0.0)
-    ).astype(BF16)
-
-
-def backward_call(with_weights, dy, x, weights, cosine, sine, starts, kept):
-    low = jax.ShapeDtypeStruct((SP, D), BF16)
-    out_shape = (low, jax.ShapeDtypeStruct((WROWS, D), BF16)) if with_weights else low
+    ids = lax.broadcasted_iota(jnp.int32, (16, D), 0)
+    tail[...] = jnp.where(ids == 0, dg_attn, jnp.where(ids == 1, dg_mlp, 0.0)).astype(BF16)
+    for copy in outs:
+        copy.wait()
+
+
+def backward_call(dy, x, weights, cosine, sine, starts, kept):
     wide = pltpu.VMEM((SP, FF), BF16)
     narrow = pltpu.VMEM((SP, D), BF16)
     return pl.pallas_call(
-        functools.partial(backward_kernel, with_weights),
-        out_shape=out_shape,
-        in_specs=[VMEM, VMEM, ANY, VMEM, VMEM, SMEM] + [VMEM] * 7,
-        out_specs=(VMEM, VMEM) if with_weights else VMEM,
-        scratch_shapes=[
+        backward_kernel,
+        out_shape=(
+            jax.ShapeDtypeStruct((SP, D), BF16),
+            jax.ShapeDtypeStruct((SP, MATS), BF16),
+            jax.ShapeDtypeStruct((6, SP, D), BF16),
+            jax.ShapeDtypeStruct((16, D), BF16),
+        ),
+        in_specs=[VMEM, VMEM, ANY, VMEM, VMEM, SMEM] + [ANY] * 7,
+        out_specs=(VMEM, ANY, ANY, VMEM),
+        scratch_shapes=[pltpu.VMEM((SP, n), t) for n, t in KEPT]
+        + [
             pltpu.VMEM((WROWS, D), BF16),
             wide,
             wide,
             wide,
             pltpu.VMEM((SP, D), F32),
-            narrow,
-            narrow,
-            narrow,
-            narrow,
+        ]
+        + [narrow] * 7
+        + [
             pltpu.VMEM((SP, SP), F32),
             pltpu.SemaphoreType.DMA((6,)),
+            pltpu.SemaphoreType.DMA((7,)),
+            pltpu.SemaphoreType.DMA((13,)),
         ],
         compiler_params=pltpu.CompilerParams(vmem_limit_bytes=60 * 2**20),
-        name="layer_backward_weights" if with_weights else "layer_backward",
+        name="layer_backward",
     )(dy, x, weights, cosine, sine, starts, *kept)
+
+
+def matrix_gradients(left, right, tail):
+    parts = [(0, 0), (D, 1), (2 * D, 2), (3 * D, 3), (4 * D, 4), (4 * D + FF, 4), (4 * D + 2 * FF, 5)]
+    ends = [start for start, _ in parts[1:]] + [MATS]
+    rows = [
+        tn(left[:, start:end], right[i]).astype(BF16) for (start, i), end in zip(parts, ends)
+    ]
+    return jnp.concatenate(rows + [tail], axis=0)
 
 
 HEAD_T = 256
@@ -1394,7 +1515,7 @@
     pl.when(sec == 2)(pick_second)
     pl.when(last)(pick_third)
     g_f = gain[...].astype(F32)[0:1]
-    own = 2 * HALF
+    own = OWN
     tiles = [(t * HEAD_T, HEAD_T) for t in range(own // HEAD_T)] + [
         (own - own % HEAD_T, own % HEAD_T)
     ]
@@ -1584,7 +1705,7 @@
         head_kernel,
         out_shape=(
             jax.ShapeDtypeStruct((SP, D), BF16),
-            jax.ShapeDtypeStruct((2 * HALF, D), F32),
+            jax.ShapeDtypeStruct((OWN, D), F32),
             jax.ShapeDtypeStruct((8, 128), F32),
         ),
         in_specs=[VMEM] * 5,
@@ -1593,8 +1714,8 @@
             low(PICKS, D),
             low(n, D),
             low(n, D),
-            wide(n, 2 * HALF),
-            low(n, 2 * HALF),
+            wide(n, OWN),
+            low(n, OWN),
             pltpu.VMEM((n, 1), jnp.int32),
             wide(n, 1),
             wide(16, 128),
@@ -1603,7 +1724,7 @@
             wide(8 * PICKS, D),
             low(8 * PICKS, D),
             low(4, PICKS, D),
-            wide(2 * HALF, D),
+            wide(OWN, D),
             pltpu.SemaphoreType.DMA,
             pltpu.SemaphoreType.DMA,
             pltpu.SemaphoreType.DMA,
@@ -1701,26 +1822,26 @@
     own = master.shape[0]
     learn_rate = rate_factor * math.sqrt(own * n_sec * n_dp)
     beside = [(0, 1), (1, 0), (2, 3), (3, 2)]
-    fast = n_sec == 4 and n_dp == 8 and own == 2 * HALF
-    table = master.astype(BF16)
+    fast = n_sec == 4 and n_dp == 8 and own == OWN
     gain_at = VOCAB // own
     frequency = rope_base ** (-jnp.arange(HD // 2, dtype=F32) * 2.0 / HD)
 
     if fast:
         wide = jnp.tile(frequency[None, :], (1, 4))
-        weights, x0, info, gain, cosine, sine = gather_and_embed(
-            table, codes, labels, picks, starts, classes, null_mask, wide
+        weights, x0, info, gain, cosine, sine, table = gather_and_embed(
+            master, codes, labels, picks, starts, classes, null_mask, wide
         )
         all_index = info[:, :2, :SP].reshape(-1)
         local = jnp.where(sec == 0, all_index, -1) - d * own
     else:
+        table = master.astype(BF16)
         opened = open_anywhere(codes, labels, picks, classes, null_mask, starts, table, frequency)
         weights, x0, local, all_labels, all_counts, g_f, cosine, sine = opened
     around = (cosine, sine, starts)
 
-    y0 = forward_call(x0, weights, *around)[0]
+    y0 = forward_call(False, x0, weights, *around)[0]
     x = jnp.where(sec < 2, x0, lax.ppermute(y0, "section", [(0, 2), (1, 3)]))
-    y, *kept = forward_call(x, weights, *around)
+    y, *kept = forward_call(True, x, weights, *around)
 
     if fast:
         d_top, d_table, small = head_call(y, picks, info, gain, table)
@@ -1729,18 +1850,19 @@
             y, picks[par], all_labels, all_counts, g_f, table
         )
 
-    dx1 = backward_call(False, d_top, x, weights, *around, kept)
-    dy = jnp.where(sec < 2, lax.ppermute(dx1, "section", [(2, 0), (3, 1)]), d_top)
-    dx0, grads = backward_call(True, dy, x, weights, *around, kept)
+    once = backward_call(d_top, x, weights, *around, kept)
+    dy = lax.ppermute(once[0], "section", [(2, 0), (3, 1)])
+    dx0, left, right, tail = lax.cond(
+        sec < 2, lambda: tuple(backward_call(dy, x, weights, *around, kept)), lambda: tuple(once)
+    )
 
     if fast:
-        grad, squares = reduce_and_scatter(grads, d_table, dx0, local[None, :])
-        squares = squares.reshape(-1, 6, 128).sum(axis=(0, 1))
-        small = small + jnp.where(jnp.arange(8)[:, None] == 7, squares[None, :], 0.0)
-        totals = jnp.sum(share(small, n_sec, n_dp, 8, "share_norm"), axis=0)
-        dg_f, loss_sum, squares = totals[:6].reshape(-1), totals[6, 0], jnp.sum(totals[7])
+        grad, squares = reduce_and_scatter(left, right, tail, d_table, dx0, local[None, :])
+        totals = share_norm(small, squares, n_sec, n_dp)
+        dg_f, loss_sum, grad_norm = totals[:6].reshape(-1), totals[6, 0], totals[8, 0]
         count_sum = jnp.sum(info[:, 4:6, :PICKS].astype(F32))
     else:
+        grads = matrix_gradients(left, right, tail)
         grads = grads.astype(F32) + lax.ppermute(grads, "section", beside).astype(F32)
         grads = jnp.pad(grads.astype(BF16), ((0, own * n_dp - WROWS), (0, 0)))
         grad = lax.psum_scatter(grads, "dp", scatter_dimension=0, tiled=True).astype(F32)
@@ -1752,7 +1874,7 @@
         totals = (dg_f, jnp.sum(grad * grad), loss_part)
         dg_f, squares, loss_sum = lax.psum(totals, ("section", "dp"))
         count_sum = jnp.sum(all_counts)
-    grad_norm = jnp.sqrt(squares + jnp.sum(dg_f * dg_f))
+        grad_norm = jnp.sqrt(squares + jnp.sum(dg_f * dg_f))
     gain_here = (jnp.arange(own) == VOCAB % own)[:, None] & (sec == 3) & (d == gain_at)
     grad = grad + jnp.where(gain_here, dg_f[None, :], 0.0)
     clipped = grad * jnp.minimum(1.0, clip_limit / (grad_norm + norm_eps))

time: 476 us -> 434 us (0.912); the launches traced: 476 us -> 429 us
  Pallas kernels: 363 us -> 333 us
  other arithmetic: 28.4 us -> 19.1 us
  local copies, waits for them, and re-layouts: 10.7 us -> 3.22 us
    pallas_call x6, Pallas kernels: 230 us -> 203 us  [the longest x1 121 us: reduce_and_scatter(): pl.pallas_call(close_kernel, out_shape=(jax.ShapeDtypeStruct((OWN, D), F3...]
    unnamed x34 -> x12, local copies, waits for them, and re-layouts: 8.92 us -> 0.03 us
    convert_element_type x1 -> x0, other arithmetic: 4.96 us -> none  [shards(): table = master.astype(BF16)]
where the time goes in v3:
time: 434 us; the launch traced here: 429 us
  Pallas kernels  333 us (77%)
  waiting for transfers between devices  68.2 us (16%)
  other arithmetic  19.1 us (4%)
    pallas_call x1, Pallas kernels, gather_and_embed(): pl.pallas_call(open_kernel, out_shape=(jax.ShapeDtypeStruct((WROWS, D), B...  124 us
    pallas_call x1, Pallas kernels, reduce_and_scatter(): pl.pallas_call(close_kernel, out_shape=(jax.ShapeDtypeStruct((OWN, D), F3...  121 us
    ppermute x1, waiting for transfers between devices, shards(): dy = lax.ppermute(once[0], 'section', [(2, 0), (3, 1)])  58.7 us
    pallas_call x2, Pallas kernels, backward_call(): pl.pallas_call(backward_kernel, out_shape=(jax.ShapeDtypeStruct((SP, D),...  42.9 us
    pallas_call x2, Pallas kernels, forward_call(): pl.pallas_call(functools.partial(forward_kernel, keep), out_shape=(low,)...  26.2 us
    add x1, other arithmetic, shards(): new_average = average_decay * average + (1.0 - average_decay) * new_master  16.7 us
    pallas_call x1, Pallas kernels, share_norm(): pl.pallas_call(functools.partial(norm_kernel, n_sec, n_dp), out_shape=jax...  12.7 us
    ppermute x1, waiting for transfers between devices, shards(): x = jnp.where(sec < 2, x0, lax.ppermute(y0, 'section', [(0, 2), (1, 3)]))  9.55 us
  transfers between devices with their start and end apart: 2, of which 2 were waited for; matrix products, arithmetic and copies ran while one was open for 1% of the time, Pallas kernels for 0%

profile of v3, /device:TPU:0, one launch (start us, length us, event | category | flops | bytes accessed | tf_op | source)
XLA Modules:
  0.0 429.0 jit_solution(2658592946348651558)
XLA Ops:
  0.6 0.0 copy-start.5
  0.7 0.6 tile.9.frequency
  1.3 124.2 %gather_and_embed.1 = (bf16[9232,768]{1,0:T(8,128)(2,1)}, bf16[272,768]{1,0:T(8,128)(2,1)}, s32[8,8,384]{2,1,0:T(8,128)}, bf16[16,768]{1,0:T(8,128)(2,1)}, f32[2...) custom-call(f32[2176,768]{1,0:T(8,128)} %master.1, s32[2,264]{1,0:T(2,128)} %codes.1, ...), custom_call_target="tpu_custom_call" | custom-call | tf_op jit(solution)/shard_map/gather_and_embed/pallas_call | solution.py:572
  125.5 12.9 %layer_forward.1 = bf16[272,768]{1,0:T(8,128)(2,1)} custom-call(bf16[272,768]{1,0:T(8,128)(2,1)} %get-tuple-element.78.x, bf16[9232,768]{1,0:T(8,128)(2,1)} %get-tuple-element.79.w_any, f32[272,128]{1,0:T(8,128)S(1)} %get-tuple-element.80.cosine, f32[272,128]{1,0:T(8,128)S(1)} %get-tuple-element.81.sine, s32[2,4]{1,0:T(2,128)S(1)} %copy-done.5), custom_call_target="tpu_custom_call" | custom-call | tf_op jit(solution)/shard_map/layer_forward/pallas_call | solution.py:1196
  138.5 1.7 collective-permute-start
  140.2 9.5 %collective-permute-done = bf16[272,768]{1,0:T(8,128)(2,1)S(1)} collective-permute-done((bf16[272,768]{1,0:T(8,128)(2,1)}, bf16[272,768]{1,0:T(8,128)(2,1)S(1)}, u32[]{:S(2)}, u32[]{:S(2)}) %collective-permute-start) | collective-permute-done | bytes 417824 | tf_op jit(solution)/shard_map/ppermute | solution.py:1843
  149.8 0.0 copy-done.4
  149.8 0.1 broadcast_select_fusion.x
  149.8 13.3 %layer_forward_kept.1 = (bf16[272,768]{1,0:T(8,128)(2,1)}, bf16[272,768]{1,0:T(8,128)(2,1)}, bf16[272,768]{1,0:T(8,128)(2,1)}, bf16[272,768]{1,0:T(8,128)(2,1)},...) custom-call(bf16[272,768]{1,0:T(8,128)(2,1)S(1)} %broadcast_select_fusion.x, ...), custom_call_target="tpu_custom_call" | custom-call | tf_op jit(solution)/shard_map/layer_forward_kept/pallas_call | solution.py:1196
  163.2 6.2 %head.1 = (bf16[272,768]{1,0:T(8,128)(2,1)}, f32[2176,768]{1,0:T(8,128)}, f32[8,128]{1,0:T(8,128)}) custom-call(bf16[272,768]{1,0:T(8,128)(2,1)} %get-tuple-element.82.y, s32[2,32]{1,0:T(2,128)} %picks.3, s32[8,8,384]{2,1,0:T(8,128)} %get-tuple-element.83.info, bf16[16,768]{1,0:T(8,128)(2,1)} %get-tuple-element.84.gain, ...), custom_call_target="tpu_custom_call" | custom-call | tf_op jit(solution)/shard_map/head/pallas_call | solution.py:1704
  169.4 0.0 copy-done.1
  169.4 21.4 %layer_backward.3 = (bf16[272,768]{1,0:T(8,128)(2,1)}, bf16[272,9216]{1,0:T(8,128)(2,1)}, bf16[6,272,768]{2,1,0:T(8,128)(2,1)}, bf16[16,768]{1,0:T(8,128)(2,1)S(1)}) custom-call(bf16[272,768]{1,0:T(8,128)(2,1)} %get-tuple-element.87.dy, bf16[272,768]{1,0:T(8,128)(2,1)S(1)} %broadcast_select_fusion.x, bf16[9232,768]{1,0:T(8,128)(2,1)} %get-tuple-element.79.w_any, ...), custom_call_target="tpu_custom_call" | custom-call | tf_op jit(solution)/shard_map/layer_backward/pallas_call | solution.py:1339
  190.8 1.3 collective-permute-start.1
  192.1 0.9 select_subtract_fusion
  193.0 0.7 sub.21.index
  193.8 1.4 convert_reduce_fusion
  195.1 58.7 %collective-permute-done.1 = bf16[272,768]{1,0:T(8,128)(2,1)} collective-permute-done((bf16[272,768]{1,0:T(8,128)(2,1)}, bf16[272,768]{1,0:T(8,128)(2,1)}, u32[]{:S(2)}, u32[]{:S(2)}) %collective-permute-start.1) | collective-permute-done | bytes 417824 | tf_op jit(solution)/shard_map/ppermute | solution.py:1854
  253.8 21.8 %conditional.1 = ((bf16[272,768]{1,0:T(8,128)(2,1)}, bf16[272,9216]{1,0:T(8,128)(2,1)}, bf16[6,272,768]{2,1,0:T(8,128)(2,1)}, bf16[16,768]{1,0:T(8,128)(2,1)S(1)})) conditional(s32[]{:T(128)} %convert_element_type.6, (bf16[272,768]{1,0:T(8,128)(2,1)}, bf16[272,9216]{1,0:T(8,128)(2,1)}, bf16[6,272,768]{2,1,0:T(8,128)(2,1)}, ...), branch_computations={%region_0.1_spmd, %region_1.2_spmd} | conditional | bytes 8 | solution.py:1855
  253.8 21.5 %layer_backward.2 = (bf16[272,768]{1,0:T(8,128)(2,1)}, bf16[272,9216]{1,0:T(8,128)(2,1)}, bf16[6,272,768]{2,1,0:T(8,128)(2,1)}, bf16[16,768]{1,0:T(8,128)(2,1)S(1)}) custom-call(bf16[272,768]{1,0:T(8,128)(2,1)} %get-tuple-element.34.dy, bf16[272,768]{1,0:T(8,128)(2,1)S(1)} %get-tuple-element.35.x, bf16[9232,768]{1,0:T(8,128)(2,1)} %get-tuple-element.36.w_any, ...), custom_call_target="tpu_custom_call" | custom-call | tf_op jit(solution)/shard_map/cond/branch_1_fun/layer_backward/pallas_call | solution.py:1339
  275.6 120.9 %reduce_and_scatter.1 = (f32[2176,768]{1,0:T(8,128)}, f32[8,128]{1,0:T(8,128)}) custom-call(bf16[272,9216]{1,0:T(8,128)(2,1)} %get-tuple-element.96.left_any, bf16[6,272,768]{2,1,0:T(8,128)(2,1)} %get-tuple-element.97.right_any, bf16[16,768]{1,0:T(8,128)(2,1)S(1)} %get-tuple-element.98.tail, ...), custom_call_target="tpu_custom_call", output_to_operand_aliasing={{0}: (3, {})} | custom-call | tf_op jit(solution)/shard_map/reduce_and_scatter/pallas_call | solution.py:952
  396.5 12.7 %share_norm.1 = f32[16,128]{1,0:T(8,128)} custom-call(f32[8,128]{1,0:T(8,128)} %get-tuple-element.86.small, f32[8,128]{1,0:T(8,128)} %get-tuple-element.101.squares), custom_call_target="tpu_custom_call" | custom-call | tf_op jit(solution)/shard_map/share_norm/pallas_call | solution.py:1049
  409.2 1.2 fusion.2
  410.4 0.7 slice_bitcast_fusion
  411.8 16.7 %multiply_add_fusion = (f32[2176,768]{1,0:T(8,128)}, f32[2176,768]{1,0:T(8,128)}, f32[2176,768]{1,0:T(8,128)}) fusion(f32[2176,768]{1,0:T(8,128)} %param.19, f32[2176,768]{1,0:T(8,128)} %master.1, f32[]{:T(128)S(6)} %min.3, f32[2176,768]{1,0:T(8,128)} %get-tuple-element.102, f32[768]{0:T(1024)S(1)} %slice_bitcast_fusion, pred[2176]{0:T(1024)(128)(4,1)S(1)} %fusion.1, ...), kind=kLoop, calls=%fused_computation | loop fusion | flops 20054016 | bytes 46797956 | tf_op jit(solution)/shard_map/add | solution.py:1883
  (12 shorter events, 0.0 us)
Async XLA Ops:
  0.6 124.9 %copy-start.5 = (s32[2,4]{1,0:T(2,128)S(1)}, s32[2,4]{1,0:T(2,128)}, u32[]{:S(2)}) copy-start(s32[2,4]{1,0:T(2,128)} %starts.7) | copy-start | bytes 100
  125.5 12.9 %copy-start = (f32[272,128]{1,0:T(8,128)}, f32[272,128]{1,0:T(8,128)S(1)}, u32[]{:S(2)}) copy-start(f32[272,128]{1,0:T(8,128)S(1)} %get-tuple-element.80.cosine) | copy-start | bytes 417796
  125.5 12.9 %copy-start.2 = (f32[272,128]{1,0:T(8,128)}, f32[272,128]{1,0:T(8,128)S(1)}, u32[]{:S(2)}) copy-start(f32[272,128]{1,0:T(8,128)S(1)} %get-tuple-element.81.sine) | copy-start | bytes 417796
  125.5 24.2 %copy-start.4 = (bf16[272,768]{1,0:T(8,128)(2,1)S(1)}, bf16[272,768]{1,0:T(8,128)(2,1)}, u32[]{:S(2)}) copy-start(bf16[272,768]{1,0:T(8,128)(2,1)} %get-tuple-element.78.x) | copy-start | bytes 1253380
  138.5 11.3 %collective-permute-start = (bf16[272,768]{1,0:T(8,128)(2,1)}, bf16[272,768]{1,0:T(8,128)(2,1)S(1)}, u32[]{:S(2)}, u32[]{:S(2)}) collective-permute-start(bf16[272,768]{1,0:T(8,128)(2,1)} %layer_forward.1), channel_id=1, source_target_pairs={{0,16},{8,24},{1,17},{9,25},{2,18},{10,26},{3,19},{11,27},{4,20},{... | collective-permute-start | bytes 1253384 | tf_op jit(solution)/shard_map/ppermute | solution.py:1843
  149.8 19.6 %copy-start.1 = (f32[272,128]{1,0:T(8,128)S(1)}, f32[272,128]{1,0:T(8,128)}, u32[]{:S(2)}) copy-start(f32[272,128]{1,0:T(8,128)} %copy-done) | copy-start | bytes 417796
  149.8 19.6 %copy-start.3 = (f32[272,128]{1,0:T(8,128)S(1)}, f32[272,128]{1,0:T(8,128)}, u32[]{:S(2)}) copy-start(f32[272,128]{1,0:T(8,128)} %copy-done.2) | copy-start | bytes 417796
  190.8 63.0 %collective-permute-start.1 = (bf16[272,768]{1,0:T(8,128)(2,1)}, bf16[272,768]{1,0:T(8,128)(2,1)}, u32[]{:S(2)}, u32[]{:S(2)}) collective-permute-start(bf16[272,768]{1,0:T(8,128)(2,1)} %get-tuple-element.95), channel_id=1, source_target_pairs={{16,0},{24,8},{17,1},{25,9},{18,2},{26,10},{19,3},{27,11},{20,4},{... | collective-permute-start | bytes 1253384 | tf_op jit(solution)/shard_map/ppermute | solution.py:1854

commit v4 on v3

--- a/solution.py
+++ b/solution.py
@@ -88,6 +88,9 @@
 COUNT = (18, 16, 18, 16, 11)
 ROWS = (64, 64, 64, 64, 48)
 HELD = (0, SPLIT, OWN, OWN + SPLIT, 2 * OWN)
+LARGE = (16, 14, 16, 14, 11)
+SMALL = 4
+SMALL_ROWS = 32
 LANE = 2 * OWN + 11 * 48
 LAG = 2
 WINDOW = 2
@@ -97,6 +100,7 @@
 CHOP = 4
 CLAG = 3
 AHEAD = 4
+CWAIT = 6
 
 
 def class_base(k, lane):
@@ -228,7 +232,7 @@
 
 def open_kernel(
     master, codes, labels, picks, starts, classes, nulls, frequency, out, x0, info, gain, cosine,
-    sine, table, exact, master_sem, own_sem, recv_sem, recv_c, core_sem, send_sem, sent, mine, rx_core, rx_up, rx_down,
+    sine, table, exact, master_sem, recv_sem, recv_c, core_sem, send_sem, sent, mine, rx_core, rx_up, rx_down,
     swap_send, swap_recv, x_send, x_recv, line_send, up_recv, down_recv, last_send, last_recv,
     note, note_send, note_recv, gain_send, gain_recv,
 ):
@@ -239,6 +243,10 @@
     holds_gain = jnp.logical_and(sec == 3, dp == gain_dp)
 
     parts = [pl.ds(k * (OWN // 4), OWN // 4) for k in range(4)]
+    def place_own(part, value):
+        start = pl.multiple_of(dp * OWN + part.start, 16)
+        out[pl.ds(start, part.size), :] = value
+
     fetch = [
         pltpu.make_async_copy(master.at[part], exact.at[part], master_sem.at[k])
         for k, part in enumerate(parts)
@@ -276,7 +284,12 @@
     info[dp] = note[...]
     for one, part in zip(fetch, parts):
         one.wait()
-        table[part, :] = exact[part, :].astype(BF16)
+        value = exact[part, :].astype(BF16)
+        table[part, :] = value
+        pl.when(jnp.logical_and(home, z < 2))(lambda part=part, value=value: place_own(part, value))
+    pl.when(classes_of[4][0])(
+        lambda: place_own(pl.ds(0, 11 * 48), exact[pl.ds(0, 11 * 48), :].astype(BF16))
+    )
     count = 8 + jnp.logical_or(sec == 0, sec == 2).astype(jnp.int32)
     pl.semaphore_wait(barrier, count + 7 * holds_gain.astype(jnp.int32))
     for k in range(1, 8):
@@ -318,26 +331,8 @@
 
     pl.when(holds_gain)(send_gain)
 
-    def keep(rows):
-        return pltpu.make_async_copy(
-            table.at[pl.ds(0, rows)],
-            out.at[pl.ds(pl.multiple_of(dp * OWN, 16), rows)],
-            own_sem,
-        )
-
-    def keep_all():
-        keep(OWN).start()
-        keep(OWN).wait()
-
-    def keep_few():
-        keep(11 * 48).start()
-        keep(11 * 48).wait()
-
-    pl.when(jnp.logical_and(home, z < 2))(keep_all)
-    pl.when(classes_of[4][0])(keep_few)
-
-    def copy(k, hop, j, rows, recv, slot):
-        part = out.at[pl.ds(pl.multiple_of(class_base(k, c) + j * rows, 16), rows)]
+    def copy(k, hop, offset, rows, recv, slot):
+        part = out.at[pl.ds(pl.multiple_of(class_base(k, c) + offset, 16), rows)]
         return pltpu.make_async_remote_copy(
             src_ref=part,
             dst_ref=part,
@@ -347,25 +342,29 @@
             device_id_type=MESH,
         )
 
-    def piece(k, j, rows):
+    def piece(k, j, small):
         source, sends, _, _ = classes_of[k]
         recv = recv_c.at[j] if k == 4 else recv_sem.at[k, j]
         slot = lax.rem(j, WINDOW)
+        rows = SMALL_ROWS if small else ROWS[k]
+        offset = ROWS[k] * LARGE[k] + rows * (j - LARGE[k]) if small else rows * j
 
         def send(hop):
             to = core_sem.at[k] if hop == "core" else recv
-            one = copy(k, hop, j, rows, to, slot)
-            before = True if hop == "core" else sends[hop](j - WINDOW)
-            pl.when(jnp.logical_and(j >= WINDOW, before))(one.wait_send)
+            before = j >= WINDOW if hop == "core" else jnp.logical_and(j >= WINDOW, sends[hop](j - WINDOW))
+            if small:
+                was_large = j < LARGE[k] + WINDOW
+                wide_one = copy(k, hop, 0, ROWS[k], to, slot)
+                pl.when(jnp.logical_and(before, was_large))(wide_one.wait_send)
+                before = jnp.logical_and(before, jnp.logical_not(was_large))
+            one = copy(k, hop, offset, rows, to, slot)
+            pl.when(before)(one.wait_send)
             one.start()
 
-        pl.when(jnp.logical_not(source))(copy(k, "x", j, rows, recv, slot).wait_recv)
+        pl.when(jnp.logical_not(source))(copy(k, "x", offset, rows, recv, slot).wait_recv)
         for hop in HOPS[:3]:
             pl.when(sends[hop](j))(lambda hop=hop: send(hop))
         send("core")
-
-    def counts(k):
-        return COUNT[k], ROWS[k]
 
     first = sec == 0
     second = sec == 2
@@ -472,12 +471,14 @@
 
     def step(i, carry):
         for k in range(5):
-            count, rows = counts(k)
             j = i - LAG * classes_of[k][3]
-            now = jnp.logical_and(j >= 0, j < count)
+            now = jnp.logical_and(j >= 0, j < LARGE[k])
             if k == 4:
                 now = jnp.logical_and(now, c == 0)
-            pl.when(now)(lambda k=k, j=j, rows=rows: piece(k, j, rows))
+            pl.when(now)(lambda k=k, j=j: piece(k, j, False))
+            if k < 4:
+                now = jnp.logical_and(j >= LARGE[k], j < LARGE[k] + SMALL)
+                pl.when(now)(lambda k=k, j=j: piece(k, j, True))
         pl.when(jnp.logical_and(first, i < 8))(lambda: lookup(i))
         pl.when(jnp.logical_or(first, second))(lambda: chains(i))
         pl.when(jnp.logical_and(second, i == last_step))(lambda: last().start())
@@ -495,7 +496,7 @@
             device_id_type=MESH,
         )
 
-    lax.fori_loop(0, max(18 + 5 * LAG, last_step + 1), step, 0)
+    lax.fori_loop(0, max(LARGE[0] + SMALL + 5 * LAG, last_step + 1), step, 0)
 
     def blocks(count, sem):
         return pltpu.make_async_remote_copy(
@@ -535,21 +536,21 @@
     pl.when(jnp.logical_and(sec >= 2, jnp.logical_not(holds_gain)))(gain_to(2, dp).wait_recv)
 
     def drain(k):
-        count, rows = counts(k)
+        count, rows = (LARGE[4], ROWS[4]) if k == 4 else (LARGE[k] + SMALL, SMALL_ROWS)
         _, sends, _, _ = classes_of[k]
         for j in range(count - WINDOW, count):
             for hop in HOPS[:3]:
-                one = copy(k, hop, j, rows, core_sem.at[k], j % WINDOW)
+                one = copy(k, hop, 0, rows, core_sem.at[k], j % WINDOW)
                 pl.when(sends[hop](j))(one.wait_send)
-            copy(k, "core", j, rows, core_sem.at[k], j % WINDOW).wait_send()
+            copy(k, "core", 0, rows, core_sem.at[k], j % WINDOW).wait_send()
         if k == 0:
             for j in range(TURN - WINDOW, TURN):
-                one = copy(k, "x", j, rows, core_sem.at[k], j % WINDOW)
+                one = copy(k, "x", 0, ROWS[0], core_sem.at[k], j % WINDOW)
                 last_one = jnp.logical_not(sends["x"](j + WINDOW))
                 pl.when(jnp.logical_and(sends["x"](j), last_one))(one.wait_send)
 
     def came(k):
-        count, rows = counts(k)
+        count, rows = COUNT[k], ROWS[k]
         part = out.at[pl.ds(pl.multiple_of(class_base(k, 1 - c), 16), count * rows)]
         pltpu.make_async_remote_copy(
             src_ref=part,
@@ -585,8 +586,7 @@
         scratch_shapes=[
             pltpu.VMEM((OWN, D), F32),
             pltpu.SemaphoreType.DMA((4,)),
-            pltpu.SemaphoreType.DMA,
-            pltpu.SemaphoreType.DMA((4, 18)),
+            pltpu.SemaphoreType.DMA((4, 20)),
             pltpu.SemaphoreType.DMA((11,)),
             pltpu.SemaphoreType.DMA((5,)),
             pltpu.SemaphoreType.DMA((5, 4, WINDOW)),
@@ -880,12 +880,13 @@
 
     def step(i, carry):
         for k in range(4):
-            pl.when(both(lax.rem(i, 2) == 0, i < COUNT[k]))(lambda k=k: form(k, i // 2))
-        pl.when(both(i == 1, c == 0))(lambda: form_last(loc))
-        pl.when(both(i == 1, c == 1))(form_for_other)
+            turn_now = both(lax.rem(i, 2) == k // 2, i < COUNT[k] + k // 2)
+            pl.when(turn_now)(lambda k=k: form(k, i // 2))
+        pl.when(both(i == CWAIT - 1, c == 0))(lambda: form_last(loc))
+        pl.when(both(i == CWAIT - 1, c == 1))(form_for_other)
         for k in range(5):
             source, _, _, depth = classes[k]
-            j = i - CLAG * ((5, 5, 4, 4, 3)[k] - depth) - (2 if k == 4 else 0)
+            j = i - CLAG * ((5, 5, 4, 4, 3)[k] - depth) - (0, 0, 1, 1, CWAIT)[k]
             now = both(j >= 0, j < COUNT[k])
             if k == 4:
                 now = both(now, c == 0)
@@ -1107,84 +1108,120 @@
 
 def forward_kernel(keep, x, w_any, cosine, sine, starts, y, *refs):
     kept = refs[:7] if keep else ()
-    q, k, v, o, h, gate, up, w, m, unseen, sems, keep_sems = refs[len(kept) :]
+    q, k, v, o, h, gate, up, w, m, unseen, sems, keep_sems, *hop_sems = refs[len(kept) :]
+    sec = lax.axis_index("section")
+    dp = lax.axis_index("dp")
+    lower = sec < 2
+    if not keep:
+        barrier = pltpu.get_barrier_semaphore()
+        pl.when(jnp.logical_not(lower))(
+            lambda: pl.semaphore_signal(barrier, 1, device_id=(sec - 2, dp), device_id_type=MESH)
+        )
+
+    def hop(b):
+        part = y.at[:, pl.ds(b * 256, 256)]
+        return pltpu.make_async_remote_copy(
+            src_ref=part,
+            dst_ref=part,
+            send_sem=hop_sems[0].at[b],
+            recv_sem=hop_sems[1].at[b],
+            device_id=(sec + 2, dp),
+            device_id_type=MESH,
+        )
 
     def put(i):
         if keep:
             pltpu.make_async_copy((q, k, v, o, h, gate, up)[i], kept[i], keep_sems.at[i]).start()
 
-    copies = weight_copies(w_any, w, sems)
-    for i in (5, 0, 1, 2, 3, 4):
-        copies[i].start()
-    unseen[...] = see(starts)
-    lanes = lax.broadcasted_iota(jnp.int32, (SP, 128), 1)
-    first = lanes < 64
-    copies[5].wait()
-    gains = w[pl.ds(MATS, 16), :].astype(F32)
-    stream = x[...].astype(F32)
-    a1 = rms_scale(stream, gains[0:1]).astype(BF16)
-    copies[0].wait()
-
-    def project(b, carry):
-        cols = pl.ds(pl.multiple_of(b * 256, 256), 256)
-        raw_q = nn(a1, w[pl.ds(0, D), cols])
-        raw_k = nn(a1, w[pl.ds(D, D), cols])
-        raw_v = nn(a1, w[pl.ds(2 * D, D), cols])
-        v[:, cols] = raw_v.astype(BF16)
-        for part in range(2):
-            there = pl.ds(pl.multiple_of(b * 256 + part * 128, 128), 128)
-            here = slice(part * 128, (part + 1) * 128)
-            turned_q = turn(raw_q[:, here], cosine[...], sine[...], lanes)
-            q[:, there] = (turned_q * HD ** (-0.5)).astype(BF16)
-            k[:, there] = turn(raw_k[:, here], cosine[...], sine[...], lanes).astype(BF16)
-        return carry
-
-    lax.fori_loop(0, D // 256, project, 0, unroll=True)
-    for i in range(3):
-        put(i)
-
-    def attend(b, carry):
-        cols = pl.ds(pl.multiple_of(b * 128, 128), 128)
-        qb, kb, vb = q[:, cols], k[:, cols], v[:, cols]
-        zero = jnp.zeros_like(qb)
-        p0 = softmax_of(nt(jnp.where(first, qb, zero), kb), unseen[...]).astype(BF16)
-        p1 = softmax_of(nt(jnp.where(first, zero, qb), kb), unseen[...]).astype(BF16)
-        o[:, cols] = jnp.where(first, nn(p0, vb), nn(p1, vb)).astype(BF16)
-        return carry
-
-    lax.fori_loop(0, HEADS // 2, attend, 0, unroll=True)
-    put(3)
-    copies[1].wait()
-    for b in range(3):
-        cols = pl.ds(b * 256, 256)
-        h[:, cols] = x[:, cols].astype(F32) + nn(o[...], w[pl.ds(3 * D, D), cols])
-    put(4)
-    a2 = rms_scale(h[...], gains[1:2]).astype(BF16)
-    copies[2].wait()
-    copies[3].wait()
-
-    def widen(b, carry):
-        cols = pl.ds(pl.multiple_of(b * FT, FT), FT)
-        g = nt(a2, w[pl.ds(pl.multiple_of(4 * D + b * FT, FT), FT), :])
-        u = nt(a2, w[pl.ds(pl.multiple_of(4 * D + FF + b * FT, FT), FT), :])
-        gate[:, cols] = g
-        up[:, cols] = u
-        m[:, cols] = (g / (1.0 + jnp.exp(-g)) * u).astype(BF16)
-        return carry
-
-    lax.fori_loop(0, FF // FT, widen, 0, unroll=True)
-    put(5)
-    put(6)
-    copies[4].wait()
-
-    def narrow(b, carry):
-        cols = pl.ds(pl.multiple_of(b * 256, 256), 256)
-        y[:, cols] = (h[:, cols] + nn(m[...], w[pl.ds(4 * D + 2 * FF, FF), cols])).astype(BF16)
-        return carry
-
-    lax.fori_loop(0, 3, narrow, 0, unroll=True)
-    for i, part in enumerate(kept):
-        pltpu.make_async_copy((q, k, v, o, h, gate, up)[i], part, keep_sems.at[i]).wait()
+    def run():
+        copies = weight_copies(w_any, w, sems)
+        for i in (5, 0, 1, 2, 3, 4):
+            copies[i].start()
+        unseen[...] = see(starts)
+        lanes = lax.broadcasted_iota(jnp.int32, (SP, 128), 1)
+        first = lanes < 64
+        copies[5].wait()
+        gains = w[pl.ds(MATS, 16), :].astype(F32)
+        stream = x[...].astype(F32)
+        a1 = rms_scale(stream, gains[0:1]).astype(BF16)
+        copies[0].wait()
+
+        def project(b, carry):
+            cols = pl.ds(pl.multiple_of(b * 256, 256), 256)
+            raw_q = nn(a1, w[pl.ds(0, D), cols])
+            raw_k = nn(a1, w[pl.ds(D, D), cols])
+            raw_v = nn(a1, w[pl.ds(2 * D, D), cols])
+            v[:, cols] = raw_v.astype(BF16)
+            for part in range(2):
+                there = pl.ds(pl.multiple_of(b * 256 + part * 128, 128), 128)
+                here = slice(part * 128, (part + 1) * 128)
+                turned_q = turn(raw_q[:, here], cosine[...], sine[...], lanes)
+                q[:, there] = (turned_q * HD ** (-0.5)).astype(BF16)
+                k[:, there] = turn(raw_k[:, here], cosine[...], sine[...], lanes).astype(BF16)
+            return carry
+
+        lax.fori_loop(0, D // 256, project, 0, unroll=True)
+        for i in range(3):
+            put(i)
+
+        def attend(b, carry):
+            cols = pl.ds(pl.multiple_of(b * 128, 128), 128)
+            qb, kb, vb = q[:, cols], k[:, cols], v[:, cols]
+            zero = jnp.zeros_like(qb)
+            p0 = softmax_of(nt(jnp.where(first, qb, zero), kb), unseen[...]).astype(BF16)
+            p1 = softmax_of(nt(jnp.where(first, zero, qb), kb), unseen[...]).astype(BF16)
+            o[:, cols] = jnp.where(first, nn(p0, vb), nn(p1, vb)).astype(BF16)
+            return carry
+
+        lax.fori_loop(0, HEADS // 2, attend, 0, unroll=True)
+        put(3)
+        copies[1].wait()
+        for b in range(3):
+            cols = pl.ds(b * 256, 256)
+            h[:, cols] = x[:, cols].astype(F32) + nn(o[...], w[pl.ds(3 * D, D), cols])
+        put(4)
+        a2 = rms_scale(h[...], gains[1:2]).astype(BF16)
+        copies[2].wait()
+        copies[3].wait()
+
+        def widen(b, carry):
+            cols = pl.ds(pl.multiple_of(b * FT, FT), FT)
+            g = nt(a2, w[pl.ds(pl.multiple_of(4 * D + b * FT, FT), FT), :])
+            u = nt(a2, w[pl.ds(pl.multiple_of(4 * D + FF + b * FT, FT), FT), :])
+            gate[:, cols] = g
+            up[:, cols] = u
+            m[:, cols] = (g / (1.0 + jnp.exp(-g)) * u).astype(BF16)
+            return carry
+
+        lax.fori_loop(0, FF // FT, widen, 0, unroll=True)
+        put(5)
+        put(6)
+        copies[4].wait()
+
+        if not keep:
+            pl.semaphore_wait(barrier, 1)
+        for b in range(3):
+            cols = pl.ds(b * 256, 256)
+            y[:, cols] = (h[:, cols] + nn(m[...], w[pl.ds(4 * D + 2 * FF, FF), cols])).astype(BF16)
+            if not keep:
+                hop(b).start()
+        for i, part in enumerate(kept):
+            pltpu.make_async_copy((q, k, v, o, h, gate, up)[i], part, keep_sems.at[i]).wait()
+        if not keep:
+            for b in range(3):
+                hop(b).wait_send()
+            y[...] = x[...]
+
+    if keep:
+        run()
+        return
+    pl.when(lower)(run)
+
+    def arrive():
+        for b in range(3):
+            hop(b).wait_recv()
+
+    pl.when(jnp.logical_not(lower))(arrive)
 
 
 KEPT = ((D, BF16), (D, BF16), (D, BF16), (D, BF16), (D, F32), (FF, F32), (FF, F32))
@@ -1205,8 +1242,13 @@
             pltpu.VMEM((SP, SP), F32),
             pltpu.SemaphoreType.DMA((6,)),
             pltpu.SemaphoreType.DMA((7,)),
-        ],
-        compiler_params=pltpu.CompilerParams(vmem_limit_bytes=56 * 2**20),
+        ]
+        + ([] if keep else [pltpu.SemaphoreType.DMA((3,))] * 2),
+        compiler_params=pltpu.CompilerParams(vmem_limit_bytes=56 * 2**20)
+        if keep
+        else pltpu.CompilerParams(
+            collective_id=6, has_side_effects=True, vmem_limit_bytes=56 * 2**20
+        ),
         name="layer_forward_kept" if keep else "layer_forward",
     )(x, weights, cosine, sine, starts)
 
@@ -1219,125 +1261,156 @@
     return grad_in, jnp.sum(grad * unit, axis=0, keepdims=True)
 
 
-def backward_kernel(dy, x, w_any, cosine, sine, starts, *refs):
+def backward_kernel(send, dy, x, w_any, cosine, sine, starts, *refs):
     kept, refs = refs[:7], refs[7:]
     dx, left, right, tail, refs = *refs[:4], refs[4:]
     q, k, v, o, h, gate, up, w, dgate, dup, m, da, do, dq, dk, dv, a1, a2, db, *refs = refs
-    unseen, sems, keep_sems, out_sems = refs
+    unseen, sems, keep_sems, out_sems, *hop_sems = refs
+    sec = lax.axis_index("section")
+    dp = lax.axis_index("dp")
+    upper = sec >= 2
+    if send:
+        barrier = pltpu.get_barrier_semaphore()
+        pl.when(jnp.logical_not(upper))(
+            lambda: pl.semaphore_signal(barrier, 1, device_id=(sec + 2, dp), device_id_type=MESH)
+        )
+
+    def hop():
+        return pltpu.make_async_remote_copy(
+            src_ref=dx,
+            dst_ref=dx,
+            send_sem=hop_sems[0],
+            recv_sem=hop_sems[1],
+            device_id=(sec - 2, dp),
+            device_id_type=MESH,
+        )
+
     outs = []
 
     def put(source, target):
         copy = pltpu.make_async_copy(source, target, out_sems.at[len(outs)])
         copy.start()
         outs.append(copy)
-    copies = weight_copies(w_any, w, sems)
-    taken = [
-        pltpu.make_async_copy(part, (q, k, v, o, h, gate, up)[i], keep_sems.at[i])
-        for i, part in enumerate(kept)
-    ]
-    for one in (
-        copies[4], taken[5], taken[6], copies[5], copies[2], copies[3], taken[4], copies[1],
-        taken[0], taken[1], taken[2], copies[0], taken[3],
-    ):
-        one.start()
-    unseen[...] = hide(starts)
-    lanes = lax.broadcasted_iota(jnp.int32, (SP, 128), 1)
-    first = lanes < 64
-    copies[4].wait()
-    taken[5].wait()
-    taken[6].wait()
-
-    def open_mlp(b, carry):
-        cols = pl.ds(pl.multiple_of(b * FT, FT), FT)
-        dm = nt(dy[...], w[pl.ds(pl.multiple_of(4 * D + 2 * FF + b * FT, FT), FT), :])
-        g = gate[:, cols]
-        u = up[:, cols]
-        sig = 1.0 / (1.0 + jnp.exp(-g))
-        dgate[:, cols] = (dm * u * sig * (1.0 + g * (1.0 - sig))).astype(BF16)
-        dup[:, cols] = (dm * g * sig).astype(BF16)
-        m[:, cols] = (g * sig * u).astype(BF16)
-        return carry
-
-    lax.fori_loop(0, FF // FT, open_mlp, 0, unroll=True)
-    for i, part in enumerate((dgate, dup, m)):
-        put(part, left.at[:, pl.ds(4 * D + i * FF, FF)])
-    put(dy, right.at[5])
-    copies[5].wait()
-    gains = w[pl.ds(MATS, 16), :].astype(F32)
-    copies[2].wait()
-    copies[3].wait()
-
-    def close_mlp(b, carry):
-        cols = pl.ds(pl.multiple_of(b * 256, 256), 256)
-        da[:, cols] = nn(dgate[...], w[pl.ds(4 * D, FF), cols]) + nn(
-            dup[...], w[pl.ds(4 * D + FF, FF), cols]
-        )
-        return carry
-
-    lax.fori_loop(0, 3, close_mlp, 0, unroll=True)
-    taken[4].wait()
-    dh, dg_mlp = rms_back(h[...], gains[1:2], da[...])
-    dh = dh + dy[...].astype(F32)
-    db[...] = dh.astype(BF16)
-    a2[...] = rms_scale(h[...], gains[1:2]).astype(BF16)
-    put(db, right.at[3])
-    put(a2, right.at[4])
-    copies[1].wait()
-    for b in range(3):
-        do[:, pl.ds(b * 256, 256)] = nt(db[...], w[pl.ds(3 * D + b * 256, 256), :]).astype(BF16)
-
-    for i in range(3):
-        taken[i].wait()
-
-    def attend(b, carry):
-        cols = pl.ds(pl.multiple_of(b * 128, 128), 128)
-        qb, kb, vb, dob = q[:, cols], k[:, cols], v[:, cols], do[:, cols]
-        zero = jnp.zeros_like(qb)
-        parts = []
-        for head in range(2):
-            keep = first if head == 0 else jnp.logical_not(first)
-            masked = nt(jnp.where(keep, kb, zero), qb) + unseen[...]
-            grown = jnp.exp(masked - jnp.max(masked, axis=0, keepdims=True))
-            probs = grown / jnp.sum(grown, axis=0, keepdims=True)
-            dprobs = nt(jnp.where(keep, vb, zero), dob)
-            along = jnp.sum(probs * dprobs, axis=0, keepdims=True)
-            dscores = (probs * (dprobs - along)).astype(BF16)
-            parts.append((tn(dscores, kb), nn(dscores, qb), nn(probs.astype(BF16), dob)))
-        dqb = jnp.where(first, parts[0][0], parts[1][0]) * HD ** (-0.5)
-        dkb = jnp.where(first, parts[0][1], parts[1][1])
-        dq[:, cols] = turn(dqb, cosine[...], -sine[...], lanes).astype(BF16)
-        dk[:, cols] = turn(dkb, cosine[...], -sine[...], lanes).astype(BF16)
-        dv[:, cols] = jnp.where(first, parts[0][2], parts[1][2]).astype(BF16)
-        return carry
-
-    lax.fori_loop(0, HEADS // 2, attend, 0, unroll=True)
-    for i, part in enumerate((dq, dk, dv)):
-        put(part, right.at[i])
-    copies[0].wait()
-    for b in range(3):
-        rows = lambda i, b=b: w[pl.ds(i * D + b * 256, 256), :]
-        da[:, pl.ds(b * 256, 256)] = (
-            nt(dq[...], rows(0)) + nt(dk[...], rows(1)) + nt(dv[...], rows(2))
-        )
-    stream = x[...].astype(F32)
-    a1[...] = rms_scale(stream, gains[0:1]).astype(BF16)
-    for i in range(3):
-        put(a1, left.at[:, pl.ds(i * D, D)])
-    taken[3].wait()
-    put(o, left.at[:, pl.ds(3 * D, D)])
-    dstream, dg_attn = rms_back(stream, gains[0:1], da[...])
-    dx[...] = (dstream + dh).astype(BF16)
-    ids = lax.broadcasted_iota(jnp.int32, (16, D), 0)
-    tail[...] = jnp.where(ids == 0, dg_attn, jnp.where(ids == 1, dg_mlp, 0.0)).astype(BF16)
-    for copy in outs:
-        copy.wait()
-
-
-def backward_call(dy, x, weights, cosine, sine, starts, kept):
+    def run():
+        copies = weight_copies(w_any, w, sems)
+        taken = [
+            pltpu.make_async_copy(part, (q, k, v, o, h, gate, up)[i], keep_sems.at[i])
+            for i, part in enumerate(kept)
+        ]
+        for one in (
+            copies[4], taken[5], taken[6], copies[5], copies[2], copies[3], taken[4], copies[1],
+            taken[0], taken[1], taken[2], copies[0], taken[3],
+        ):
+            one.start()
+        unseen[...] = hide(starts)
+        lanes = lax.broadcasted_iota(jnp.int32, (SP, 128), 1)
+        first = lanes < 64
+        copies[4].wait()
+        taken[5].wait()
+        taken[6].wait()
+
+        def open_mlp(b, carry):
+            cols = pl.ds(pl.multiple_of(b * FT, FT), FT)
+            dm = nt(dy[...], w[pl.ds(pl.multiple_of(4 * D + 2 * FF + b * FT, FT), FT), :])
+            g = gate[:, cols]
+            u = up[:, cols]
+            sig = 1.0 / (1.0 + jnp.exp(-g))
+            dgate[:, cols] = (dm * u * sig * (1.0 + g * (1.0 - sig))).astype(BF16)
+            dup[:, cols] = (dm * g * sig).astype(BF16)
+            m[:, cols] = (g * sig * u).astype(BF16)
+            return carry
+
+        lax.fori_loop(0, FF // FT, open_mlp, 0, unroll=True)
+        for i, part in enumerate((dgate, dup, m)):
+            put(part, left.at[:, pl.ds(4 * D + i * FF, FF)])
+        put(dy, right.at[5])
+        copies[5].wait()
+        gains = w[pl.ds(MATS, 16), :].astype(F32)
+        copies[2].wait()
+        copies[3].wait()
+
+        def close_mlp(b, carry):
+            cols = pl.ds(pl.multiple_of(b * 256, 256), 256)
+            da[:, cols] = nn(dgate[...], w[pl.ds(4 * D, FF), cols]) + nn(
+                dup[...], w[pl.ds(4 * D + FF, FF), cols]
+            )
+            return carry
+
+        lax.fori_loop(0, 3, close_mlp, 0, unroll=True)
+        taken[4].wait()
+        dh, dg_mlp = rms_back(h[...], gains[1:2], da[...])
+        dh = dh + dy[...].astype(F32)
+        db[...] = dh.astype(BF16)
+        a2[...] = rms_scale(h[...], gains[1:2]).astype(BF16)
+        put(db, right.at[3])
+        put(a2, right.at[4])
+        copies[1].wait()
+        for b in range(3):
+            do[:, pl.ds(b * 256, 256)] = nt(db[...], w[pl.ds(3 * D + b * 256, 256), :]).astype(BF16)
+
+        for i in range(3):
+            taken[i].wait()
+
+        def attend(b, carry):
+            cols = pl.ds(pl.multiple_of(b * 128, 128), 128)
+            qb, kb, vb, dob = q[:, cols], k[:, cols], v[:, cols], do[:, cols]
+            zero = jnp.zeros_like(qb)
+            parts = []
+            for head in range(2):
+                keep = first if head == 0 else jnp.logical_not(first)
+                masked = nt(jnp.where(keep, kb, zero), qb) + unseen[...]
+                grown = jnp.exp(masked - jnp.max(masked, axis=0, keepdims=True))
+                probs = grown / jnp.sum(grown, axis=0, keepdims=True)
+                dprobs = nt(jnp.where(keep, vb, zero), dob)
+                along = jnp.sum(probs * dprobs, axis=0, keepdims=True)
+                dscores = (probs * (dprobs - along)).astype(BF16)
+                parts.append((tn(dscores, kb), nn(dscores, qb), nn(probs.astype(BF16), dob)))
+            dqb = jnp.where(first, parts[0][0], parts[1][0]) * HD ** (-0.5)
+            dkb = jnp.where(first, parts[0][1], parts[1][1])
+            dq[:, cols] = turn(dqb, cosine[...], -sine[...], lanes).astype(BF16)
+            dk[:, cols] = turn(dkb, cosine[...], -sine[...], lanes).astype(BF16)
+            dv[:, cols] = jnp.where(first, parts[0][2], parts[1][2]).astype(BF16)
+            return carry
+
+        lax.fori_loop(0, HEADS // 2, attend, 0, unroll=True)
+        for i, part in enumerate((dq, dk, dv)):
+            put(part, right.at[i])
+        copies[0].wait()
+        for b in range(3):
+            rows = lambda i, b=b: w[pl.ds(i * D + b * 256, 256), :]
+            da[:, pl.ds(b * 256, 256)] = (
+                nt(dq[...], rows(0)) + nt(dk[...], rows(1)) + nt(dv[...], rows(2))
+            )
+        stream = x[...].astype(F32)
+        a1[...] = rms_scale(stream, gains[0:1]).astype(BF16)
+        for i in range(3):
+            put(a1, left.at[:, pl.ds(i * D, D)])
+        taken[3].wait()
+        put(o, left.at[:, pl.ds(3 * D, D)])
+        dstream, dg_attn = rms_back(stream, gains[0:1], da[...])
+        dx[...] = (dstream + dh).astype(BF16)
+        if send:
+            pl.semaphore_wait(barrier, 1)
+            hop().start()
+        ids = lax.broadcasted_iota(jnp.int32, (16, D), 0)
+        tail[...] = jnp.where(ids == 0, dg_attn, jnp.where(ids == 1, dg_mlp, 0.0)).astype(BF16)
+        for copy in outs:
+            copy.wait()
+        if send:
+            hop().wait_send()
+
+    if not send:
+        run()
+        return
+    pl.when(upper)(run)
+    pl.when(jnp.logical_not(upper))(lambda: hop().wait_recv())
+
+
+def backward_call(send, dy, x, weights, cosine, sine, starts, kept):
     wide = pltpu.VMEM((SP, FF), BF16)
     narrow = pltpu.VMEM((SP, D), BF16)
     return pl.pallas_call(
-        backward_kernel,
+        functools.partial(backward_kernel, send),
         out_shape=(
             jax.ShapeDtypeStruct((SP, D), BF16),
             jax.ShapeDtypeStruct((SP, MATS), BF16),
@@ -1360,9 +1433,14 @@
             pltpu.SemaphoreType.DMA((6,)),
             pltpu.SemaphoreType.DMA((7,)),
             pltpu.SemaphoreType.DMA((13,)),
-        ],
-        compiler_params=pltpu.CompilerParams(vmem_limit_bytes=60 * 2**20),
-        name="layer_backward",
+        ]
+        + ([pltpu.SemaphoreType.DMA] * 2 if send else []),
+        compiler_params=pltpu.CompilerParams(
+            collective_id=7, has_side_effects=True, vmem_limit_bytes=60 * 2**20
+        )
+        if send
+        else pltpu.CompilerParams(vmem_limit_bytes=60 * 2**20),
+        name="layer_backward_send" if send else "layer_backward",
     )(dy, x, weights, cosine, sine, starts, *kept)
 
 
@@ -1525,7 +1603,7 @@
             body(pl.multiple_of(t * HEAD_T, HEAD_T), HEAD_T)
             return carry
 
-        lax.fori_loop(0, own // HEAD_T, step, 0)
+        lax.fori_loop(0, own // HEAD_T, step, 0, unroll=True)
         body(own - own % HEAD_T, own % HEAD_T)
 
     def forward_part():
@@ -1659,7 +1737,7 @@
             table_part(pl.multiple_of(t * HEAD_T, HEAD_T), HEAD_T)
             return carry
 
-        lax.fori_loop(0, own // HEAD_T, step, 0)
+        lax.fori_loop(0, own // HEAD_T, step, 0, unroll=True)
         rx[z] = low[pl.ds(pl.multiple_of((2 * z + 1) * PICKS, PICKS), PICKS), :]
         span(rx_core, 8 * PICKS, swap_send, swap_recv).wait_send()
         span(low, 7 * PICKS, daf_send, daf_recv).wait_send()
@@ -1839,8 +1917,7 @@
         weights, x0, local, all_labels, all_counts, g_f, cosine, sine = opened
     around = (cosine, sine, starts)
 
-    y0 = forward_call(False, x0, weights, *around)[0]
-    x = jnp.where(sec < 2, x0, lax.ppermute(y0, "section", [(0, 2), (1, 3)]))
+    x = forward_call(False, x0, weights, *around)[0]
     y, *kept = forward_call(True, x, weights, *around)
 
     if fast:
@@ -1850,10 +1927,11 @@
             y, picks[par], all_labels, all_counts, g_f, table
         )
 
-    once = backward_call(d_top, x, weights, *around, kept)
-    dy = lax.ppermute(once[0], "section", [(2, 0), (3, 1)])
+    once = backward_call(True, d_top, x, weights, *around, kept)
     dx0, left, right, tail = lax.cond(
-        sec < 2, lambda: tuple(backward_call(dy, x, weights, *around, kept)), lambda: tuple(once)
+        sec < 2,
+        lambda: tuple(backward_call(False, once[0], x, weights, *around, kept)),
+        lambda: tuple(once),
     )
 
     if fast:

time: 434 us -> 421 us (0.970)
  waiting for transfers between devices: 68.2 us -> 0 us
  Pallas kernels: 333 us -> 390 us
    ppermute x2 -> x0, waiting for transfers between devices: 68.2 us -> none  [the longest x1 58.7 us: shards(): dy = lax.ppermute(once[0], 'section', [(2, 0), (3, 1)])]
    pallas_call x2, Pallas kernels: 42.9 us -> 91.9 us  [backward_call(): pl.pallas_call(functools.partial(backward_kernel, send), out_shape=(jax.S...]
    pallas_call x2, Pallas kernels: 26.2 us -> 35 us  [forward_call(): pl.pallas_call(functools.partial(forward_kernel, keep), out_shape=(low,)...]
  transfers between devices with their start and end apart: 2 -> 0, of which waited for: 2 -> 0; matrix products, arithmetic and copies ran while one was open for 1% -> 0% of each run, Pallas kernels for 0% -> 0%
where the time goes in v4:
time: 421 us; the launch traced here: 416 us
  Pallas kernels  390 us (93%)
  other arithmetic  19 us (5%)
  local copies, waits for them, and re-layouts  4.98 us (1%)
    pallas_call x1, Pallas kernels, gather_and_embed(): pl.pallas_call(open_kernel, out_shape=(jax.ShapeDtypeStruct((WROWS, D), B...  125 us
    pallas_call x1, Pallas kernels, reduce_and_scatter(): pl.pallas_call(close_kernel, out_shape=(jax.ShapeDtypeStruct((OWN, D), F3...  117 us
    pallas_call x2, Pallas kernels, backward_call(): pl.pallas_call(functools.partial(backward_kernel, send), out_shape=(jax.S...  91.9 us
    pallas_call x2, Pallas kernels, forward_call(): pl.pallas_call(functools.partial(forward_kernel, keep), out_shape=(low,)...  35 us
    add x1, other arithmetic, shards(): new_average = average_decay * average + (1.0 - average_decay) * new_master  16.7 us
    pallas_call x1, Pallas kernels, share_norm(): pl.pallas_call(functools.partial(norm_kernel, n_sec, n_dp), out_shape=jax...  14.7 us

profile of v4, /device:TPU:0, one launch (start us, length us, event | category | flops | bytes accessed | tf_op | source)
XLA Modules:
  0.0 415.8 jit_solution(169917301812392175)
XLA Ops:
  0.6 0.0 copy-start
  0.7 0.6 tile.9.frequency
  1.3 124.9 %gather_and_embed.1 = (bf16[9232,768]{1,0:T(8,128)(2,1)}, bf16[272,768]{1,0:T(8,128)(2,1)}, s32[8,8,384]{2,1,0:T(8,128)}, bf16[16,768]{1,0:T(8,128)(2,1)}, f32[2...) custom-call(f32[2176,768]{1,0:T(8,128)} %master.1, s32[2,264]{1,0:T(2,128)} %codes.1, ...), custom_call_target="tpu_custom_call" | custom-call | tf_op jit(solution)/shard_map/gather_and_embed/pallas_call | solution.py:573
  126.2 1.4 convert_reduce_fusion
  127.6 0.0 copy-done
  127.6 22.1 %layer_forward.1.x = bf16[272,768]{1,0:T(8,128)(2,1)S(1)} custom-call(bf16[272,768]{1,0:T(8,128)(2,1)} %get-tuple-element.78.x, bf16[9232,768]{1,0:T(8,128)(2,1)} %get-tuple-element.79.w_any, f32[272,128]{1,0:T(8,128)S(1)} %get-tuple-element.80.cosine, f32[272,128]{1,0:T(8,128)S(1)} %get-tuple-element.81.sine, s32[2,4]{1,0:T(2,128)S(1)} %copy-done), custom_call_target="tpu_custom_call" | custom-call | tf_op jit(solution)/shard_map/layer_forward/pallas_call | solution.py:1233
  149.7 0.9 select_subtract_fusion
  150.6 0.7 sub.21.index
  151.4 12.9 %layer_forward_kept.1 = (bf16[272,768]{1,0:T(8,128)(2,1)}, bf16[272,768]{1,0:T(8,128)(2,1)}, bf16[272,768]{1,0:T(8,128)(2,1)}, bf16[272,768]{1,0:T(8,128)(2,1)},...) custom-call(bf16[272,768]{1,0:T(8,128)(2,1)S(1)} %layer_forward.1.x, ...), custom_call_target="tpu_custom_call" | custom-call | tf_op jit(solution)/shard_map/layer_forward_kept/pallas_call | solution.py:1233
  164.2 6.3 %head.1 = (bf16[272,768]{1,0:T(8,128)(2,1)}, f32[2176,768]{1,0:T(8,128)}, f32[8,128]{1,0:T(8,128)}) custom-call(bf16[272,768]{1,0:T(8,128)(2,1)} %get-tuple-element.82.y, s32[2,32]{1,0:T(2,128)} %picks.3, s32[8,8,384]{2,1,0:T(8,128)} %get-tuple-element.83.info, bf16[16,768]{1,0:T(8,128)(2,1)} %get-tuple-element.84.gain, ...), custom_call_target="tpu_custom_call" | custom-call | tf_op jit(solution)/shard_map/head/pallas_call | solution.py:1782
  170.5 70.5 %layer_backward_send.1 = (bf16[272,768]{1,0:T(8,128)(2,1)}, bf16[272,9216]{1,0:T(8,128)(2,1)}, bf16[6,272,768]{2,1,0:T(8,128)(2,1)}, bf16[16,768]{1,0:T(8,128)(2,1)S(1)}) custom-call(bf16[272,768]{1,0:T(8,128)(2,1)} %get-tuple-element.87.dy, bf16[272,768]{1,0:T(8,128)(2,1)S(1)} %layer_forward.1.x, bf16[9232,768]{1,0:T(8,128)(2,1)} %get-tuple-element.79.w_any, ...), custom_call_target="tpu_custom_call" | custom-call | tf_op jit(solution)/shard_map/layer_backward_send/pallas_call | solution.py:1412
  241.0 23.4 %conditional.1 = ((bf16[272,768]{1,0:T(8,128)(2,1)}, bf16[272,9216]{1,0:T(8,128)(2,1)}, bf16[6,272,768]{2,1,0:T(8,128)(2,1)}, bf16[16,768]{1,0:T(8,128)(2,1)S(1)})) conditional(s32[]{:T(128)} %convert_element_type.6, (bf16[272,768]{1,0:T(8,128)(2,1)}, bf16[272,9216]{1,0:T(8,128)(2,1)}, bf16[6,272,768]{2,1,0:T(8,128)(2,1)}, ...), branch_computations={%region_0.1_spmd, %region_1.2_spmd} | conditional | bytes 835592 | solution.py:1931
  241.1 1.8 copy.26.dy
  242.8 21.4 %layer_backward.1 = (bf16[272,768]{1,0:T(8,128)(2,1)}, bf16[272,9216]{1,0:T(8,128)(2,1)}, bf16[6,272,768]{2,1,0:T(8,128)(2,1)}, bf16[16,768]{1,0:T(8,128)(2,1)S(1)}) custom-call(bf16[272,768]{1,0:T(8,128)(2,1)} %copy.26.dy, bf16[272,768]{1,0:T(8,128)(2,1)S(1)} %get-tuple-element.35.x, bf16[9232,768]{1,0:T(8,128)(2,1)} %get-tuple-element.36.w_any, ...), custom_call_target="tpu_custom_call" | custom-call | tf_op jit(solution)/shard_map/cond/branch_1_fun/layer_backward/pallas_call | solution.py:1412
  264.4 117.2 %reduce_and_scatter.1 = (f32[2176,768]{1,0:T(8,128)}, f32[8,128]{1,0:T(8,128)}) custom-call(bf16[272,9216]{1,0:T(8,128)(2,1)} %get-tuple-element.96.left_any, bf16[6,272,768]{2,1,0:T(8,128)(2,1)} %get-tuple-element.97.right_any, bf16[16,768]{1,0:T(8,128)(2,1)S(1)} %get-tuple-element.98.tail, ...), custom_call_target="tpu_custom_call", output_to_operand_aliasing={{0}: (3, {})} | custom-call | tf_op jit(solution)/shard_map/reduce_and_scatter/pallas_call | solution.py:953
  381.6 14.7 %share_norm.1 = f32[16,128]{1,0:T(8,128)} custom-call(f32[8,128]{1,0:T(8,128)} %get-tuple-element.86.small, f32[8,128]{1,0:T(8,128)} %get-tuple-element.101.squares), custom_call_target="tpu_custom_call" | custom-call | tf_op jit(solution)/shard_map/share_norm/pallas_call | solution.py:1050
  396.4 1.2 fusion.2
  398.3 0.7 slice_bitcast_fusion
  398.9 16.7 %multiply_add_fusion = (f32[2176,768]{1,0:T(8,128)}, f32[2176,768]{1,0:T(8,128)}, f32[2176,768]{1,0:T(8,128)}) fusion(f32[2176,768]{1,0:T(8,128)} %param.19, f32[2176,768]{1,0:T(8,128)} %master.1, f32[]{:T(128)S(6)} %min.3, f32[2176,768]{1,0:T(8,128)} %get-tuple-element.102, f32[768]{0:T(1024)S(1)} %slice_bitcast_fusion, pred[2176]{0:T(1024)(128)(4,1)S(1)} %fusion.1, ...), kind=kLoop, calls=%fused_computation | loop fusion | flops 20054016 | bytes 46797956 | tf_op jit(solution)/shard_map/add | solution.py:1961
  (3 shorter events, 0.0 us)
Async XLA Ops:
  0.6 127.0 %copy-start = (s32[2,4]{1,0:T(2,128)S(1)}, s32[2,4]{1,0:T(2,128)}, u32[]{:S(2)}) copy-start(s32[2,4]{1,0:T(2,128)} %starts.7) | copy-start | bytes 100

commit v5 on v4

--- a/solution.py
+++ b/solution.py
@@ -1058,7 +1058,12 @@
             pltpu.SemaphoreType.DMA,
             pltpu.SemaphoreType.DMA,
         ],
-        compiler_params=pltpu.CompilerParams(collective_id=8, has_side_effects=True),
+        compiler_params=pltpu.CompilerParams(
+            collective_id=8, has_side_effects=True, vmem_limit_bytes=2**20
+        ),
+        cost_estimate=pl.CostEstimate(
+            flops=10**10, bytes_accessed=4 * 10**7, transcendentals=0
+        ),
         name="share_norm",
     )(small, squares)
 
@@ -1891,6 +1896,42 @@
     return d_top, d_table, dg_f, loss_part
 
 
+UPDATE_ROWS = 272
+
+
+def update_kernel(rate, gain_block, gain_row, totals, grad, master, momentum, average, out_m, out_v, out_a):
+    block = pl.program_id(0)
+    value = grad[...]
+    sec = lax.axis_index("section")
+    dp = lax.axis_index("dp")
+    here = jnp.logical_and(jnp.logical_and(sec == 3, dp == VOCAB // OWN), block == gain_block)
+    ids = lax.broadcasted_iota(jnp.int32, value.shape, 0)
+    gain = jnp.concatenate([totals[k : k + 1, :] for k in range(6)], axis=1)
+    value = value + jnp.where(jnp.logical_and(ids == gain_row, here), gain, 0.0)
+    scale = jnp.minimum(1.0, clip_limit / (totals[8:9, 0:1] + norm_eps))
+    clipped = value * scale
+    new_momentum = momentum_decay * momentum[...] + clipped
+    new_master = master[...] - rate * (clipped + momentum_decay * new_momentum)
+    out_v[...] = new_momentum
+    out_m[...] = new_master
+    out_a[...] = average_decay * average[...] + (1.0 - average_decay) * new_master
+
+
+def update(rate, totals, grad, master, momentum, average):
+    rows = pl.BlockSpec((UPDATE_ROWS, D), lambda i: (i, 0))
+    like = jax.ShapeDtypeStruct((OWN, D), F32)
+    at = VOCAB % OWN
+    return pl.pallas_call(
+        functools.partial(update_kernel, rate, at // UPDATE_ROWS, at % UPDATE_ROWS),
+        grid=(OWN // UPDATE_ROWS,),
+        out_shape=(like, like, like),
+        in_specs=[pl.BlockSpec((16, 128), lambda i: (0, 0))] + [rows] * 4,
+        out_specs=(rows, rows, rows),
+        compiler_params=pltpu.CompilerParams(vmem_limit_bytes=47 * 2**20),
+        name="update",
+    )(totals, grad, master, momentum, average)
+
+
 def shards(codes, labels, picks, classes, null_mask, starts, master, momentum, average):
     sec = lax.axis_index("section")
     d = lax.axis_index("dp")
@@ -1937,8 +1978,9 @@
     if fast:
         grad, squares = reduce_and_scatter(left, right, tail, d_table, dx0, local[None, :])
         totals = share_norm(small, squares, n_sec, n_dp)
-        dg_f, loss_sum, grad_norm = totals[:6].reshape(-1), totals[6, 0], totals[8, 0]
         count_sum = jnp.sum(info[:, 4:6, :PICKS].astype(F32))
+        updated = update(learn_rate, totals, grad, master, momentum, average)
+        return totals[6, 0], count_sum, totals[8, 0], *updated
     else:
         grads = matrix_gradients(left, right, tail)
         grads = grads.astype(F32) + lax.ppermute(grads, "section", beside).astype(F32)

time: 421 us -> 418 us (level)
  other arithmetic: 19 us -> 2.34 us
  Pallas kernels: 390 us -> 405 us
    add x1 -> x0, other arithmetic: 16.7 us -> none  [shards(): new_average = average_decay * average + (1.0 - average_decay) * new_master]
    pallas_call x0 -> x1, Pallas kernels: none -> 15.4 us  [update(): pl.pallas_call(functools.partial(update_kernel, rate, at // UPDATE_ROWS,...]
where the time goes in v5:
time: 418 us; the launch traced here: 412 us
  Pallas kernels  405 us (97%)
  local copies, waits for them, and re-layouts  4.31 us (1%)
    pallas_call x1, Pallas kernels, gather_and_embed(): pl.pallas_call(open_kernel, out_shape=(jax.ShapeDtypeStruct((WROWS, D), B...  125 us
    pallas_call x1, Pallas kernels, reduce_and_scatter(): pl.pallas_call(close_kernel, out_shape=(jax.ShapeDtypeStruct((OWN, D), F3...  117 us
    pallas_call x2, Pallas kernels, backward_call(): pl.pallas_call(functools.partial(backward_kernel, send), out_shape=(jax.S...  91.9 us
    pallas_call x2, Pallas kernels, forward_call(): pl.pallas_call(functools.partial(forward_kernel, keep), out_shape=(low,)...  35.4 us
    pallas_call x1, Pallas kernels, update(): pl.pallas_call(functools.partial(update_kernel, rate, at // UPDATE_ROWS,...  15.4 us
    pallas_call x1, Pallas kernels, share_norm(): pl.pallas_call(functools.partial(norm_kernel, n_sec, n_dp), out_shape=jax...  13.6 us

profile of v5, /device:TPU:0, one launch (start us, length us, event | category | flops | bytes accessed | tf_op | source)
XLA Modules:
  0.0 412.5 jit_solution(6044784416858515999)
XLA Ops:
  0.6 0.0 copy-start.7
  0.7 0.6 tile.9.frequency
  1.3 124.9 %gather_and_embed.1 = (bf16[9232,768]{1,0:T(8,128)(2,1)}, bf16[272,768]{1,0:T(8,128)(2,1)}, s32[8,8,384]{2,1,0:T(8,128)}, bf16[16,768]{1,0:T(8,128)(2,1)}, f32[2...) custom-call(f32[2176,768]{1,0:T(8,128)} %master.3, s32[2,264]{1,0:T(2,128)} %codes.1, ...), custom_call_target="tpu_custom_call" | custom-call | tf_op jit(solution)/shard_map/gather_and_embed/pallas_call | solution.py:573
  126.2 0.0 copy-start.3
  126.2 0.0 copy-start.5
  126.2 1.4 convert_reduce_fusion
  127.7 0.0 copy-done.7
  127.7 22.1 %layer_forward.1.x = bf16[272,768]{1,0:T(8,128)(2,1)S(1)} custom-call(bf16[272,768]{1,0:T(8,128)(2,1)} %get-tuple-element.81.x, bf16[9232,768]{1,0:T(8,128)(2,1)} %get-tuple-element.82.w_any, f32[272,128]{1,0:T(8,128)S(1)} %get-tuple-element.83.cosine, f32[272,128]{1,0:T(8,128)S(1)} %get-tuple-element.84.sine, s32[2,4]{1,0:T(2,128)S(1)} %copy-done.7), custom_call_target="tpu_custom_call" | custom-call | tf_op jit(solution)/shard_map/layer_forward/pallas_call | solution.py:1238
  149.8 0.0 copy-done.3
  149.8 0.0 copy-done.5
  149.8 0.9 select_subtract_fusion
  150.7 0.7 sub.18.index
  151.4 13.3 %layer_forward_kept.1 = (bf16[272,768]{1,0:T(8,128)(2,1)}, bf16[272,768]{1,0:T(8,128)(2,1)}, bf16[272,768]{1,0:T(8,128)(2,1)}, bf16[272,768]{1,0:T(8,128)(2,1)},...) custom-call(bf16[272,768]{1,0:T(8,128)(2,1)S(1)} %layer_forward.1.x, ...), custom_call_target="tpu_custom_call" | custom-call | tf_op jit(solution)/shard_map/layer_forward_kept/pallas_call | solution.py:1238
  164.8 6.3 %head.1 = (bf16[272,768]{1,0:T(8,128)(2,1)}, f32[2176,768]{1,0:T(8,128)}, f32[8,128]{1,0:T(8,128)}) custom-call(bf16[272,768]{1,0:T(8,128)(2,1)} %get-tuple-element.85.y, s32[2,32]{1,0:T(2,128)} %picks.3, s32[8,8,384]{2,1,0:T(8,128)} %get-tuple-element.86.info, bf16[16,768]{1,0:T(8,128)(2,1)} %get-tuple-element.87.gain, ...), custom_call_target="tpu_custom_call" | custom-call | tf_op jit(solution)/shard_map/head/pallas_call | solution.py:1787
  171.0 0.0 copy-done.4
  171.1 70.5 %layer_backward_send.1 = (bf16[272,768]{1,0:T(8,128)(2,1)}, bf16[272,9216]{1,0:T(8,128)(2,1)}, bf16[6,272,768]{2,1,0:T(8,128)(2,1)}, bf16[16,768]{1,0:T(8,128)(2,1)S(1)}) custom-call(bf16[272,768]{1,0:T(8,128)(2,1)} %get-tuple-element.90.dy, bf16[272,768]{1,0:T(8,128)(2,1)S(1)} %layer_forward.1.x, bf16[9232,768]{1,0:T(8,128)(2,1)} %get-tuple-element.82.w_any, ...), custom_call_target="tpu_custom_call" | custom-call | tf_op jit(solution)/shard_map/layer_backward_send/pallas_call | solution.py:1417
  241.5 23.4 %conditional.1 = ((bf16[272,768]{1,0:T(8,128)(2,1)}, bf16[272,9216]{1,0:T(8,128)(2,1)}, bf16[6,272,768]{2,1,0:T(8,128)(2,1)}, bf16[16,768]{1,0:T(8,128)(2,1)S(1)})) conditional(s32[]{:T(128)} %convert_element_type.6, (bf16[272,768]{1,0:T(8,128)(2,1)}, bf16[272,9216]{1,0:T(8,128)(2,1)}, bf16[6,272,768]{2,1,0:T(8,128)(2,1)}, ...), branch_computations={%region_0.1_spmd, %region_1.2_spmd} | conditional | bytes 835592 | solution.py:1972
  241.5 1.8 copy.26.dy
  243.3 21.4 %layer_backward.1 = (bf16[272,768]{1,0:T(8,128)(2,1)}, bf16[272,9216]{1,0:T(8,128)(2,1)}, bf16[6,272,768]{2,1,0:T(8,128)(2,1)}, bf16[16,768]{1,0:T(8,128)(2,1)S(1)}) custom-call(bf16[272,768]{1,0:T(8,128)(2,1)} %copy.26.dy, bf16[272,768]{1,0:T(8,128)(2,1)S(1)} %get-tuple-element.35.x, bf16[9232,768]{1,0:T(8,128)(2,1)} %get-tuple-element.36.w_any, ...), custom_call_target="tpu_custom_call" | custom-call | tf_op jit(solution)/shard_map/cond/branch_1_fun/layer_backward/pallas_call | solution.py:1417
  264.9 117.2 %reduce_and_scatter.1 = (f32[2176,768]{1,0:T(8,128)}, f32[8,128]{1,0:T(8,128)}) custom-call(bf16[272,9216]{1,0:T(8,128)(2,1)} %get-tuple-element.99.left_any, bf16[6,272,768]{2,1,0:T(8,128)(2,1)} %get-tuple-element.100.right_any, bf16[16,768]{1,0:T(8,128)(2,1)S(1)} %get-tuple-element.101.tail, ...), custom_call_target="tpu_custom_call", output_to_operand_aliasing={{0}: (3, {})} | custom-call | tf_op jit(solution)/shard_map/reduce_and_scatter/pallas_call | solution.py:953
  382.1 0.7 copy-done.2
  382.8 13.6 %share_norm.1.totals = f32[16,128]{1,0:T(8,128)S(1)} custom-call(f32[8,128]{1,0:T(8,128)S(1)} %copy-done.1, f32[8,128]{1,0:T(8,128)S(1)} %copy-done.2), custom_call_target="tpu_custom_call" | custom-call | flops 10000000000 | bytes 40000000 | tf_op jit(solution)/shard_map/share_norm/pallas_call | solution.py:1050
  396.4 0.5 fusion
  396.9 15.4 %update.1 = (f32[2176,768]{1,0:T(8,128)}, f32[2176,768]{1,0:T(8,128)}, f32[2176,768]{1,0:T(8,128)}) custom-call(f32[16,128]{1,0:T(8,128)S(1)} %share_norm.1.totals, f32[2176,768]{1,0:T(8,128)S(1)} %copy-done, f32[2176,768]{1,0:T(8,128)} %master.3, f32[2176,768]{1,0:T(8,128)} %momentum.1, f32[2176,768]{1,0:T(8,128)} %average.1), custom_call_target="tpu_custom_call" | custom-call | tf_op jit(solution)/shard_map/update/pallas_call | solution.py:1924
  (10 shorter events, 0.0 us)
Async XLA Ops:
  0.6 127.0 %copy-start.7 = (s32[2,4]{1,0:T(2,128)S(1)}, s32[2,4]{1,0:T(2,128)}, u32[]{:S(2)}) copy-start(s32[2,4]{1,0:T(2,128)} %starts.7) | copy-start | bytes 100
  126.2 23.6 %copy-start.3 = (f32[272,128]{1,0:T(8,128)}, f32[272,128]{1,0:T(8,128)S(1)}, u32[]{:S(2)}) copy-start(f32[272,128]{1,0:T(8,128)S(1)} %get-tuple-element.83.cosine) | copy-start | bytes 417796
  126.2 23.6 %copy-start.5 = (f32[272,128]{1,0:T(8,128)}, f32[272,128]{1,0:T(8,128)S(1)}, u32[]{:S(2)}) copy-start(f32[272,128]{1,0:T(8,128)S(1)} %get-tuple-element.84.sine) | copy-start | bytes 417796
  151.4 19.6 %copy-start.4 = (f32[272,128]{1,0:T(8,128)S(1)}, f32[272,128]{1,0:T(8,128)}, u32[]{:S(2)}) copy-start(f32[272,128]{1,0:T(8,128)} %copy-done.3) | copy-start | bytes 417796
  151.4 19.6 %copy-start.6 = (f32[272,128]{1,0:T(8,128)S(1)}, f32[272,128]{1,0:T(8,128)}, u32[]{:S(2)}) copy-start(f32[272,128]{1,0:T(8,128)} %copy-done.5) | copy-start | bytes 417796
  264.9 117.2 %copy-start.1 = (f32[8,128]{1,0:T(8,128)S(1)}, f32[8,128]{1,0:T(8,128)}, u32[]{:S(2)}) copy-start(f32[8,128]{1,0:T(8,128)} %get-tuple-element.89.small) | copy-start | bytes 12292
  382.1 0.7 copy-start.2
  382.8 14.1 %copy-start = (f32[2176,768]{1,0:T(8,128)S(1)}, f32[2176,768]{1,0:T(8,128)}, u32[]{:S(2)}) copy-start(f32[2176,768]{1,0:T(8,128)} %get-tuple-element.105.grad) | copy-start | bytes 20054020

commit v6 on v5

--- a/solution.py
+++ b/solution.py
@@ -615,10 +615,10 @@
 
 
 def close_kernel(
-    left_any, right_any, tail, start, block, index, out, squares, left, right, loc, sent, rx_core,
+    left_any, right_any, tail, start, block, info, out, squares, left, right, loc, sent, rx_core,
     rx_up, rx_down, rx_x, summed, ring, all_dx, load_sem, core_sem, recv_sem, recv_c, core_send,
     send_sem, ring_sem, dx_own, dx_send, line_recv, cross_recv, turn_recv, dx_core_send,
-    dx_core_recv, ready,
+    dx_core_recv, index, ready,
 ):
     sec, dp, z, c, par, home = place()
     targets = hop_targets(sec, dp, c, par)
@@ -832,6 +832,14 @@
 
     pl.when(first)(own_first)
 
+    def list_rows():
+        for e in range(8):
+            for p in range(2):
+                there = pl.ds((2 * e + p) * SP, SP)
+                index[:, there] = info[e, p : p + 1, :][:, :SP] - dp * OWN
+
+    pl.when(first)(list_rows)
+
     def from_below(k):
         line(z - k, "up").wait_recv()
         pl.when(z < 3)(lambda: line(z - k, "up").start())
@@ -947,7 +955,7 @@
     pl.when(first)(drain_tiles)
 
 
-def reduce_and_scatter(left, right, tail, start, block, index):
+def reduce_and_scatter(left, right, tail, start, block, info):
     low = lambda *shape: pltpu.VMEM(shape, BF16)
     dma = pltpu.SemaphoreType.DMA
     return pl.pallas_call(
@@ -985,13 +993,14 @@
             dma,
             dma,
             dma,
+            pltpu.VMEM((1, 16 * SP), jnp.int32),
             pltpu.SemaphoreType.REGULAR,
         ],
         compiler_params=pltpu.CompilerParams(
             collective_id=1, has_side_effects=True, vmem_limit_bytes=63 * 2**20
         ),
         name="reduce_and_scatter",
-    )(left, right, tail, start, block, index)
+    )(left, right, tail, start, block, info)
 
 
 def norm_kernel(n_sec, n_dp, small, squares, out, block, every, send_sem, recv_sem):
@@ -1674,7 +1683,9 @@
             jnp.where(counts[...] > 0, log_col - hit_col, 0.0), axis=0, keepdims=True
         )
         lane = lax.broadcasted_iota(jnp.int32, (1, 128), 1)
-        small[6:7, :] = jnp.where(jnp.logical_and(lane == 0, dp == 0), loss, 0.0)
+        number = jnp.sum(counts[...], axis=0, keepdims=True)
+        pair = jnp.where(lane == 0, loss, jnp.where(lane == 1, number, 0.0))
+        small[6:7, :] = jnp.where(dp == 0, pair, 0.0)
         shrink = jnp.exp(top_col - log_col)
 
         def slopes(start, size):
@@ -1950,8 +1961,6 @@
         weights, x0, info, gain, cosine, sine, table = gather_and_embed(
             master, codes, labels, picks, starts, classes, null_mask, wide
         )
-        all_index = info[:, :2, :SP].reshape(-1)
-        local = jnp.where(sec == 0, all_index, -1) - d * own
     else:
         table = master.astype(BF16)
         opened = open_anywhere(codes, labels, picks, classes, null_mask, starts, table, frequency)
@@ -1976,11 +1985,10 @@
     )
 
     if fast:
-        grad, squares = reduce_and_scatter(left, right, tail, d_table, dx0, local[None, :])
+        grad, squares = reduce_and_scatter(left, right, tail, d_table, dx0, info)
         totals = share_norm(small, squares, n_sec, n_dp)
-        count_sum = jnp.sum(info[:, 4:6, :PICKS].astype(F32))
         updated = update(learn_rate, totals, grad, master, momentum, average)
-        return totals[6, 0], count_sum, totals[8, 0], *updated
+        return totals[6, 0], totals[6, 1], totals[8, 0], *updated
     else:
         grads = matrix_gradients(left, right, tail)
         grads = grads.astype(F32) + lax.ppermute(grads, "section", beside).astype(F32)

time: 418 us -> 415 us (level)
  no operation moved by 1% of the time
where the time goes in v6:
time: 415 us; the launch traced here: 409 us
  Pallas kernels  404 us (97%)
    pallas_call x1, Pallas kernels, gather_and_embed(): pl.pallas_call(open_kernel, out_shape=(jax.ShapeDtypeStruct((WROWS, D), B...  125 us
    pallas_call x1, Pallas kernels, reduce_and_scatter(): pl.pallas_call(close_kernel, out_shape=(jax.ShapeDtypeStruct((OWN, D), F3...  117 us
    pallas_call x2, Pallas kernels, backward_call(): pl.pallas_call(functools.partial(backward_kernel, send), out_shape=(jax.S...  92 us
    pallas_call x2, Pallas kernels, forward_call(): pl.pallas_call(functools.partial(forward_kernel, keep), out_shape=(low,)...  35 us
    pallas_call x1, Pallas kernels, update(): pl.pallas_call(functools.partial(update_kernel, rate, at // UPDATE_ROWS,...  15.4 us
    pallas_call x1, Pallas kernels, share_norm(): pl.pallas_call(functools.partial(norm_kernel, n_sec, n_dp), out_shape=jax...  13.6 us

profile of v6, /device:TPU:0, one launch (start us, length us, event | category | flops | bytes accessed | tf_op | source)
XLA Modules:
  0.0 409.1 jit_solution(10844894186874012820)
XLA Ops:
  0.6 0.0 copy-start.3
  0.7 0.6 tile.9.frequency
  1.3 124.9 %gather_and_embed.1 = (bf16[9232,768]{1,0:T(8,128)(2,1)}, bf16[272,768]{1,0:T(8,128)(2,1)}, s32[8,8,384]{2,1,0:T(8,128)}, bf16[16,768]{1,0:T(8,128)(2,1)}, f32[2...) custom-call(f32[2176,768]{1,0:T(8,128)} %master.3, s32[2,264]{1,0:T(2,128)} %codes.1, ...), custom_call_target="tpu_custom_call" | custom-call | tf_op jit(solution)/shard_map/gather_and_embed/pallas_call | solution.py:573
  126.2 0.0 copy-done.3
  126.2 22.1 %layer_forward.1.x = bf16[272,768]{1,0:T(8,128)(2,1)S(1)} custom-call(bf16[272,768]{1,0:T(8,128)(2,1)} %get-tuple-element.81.x, bf16[9232,768]{1,0:T(8,128)(2,1)} %get-tuple-element.82.w_any, f32[272,128]{1,0:T(8,128)S(1)} %get-tuple-element.83.cosine, f32[272,128]{1,0:T(8,128)S(1)} %get-tuple-element.84.sine, s32[2,4]{1,0:T(2,128)S(1)} %copy-done.3), custom_call_target="tpu_custom_call" | custom-call | tf_op jit(solution)/shard_map/layer_forward/pallas_call | solution.py:1247
  148.4 12.9 %layer_forward_kept.1 = (bf16[272,768]{1,0:T(8,128)(2,1)}, bf16[272,768]{1,0:T(8,128)(2,1)}, bf16[272,768]{1,0:T(8,128)(2,1)}, bf16[272,768]{1,0:T(8,128)(2,1)},...) custom-call(bf16[272,768]{1,0:T(8,128)(2,1)S(1)} %layer_forward.1.x, ...), custom_call_target="tpu_custom_call" | custom-call | tf_op jit(solution)/shard_map/layer_forward_kept/pallas_call | solution.py:1247
  161.2 6.3 %head.1 = (bf16[272,768]{1,0:T(8,128)(2,1)}, f32[2176,768]{1,0:T(8,128)}, f32[8,128]{1,0:T(8,128)}) custom-call(bf16[272,768]{1,0:T(8,128)(2,1)} %get-tuple-element.85.y, s32[2,32]{1,0:T(2,128)} %picks.3, s32[8,8,384]{2,1,0:T(8,128)} %get-tuple-element.86.info, bf16[16,768]{1,0:T(8,128)(2,1)} %get-tuple-element.87.gain, ...), custom_call_target="tpu_custom_call" | custom-call | tf_op jit(solution)/shard_map/head/pallas_call | solution.py:1798
  167.5 70.5 %layer_backward_send.1 = (bf16[272,768]{1,0:T(8,128)(2,1)}, bf16[272,9216]{1,0:T(8,128)(2,1)}, bf16[6,272,768]{2,1,0:T(8,128)(2,1)}, bf16[16,768]{1,0:T(8,128)(2,1)S(1)}) custom-call(bf16[272,768]{1,0:T(8,128)(2,1)} %get-tuple-element.90.dy, bf16[272,768]{1,0:T(8,128)(2,1)S(1)} %layer_forward.1.x, bf16[9232,768]{1,0:T(8,128)(2,1)} %get-tuple-element.82.w_any, ...), custom_call_target="tpu_custom_call" | custom-call | tf_op jit(solution)/shard_map/layer_backward_send/pallas_call | solution.py:1426
  238.0 23.4 %conditional.1 = ((bf16[272,768]{1,0:T(8,128)(2,1)}, bf16[272,9216]{1,0:T(8,128)(2,1)}, bf16[6,272,768]{2,1,0:T(8,128)(2,1)}, bf16[16,768]{1,0:T(8,128)(2,1)S(1)})) conditional(s32[]{:T(128)} %convert_element_type.3, (bf16[272,768]{1,0:T(8,128)(2,1)}, bf16[272,9216]{1,0:T(8,128)(2,1)}, bf16[6,272,768]{2,1,0:T(8,128)(2,1)}, ...), branch_computations={%region_0.0_spmd, %region_1.0_spmd} | conditional | bytes 835592 | solution.py:1981
  238.0 1.8 copy.26.dy
  239.8 21.5 %layer_backward.1 = (bf16[272,768]{1,0:T(8,128)(2,1)}, bf16[272,9216]{1,0:T(8,128)(2,1)}, bf16[6,272,768]{2,1,0:T(8,128)(2,1)}, bf16[16,768]{1,0:T(8,128)(2,1)S(1)}) custom-call(bf16[272,768]{1,0:T(8,128)(2,1)} %copy.26.dy, bf16[272,768]{1,0:T(8,128)(2,1)S(1)} %get-tuple-element.35.x, bf16[9232,768]{1,0:T(8,128)(2,1)} %get-tuple-element.36.w_any, ...), custom_call_target="tpu_custom_call" | custom-call | tf_op jit(solution)/shard_map/cond/branch_1_fun/layer_backward/pallas_call | solution.py:1426
  261.4 0.0 copy-start.1
  261.5 117.1 %reduce_and_scatter.1 = (f32[2176,768]{1,0:T(8,128)}, f32[8,128]{1,0:T(8,128)}) custom-call(bf16[272,9216]{1,0:T(8,128)(2,1)} %get-tuple-element.99.left_any, bf16[6,272,768]{2,1,0:T(8,128)(2,1)} %get-tuple-element.100.right_any, bf16[16,768]{1,0:T(8,128)(2,1)S(1)} %get-tuple-element.101.tail, ...), custom_call_target="tpu_custom_call", output_to_operand_aliasing={{0}: (3, {})} | custom-call | tf_op jit(solution)/shard_map/reduce_and_scatter/pallas_call | solution.py:961
  378.6 0.0 copy-done.1
  378.6 0.0 copy-start.2
  378.6 0.7 copy-done.2
  379.2 0.0 copy-start
  379.3 13.6 %share_norm.1.totals = f32[16,128]{1,0:T(8,128)S(1)} custom-call(f32[8,128]{1,0:T(8,128)S(1)} %copy-done.1, f32[8,128]{1,0:T(8,128)S(1)} %copy-done.2), custom_call_target="tpu_custom_call" | custom-call | flops 10000000000 | bytes 40000000 | tf_op jit(solution)/shard_map/share_norm/pallas_call | solution.py:1059
  392.9 0.6 fusion
  393.5 0.0 copy-done
  393.5 15.4 %update.1 = (f32[2176,768]{1,0:T(8,128)}, f32[2176,768]{1,0:T(8,128)}, f32[2176,768]{1,0:T(8,128)}) custom-call(f32[16,128]{1,0:T(8,128)S(1)} %share_norm.1.totals, f32[2176,768]{1,0:T(8,128)S(1)} %copy-done, f32[2176,768]{1,0:T(8,128)} %master.3, f32[2176,768]{1,0:T(8,128)} %momentum.1, f32[2176,768]{1,0:T(8,128)} %average.1), custom_call_target="tpu_custom_call" | custom-call | tf_op jit(solution)/shard_map/update/pallas_call | solution.py:1935
  (2 shorter events, 0.0 us)
Async XLA Ops:
  0.6 125.6 %copy-start.3 = (s32[2,4]{1,0:T(2,128)S(1)}, s32[2,4]{1,0:T(2,128)}, u32[]{:S(2)}) copy-start(s32[2,4]{1,0:T(2,128)} %starts.7) | copy-start | bytes 100
  261.4 117.1 %copy-start.1 = (f32[8,128]{1,0:T(8,128)S(1)}, f32[8,128]{1,0:T(8,128)}, u32[]{:S(2)}) copy-start(f32[8,128]{1,0:T(8,128)} %get-tuple-element.89.small) | copy-start | bytes 12292
  378.6 0.7 copy-start.2
  379.2 14.2 %copy-start = (f32[2176,768]{1,0:T(8,128)S(1)}, f32[2176,768]{1,0:T(8,128)}, u32[]{:S(2)}) copy-start(f32[2176,768]{1,0:T(8,128)} %get-tuple-element.105.grad) | copy-start | bytes 20054020

commit v7 on v6

--- a/solution.py
+++ b/solution.py
@@ -1275,11 +1275,11 @@
     return grad_in, jnp.sum(grad * unit, axis=0, keepdims=True)
 
 
-def backward_kernel(send, dy, x, w_any, cosine, sine, starts, *refs):
+def backward_kernel(send, dy_any, x, w_any, cosine, sine, starts, *refs):
     kept, refs = refs[:7], refs[7:]
     dx, left, right, tail, refs = *refs[:4], refs[4:]
     q, k, v, o, h, gate, up, w, dgate, dup, m, da, do, dq, dk, dv, a1, a2, db, *refs = refs
-    unseen, sems, keep_sems, out_sems, *hop_sems = refs
+    unseen, sems, keep_sems, out_sems, dy, dy_sem, *hop_sems = refs
     sec = lax.axis_index("section")
     dp = lax.axis_index("dp")
     upper = sec >= 2
@@ -1306,6 +1306,8 @@
         copy.start()
         outs.append(copy)
     def run():
+        fetch = pltpu.make_async_copy(dy_any, dy, dy_sem)
+        fetch.start()
         copies = weight_copies(w_any, w, sems)
         taken = [
             pltpu.make_async_copy(part, (q, k, v, o, h, gate, up)[i], keep_sems.at[i])
@@ -1319,6 +1321,7 @@
         unseen[...] = hide(starts)
         lanes = lax.broadcasted_iota(jnp.int32, (SP, 128), 1)
         first = lanes < 64
+        fetch.wait()
         copies[4].wait()
         taken[5].wait()
         taken[6].wait()
@@ -1431,7 +1434,7 @@
             jax.ShapeDtypeStruct((6, SP, D), BF16),
             jax.ShapeDtypeStruct((16, D), BF16),
         ),
-        in_specs=[VMEM, VMEM, ANY, VMEM, VMEM, SMEM] + [ANY] * 7,
+        in_specs=[ANY, VMEM, ANY, VMEM, VMEM, SMEM] + [ANY] * 7,
         out_specs=(VMEM, ANY, ANY, VMEM),
         scratch_shapes=[pltpu.VMEM((SP, n), t) for n, t in KEPT]
         + [
@@ -1447,6 +1450,8 @@
             pltpu.SemaphoreType.DMA((6,)),
             pltpu.SemaphoreType.DMA((7,)),
             pltpu.SemaphoreType.DMA((13,)),
+            narrow,
+            pltpu.SemaphoreType.DMA,
         ]
         + ([pltpu.SemaphoreType.DMA] * 2 if send else []),
         compiler_params=pltpu.CompilerParams(

time: 415 us -> 414 us (level)
  no operation moved by 1% of the time
where the time goes in v7:
time: 414 us; the launch traced here: 408 us
  Pallas kernels  404 us (98%)
    pallas_call x1, Pallas kernels, gather_and_embed(): pl.pallas_call(open_kernel, out_shape=(jax.ShapeDtypeStruct((WROWS, D), B...  125 us
    pallas_call x1, Pallas kernels, reduce_and_scatter(): pl.pallas_call(close_kernel, out_shape=(jax.ShapeDtypeStruct((OWN, D), F3...  117 us
    pallas_call x2, Pallas kernels, backward_call(): pl.pallas_call(functools.partial(backward_kernel, send), out_shape=(jax.S...  91.3 us
    pallas_call x2, Pallas kernels, forward_call(): pl.pallas_call(functools.partial(forward_kernel, keep), out_shape=(low,)...  35 us
    pallas_call x1, Pallas kernels, update(): pl.pallas_call(functools.partial(update_kernel, rate, at // UPDATE_ROWS,...  15.4 us
    pallas_call x1, Pallas kernels, share_norm(): pl.pallas_call(functools.partial(norm_kernel, n_sec, n_dp), out_shape=jax...  13.6 us

profile of v7, /device:TPU:0, one launch (start us, length us, event | category | flops | bytes accessed | tf_op | source)
XLA Modules:
  0.0 408.4 jit_solution(1178026191582442045)
XLA Ops:
  0.6 0.0 copy-start.3
  0.7 0.6 tile.9.frequency
  1.3 124.9 %gather_and_embed.1 = (bf16[9232,768]{1,0:T(8,128)(2,1)}, bf16[272,768]{1,0:T(8,128)(2,1)}, s32[8,8,384]{2,1,0:T(8,128)}, bf16[16,768]{1,0:T(8,128)(2,1)}, f32[2...) custom-call(f32[2176,768]{1,0:T(8,128)} %master.3, s32[2,264]{1,0:T(2,128)} %codes.1, ...), custom_call_target="tpu_custom_call" | custom-call | tf_op jit(solution)/shard_map/gather_and_embed/pallas_call | solution.py:573
  126.2 0.0 copy-done.3
  126.2 22.1 %layer_forward.1.x = bf16[272,768]{1,0:T(8,128)(2,1)S(1)} custom-call(bf16[272,768]{1,0:T(8,128)(2,1)} %get-tuple-element.81.x, bf16[9232,768]{1,0:T(8,128)(2,1)} %get-tuple-element.82.w_any, f32[272,128]{1,0:T(8,128)S(1)} %get-tuple-element.83.cosine, f32[272,128]{1,0:T(8,128)S(1)} %get-tuple-element.84.sine, s32[2,4]{1,0:T(2,128)S(1)} %copy-done.3), custom_call_target="tpu_custom_call" | custom-call | tf_op jit(solution)/shard_map/layer_forward/pallas_call | solution.py:1247
  148.4 12.9 %layer_forward_kept.1 = (bf16[272,768]{1,0:T(8,128)(2,1)}, bf16[272,768]{1,0:T(8,128)(2,1)}, bf16[272,768]{1,0:T(8,128)(2,1)}, bf16[272,768]{1,0:T(8,128)(2,1)},...) custom-call(bf16[272,768]{1,0:T(8,128)(2,1)S(1)} %layer_forward.1.x, ...), custom_call_target="tpu_custom_call" | custom-call | tf_op jit(solution)/shard_map/layer_forward_kept/pallas_call | solution.py:1247
  161.2 6.3 %head.1 = (bf16[272,768]{1,0:T(8,128)(2,1)}, f32[2176,768]{1,0:T(8,128)}, f32[8,128]{1,0:T(8,128)}) custom-call(bf16[272,768]{1,0:T(8,128)(2,1)} %get-tuple-element.85.y, s32[2,32]{1,0:T(2,128)} %picks.3, s32[8,8,384]{2,1,0:T(8,128)} %get-tuple-element.86.info, bf16[16,768]{1,0:T(8,128)(2,1)} %get-tuple-element.87.gain, ...), custom_call_target="tpu_custom_call" | custom-call | tf_op jit(solution)/shard_map/head/pallas_call | solution.py:1803
  167.5 70.1 %layer_backward_send.1 = (bf16[272,768]{1,0:T(8,128)(2,1)}, bf16[272,9216]{1,0:T(8,128)(2,1)}, bf16[6,272,768]{2,1,0:T(8,128)(2,1)}, bf16[16,768]{1,0:T(8,128)(2,1)S(1)}) custom-call(bf16[272,768]{1,0:T(8,128)(2,1)} %get-tuple-element.90.dy_any, bf16[272,768]{1,0:T(8,128)(2,1)S(1)} %layer_forward.1.x, bf16[9232,768]{1,0:T(8,128)(2,1)} %get-tuple-element.82.w_any, ...), custom_call_target="tpu_custom_call" | custom-call | tf_op jit(solution)/shard_map/layer_backward_send/pallas_call | solution.py:1429
  237.6 23.1 %conditional.1 = ((bf16[272,768]{1,0:T(8,128)(2,1)}, bf16[272,9216]{1,0:T(8,128)(2,1)}, bf16[6,272,768]{2,1,0:T(8,128)(2,1)}, bf16[16,768]{1,0:T(8,128)(2,1)S(1)})) conditional(s32[]{:T(128)} %convert_element_type.3, (bf16[272,768]{1,0:T(8,128)(2,1)}, bf16[272,9216]{1,0:T(8,128)(2,1)}, bf16[6,272,768]{2,1,0:T(8,128)(2,1)}, ...), branch_computations={%region_0.0_spmd, %region_1.0_spmd} | conditional | bytes 835592 | solution.py:1986
  237.7 1.8 copy.26.dy_any
  239.5 21.1 %layer_backward.1 = (bf16[272,768]{1,0:T(8,128)(2,1)}, bf16[272,9216]{1,0:T(8,128)(2,1)}, bf16[6,272,768]{2,1,0:T(8,128)(2,1)}, bf16[16,768]{1,0:T(8,128)(2,1)S(1)}) custom-call(bf16[272,768]{1,0:T(8,128)(2,1)} %copy.26.dy_any, bf16[272,768]{1,0:T(8,128)(2,1)S(1)} %get-tuple-element.35.x, bf16[9232,768]{1,0:T(8,128)(2,1)} %get-tuple-element.36.w_any, ...), custom_call_target="tpu_custom_call" | custom-call | tf_op jit(solution)/shard_map/cond/branch_1_fun/layer_backward/pallas_call | solution.py:1429
  260.8 0.0 copy-start.1
  260.8 117.1 %reduce_and_scatter.1 = (f32[2176,768]{1,0:T(8,128)}, f32[8,128]{1,0:T(8,128)}) custom-call(bf16[272,9216]{1,0:T(8,128)(2,1)} %get-tuple-element.99.left_any, bf16[6,272,768]{2,1,0:T(8,128)(2,1)} %get-tuple-element.100.right_any, bf16[16,768]{1,0:T(8,128)(2,1)S(1)} %get-tuple-element.101.tail, ...), custom_call_target="tpu_custom_call", output_to_operand_aliasing={{0}: (3, {})} | custom-call | tf_op jit(solution)/shard_map/reduce_and_scatter/pallas_call | solution.py:961
  377.9 0.0 copy-done.1
  377.9 0.0 copy-start.2
  377.9 0.7 copy-done.2
  378.6 0.0 copy-start
  378.6 13.6 %share_norm.1.totals = f32[16,128]{1,0:T(8,128)S(1)} custom-call(f32[8,128]{1,0:T(8,128)S(1)} %copy-done.1, f32[8,128]{1,0:T(8,128)S(1)} %copy-done.2), custom_call_target="tpu_custom_call" | custom-call | flops 10000000000 | bytes 40000000 | tf_op jit(solution)/shard_map/share_norm/pallas_call | solution.py:1059
  392.2 0.6 fusion
  392.8 0.0 copy-done
  392.8 15.4 %update.1 = (f32[2176,768]{1,0:T(8,128)}, f32[2176,768]{1,0:T(8,128)}, f32[2176,768]{1,0:T(8,128)}) custom-call(f32[16,128]{1,0:T(8,128)S(1)} %share_norm.1.totals, f32[2176,768]{1,0:T(8,128)S(1)} %copy-done, f32[2176,768]{1,0:T(8,128)} %master.3, f32[2176,768]{1,0:T(8,128)} %momentum.1, f32[2176,768]{1,0:T(8,128)} %average.1), custom_call_target="tpu_custom_call" | custom-call | tf_op jit(solution)/shard_map/update/pallas_call | solution.py:1940
  (2 shorter events, 0.0 us)
Async XLA Ops:
  0.6 125.6 %copy-start.3 = (s32[2,4]{1,0:T(2,128)S(1)}, s32[2,4]{1,0:T(2,128)}, u32[]{:S(2)}) copy-start(s32[2,4]{1,0:T(2,128)} %starts.7) | copy-start | bytes 100
  260.8 117.1 %copy-start.1 = (f32[8,128]{1,0:T(8,128)S(1)}, f32[8,128]{1,0:T(8,128)}, u32[]{:S(2)}) copy-start(f32[8,128]{1,0:T(8,128)} %get-tuple-element.89.small) | copy-start | bytes 12292
  377.9 0.7 copy-start.2
  378.6 14.2 %copy-start = (f32[2176,768]{1,0:T(8,128)S(1)}, f32[2176,768]{1,0:T(8,128)}, u32[]{:S(2)}) copy-start(f32[2176,768]{1,0:T(8,128)} %get-tuple-element.105.grad) | copy-start | bytes 20054020
